TPU v7x, 32 devices: a whole 2x2x4 slice. The times are simulated.
32 devices in a mesh: gz: 8 (over y, x, core), gy: 4 (over z).
Axes of the slice: x: 2, y: 2, z: 4, core: 2. Of those that a mesh axis runs over, the one named last changes fastest.
Arguments:
- electric: float32 [3, 128, 32, 256], P(None, 'gz', 'gy'), may hold values from -6 to 6
- magnetic: float32 [3, 128, 32, 256], P(None, 'gz', 'gy'), may hold values from -6 to 6
- material: int32 [128, 32, 256], P('gz', 'gy'), may hold values from 0 to 15
- incoming: int32 [32, 32, 256], P(None, 'gy'), may hold values from 0 to 15
- shift_flags: int32 [8], replicated, may hold values from 0 to 1, as said below
- eps_table: float32 [16], replicated, may hold values from 1 to 6
- sigma_table: float32 [16], replicated, may hold values from 0 to 1
- kerr_table: float32 [16], replicated, may hold values from 0.05 to 0.5
Outputs:
- electric_out: float32 [3, 128, 32, 256], P(None, 'gz', 'gy')
- magnetic_out: float32 [3, 128, 32, 256], P(None, 'gz', 'gy')
Inputs may be any that keep to these rules, and one draw needn't show every extreme that they name: `shift_flags`: exactly 4 entries are 1, the others 0.
All inputs are finite; a program needn't handle non-finite values.
Results may differ from a plain program's by a relative error of at most 0.00002.
Values sent between devices are 32-bit elements; how exact they have to be, the bound alone decides.
No kernel may reach another device: no remote copies, remote signals or barrier semaphores. Data moves between devices by JAX's collectives and lax.ppermute only.
A program may use at most 64 MiB of HBM per device.

v0:
```python
import jax
import jax.numpy as jnp
from jax import lax
from jax.sharding import PartitionSpec as P

STEPS = 8
SHIFT = 8


courant_number = 0.5


def from_behind(value, axis, steps):
    count = lax.axis_size(axis)
    leading, last = (max(0, -steps), min(count, count - steps))
    return lax.ppermute(value, axis, [(source, source + steps) for source in range(leading, last)])


def forward_face(field, face, axis_no):
    length = field.shape[axis_no]
    shifted = jnp.concatenate(
        [lax.slice_in_dim(field, 1, length, axis=axis_no), face], axis=axis_no
    )
    return shifted - field


def backward_face(field, face, axis_no):
    length = field.shape[axis_no]
    shifted = jnp.concatenate(
        [face, lax.slice_in_dim(field, 0, length - 1, axis=axis_no)], axis=axis_no
    )
    return field - shifted


def forward_zero(field, axis_no):
    length = field.shape[axis_no]
    shifted = jnp.concatenate(
        [
            lax.slice_in_dim(field, 1, length, axis=axis_no),
            jnp.zeros_like(lax.slice_in_dim(field, 0, 1, axis=axis_no)),
        ],
        axis=axis_no,
    )
    return shifted - field


def backward_zero(field, axis_no):
    length = field.shape[axis_no]
    shifted = jnp.concatenate(
        [
            jnp.zeros_like(lax.slice_in_dim(field, 0, 1, axis=axis_no)),
            lax.slice_in_dim(field, 0, length - 1, axis=axis_no),
        ],
        axis=axis_no,
    )
    return field - shifted


def curl_faces(vector, face_z, face_y, with_face, with_zero):

    def derivative(component, axis_no):
        if axis_no == 0:
            return with_face(vector[component], face_z[component], 0)
        if axis_no == 1:
            return with_face(vector[component], face_y[component], 1)
        return with_zero(vector[component], 2)

    part_x = derivative(2, 1) - derivative(1, 0)
    part_y = derivative(0, 0) - derivative(2, 2)
    part_z = derivative(1, 2) - derivative(0, 1)
    return jnp.stack([part_x, part_y, part_z])


def e_update(electric, curl_h, coefs):
    square = electric[0] * electric[0] + electric[1] * electric[1] + electric[2] * electric[2]
    permit = coefs[0] + coefs[2] * square
    damping = 0.5 * coefs[1] / permit
    return ((1.0 - damping) * electric + courant_number / permit * curl_h) / (1.0 + damping)


def lookup(id_map, eps_table, sigma_table, kerr_table):
    results = []
    for tables in (eps_table, sigma_table, kerr_table):
        summed = jnp.zeros(id_map.shape, jnp.float32)
        for entry_no in range(tables.shape[0]):
            summed = summed + jnp.where(id_map == entry_no, tables[entry_no], jnp.float32(0.0))
        results.append(summed)
    return jnp.stack(results)


def body(electric, magnetic, material, incoming, shift_flags, eps_table, sigma_table, kerr_table):
    coefs = lookup(material, eps_table, sigma_table, kerr_table)
    is_last = lax.axis_index("gz") == lax.axis_size("gz") - 1
    done_count = jnp.int32(0)
    for step_no in range(STEPS):
        shift_on = shift_flags[step_no] == 1
        new_ids = lax.dynamic_slice_in_dim(incoming, done_count * SHIFT, SHIFT, 0)
        new_coefs = lookup(new_ids, eps_table, sigma_table, kerr_table)
        stacked = jnp.concatenate([electric, magnetic, coefs], 0)
        arrived = from_behind(stacked[:, : SHIFT + 1], "gz", -1)
        moved_part = arrived[:, :SHIFT]
        after_face = jnp.where(shift_on, arrived[0:3, SHIFT : SHIFT + 1], arrived[0:3, 0:1])
        entering = jnp.concatenate(
            [moved_part[:6], jnp.where(is_last, new_coefs, moved_part[6:])], 0
        )
        moved = jnp.concatenate([stacked[:, SHIFT:], entering], 1)
        stacked = jnp.where(shift_on, moved, stacked)
        electric, magnetic, coefs = (stacked[0:3], stacked[3:6], stacked[6:9])
        done_count = done_count + shift_flags[step_no]
        upper_y = from_behind(electric[:, :, 0:1], "gy", -1)
        magnetic = magnetic - courant_number * curl_faces(
            electric, after_face, upper_y, forward_face, forward_zero
        )
        lower_z = from_behind(magnetic[:, -1:], "gz", 1)
        lower_y = from_behind(magnetic[:, :, -1:], "gy", 1)
        curl_h = curl_faces(magnetic, lower_z, lower_y, backward_face, backward_zero)
        electric = e_update(electric, curl_h, coefs)
    return (electric, magnetic)


def solution(mesh):
    return jax.shard_map(
        body,
        mesh=mesh,
        in_specs=(
            P(None, "gz", "gy", None),
            P(None, "gz", "gy", None),
            P("gz", "gy", None),
            P(None, "gy", None),
            P(),
            P(),
            P(),
            P(),
        ),
        out_specs=(P(None, "gz", "gy", None), P(None, "gz", "gy", None)),
        check_vma=False,
    )
```

profile of v0, /device:TPU:11, one launch (start us, length us, event | category | flops | bytes accessed | tf_op | source)
XLA Modules:
  0.0 419.5 jit_solution(476217595961296188)
XLA Ops:
  8.6 10.5 %bitcast_dynamic-update-slice_fusion.2 = (f32[9,16,8,256]{3,2,1,0:T(8,128)S(1)}, pred[16,8,256]{2,1,0:T(8,128)(4,1)S(1)}, pred[16,8,256]{2,1,0:T(8,128)(4,1)S(1)...) fusion(f32[9,16,8,256]{3,2,1,0:T(8,128)S(1)} %constant_dynamic-, ...), kind=kLoop, calls=%fused_computation.273 | loop fusion | flops 1540096 | bytes 786496
  19.1 10.2 %bitcast_dynamic-update-slice_fusion.1 = f32[9,16,8,256]{3,2,1,0:T(8,128)S(1)} fusion(f32[9,16,8,256]{3,2,1,0:T(8,128)S(1)} %get-tuple-element.154, pred[16,8,256]{2,1,0:T(8,128)(4,1)S(1)} %get-tuple-element.170, pred[16,8,256]{2,1,0:T(8,128)(4,1)S(1)} %get-tuple-element.169, pred[16,8,256]{2,1,0:T(8,128)(4,1)S(1)} %get-tuple-element.168, ...), kind=kLoop, calls=%fused_computation.272 | loop fusion | flops 1015808 | bytes 655424
  29.4 10.2 %bitcast_dynamic-update-slice_fusion = f32[9,16,8,256]{3,2,1,0:T(8,128)S(1)} fusion(f32[9,16,8,256]{3,2,1,0:T(8,128)S(1)} %bitcast_dynamic-update-slice_fusion.1, pred[16,8,256]{2,1,0:T(8,128)(4,1)S(1)} %get-tuple-element.170, pred[16,8,256]{2,1,0:T(8,128)(4,1)S(1)} %get-tuple-element.169, pred[16,8,256]{2,1,0:T(8,128)(4,1)S(1)} %get-tuple-element.168, ...), kind=kLoop, calls=%fused_computation.271 | loop fusion | flops 1015808 | bytes 655424 | tf_op jit(solution)/shard_map/concatenate | solution.py:99
  39.6 2.7 collective-permute-start
  46.3 11.2 %add_bitcast_fusion.19 = (f32[1,8,8,256]{3,2,1,0:T(8,128)S(1)}, pred[8,8,256]{2,1,0:T(8,128)(4,1)}, pred[8,8,256]{2,1,0:T(8,128)(4,1)}, pred[8,8,256]{2,1,0:T(8,...) fusion(f32[]{:T(128)} %bitcast.23, f32[]{:T(128)} %bitcast.22, ...), kind=kLoop, calls=%fused_computation.365 | loop fusion | flops 1540096 | bytes 786500 | tf_op jit(solution)/shard_map/stack | solution.py:88
  57.4 10.0 %add_bitcast_fusion.29 = f32[1,8,8,256]{3,2,1,0:T(8,128)S(1)} fusion(pred[8,8,256]{2,1,0:T(8,128)(4,1)S(1)} %get-tuple-element.365, pred[8,8,256]{2,1,0:T(8,128)(4,1)S(1)} %get-tuple-element.366, pred[8,8,256]{2,1,0:T(8,128)(4,1)S(1)} %get-tuple-element.367, pred[8,8,256]{2,1,0:T(8,128)(4,1)S(1)} %get-tuple-element.368, ...), kind=kLoop, calls=%fused_computation.375 | loop fusion | flops 507904 | bytes 327744 | tf_op jit(solution)/shard_map/stack | solution.py:88
  67.5 10.1 %add_bitcast_fusion.30 = f32[1,8,8,256]{3,2,1,0:T(8,128)S(1)} fusion(pred[8,8,256]{2,1,0:T(8,128)(4,1)S(1)} %get-tuple-element.365, pred[8,8,256]{2,1,0:T(8,128)(4,1)S(1)} %get-tuple-element.366, pred[8,8,256]{2,1,0:T(8,128)(4,1)S(1)} %get-tuple-element.367, pred[8,8,256]{2,1,0:T(8,128)(4,1)S(1)} %get-tuple-element.368, ...), kind=kLoop, calls=%fused_computation.376 | loop fusion | flops 507904 | bytes 327744 | tf_op jit(solution)/shard_map/stack | solution.py:88
  82.9 2.3 collective-permute-done.1
  85.6 4.6 %collective-permute-start.3 = (f32[3,1,8,256]{3,2,1,0:T(8,128)S(1)}, f32[3,1,8,256]{3,2,1,0:T(8,128)S(1)}, u32[]{:S(2)}, u32[]{:S(2)}) collective-permute-start(f32[3,1,8,256]{3,2,1,0:T(8,128)S(1)} %slice.2242), channel_id=1, source_target_pairs={{0,4},{4,8},{8,12},{12,16},{16,20},{20,24},{24,28},{1,5},{5,9},{9,... | collective-permute-start | bytes 73736 | tf_op jit(solution)/shard_map/ppermute | solution.py:16
  90.3 3.2 collective-permute-start.2
  100.8 11.2 %add_bitcast_fusion.10 = (f32[1,8,8,256]{3,2,1,0:T(8,128)S(1)}, pred[8,8,256]{2,1,0:T(8,128)(4,1)S(1)}, pred[8,8,256]{2,1,0:T(8,128)(4,1)S(1)}, pred[8,8,256]{2,...) fusion(f32[]{:T(128)} %bitcast.23, f32[]{:T(128)} %bitcast.22, ...), kind=kLoop, calls=%fused_computation.356 | loop fusion | flops 1540096 | bytes 786504 | tf_op jit(solution)/shard_map/stack | solution.py:88
  112.0 10.0 %add_bitcast_fusion.26 = f32[1,8,8,256]{3,2,1,0:T(8,128)S(1)} fusion(pred[8,8,256]{2,1,0:T(8,128)(4,1)S(1)} %get-tuple-element.314, pred[8,8,256]{2,1,0:T(8,128)(4,1)S(1)} %get-tuple-element.315, pred[8,8,256]{2,1,0:T(8,128)(4,1)S(1)} %get-tuple-element.316, pred[8,8,256]{2,1,0:T(8,128)(4,1)S(1)} %get-tuple-element.317, ...), kind=kLoop, calls=%fused_computation.372 | loop fusion | flops 507904 | bytes 327744 | tf_op jit(solution)/shard_map/stack | solution.py:88
  122.0 10.1 %add_bitcast_fusion.27 = f32[1,8,8,256]{3,2,1,0:T(8,128)S(1)} fusion(pred[8,8,256]{2,1,0:T(8,128)(4,1)S(1)} %get-tuple-element.314, pred[8,8,256]{2,1,0:T(8,128)(4,1)S(1)} %get-tuple-element.315, pred[8,8,256]{2,1,0:T(8,128)(4,1)S(1)} %get-tuple-element.316, pred[8,8,256]{2,1,0:T(8,128)(4,1)S(1)} %get-tuple-element.317, ...), kind=kLoop, calls=%fused_computation.373 | loop fusion | flops 507904 | bytes 327744 | tf_op jit(solution)/shard_map/stack | solution.py:88
  137.4 2.5 collective-permute-done.5
  140.4 5.2 %collective-permute-start.7 = (f32[3,1,8,256]{3,2,1,0:T(8,128)S(1)}, f32[3,1,8,256]{3,2,1,0:T(8,128)S(1)}, u32[]{:S(2)}, u32[]{:S(2)}) collective-permute-start(f32[3,1,8,256]{3,2,1,0:T(8,128)S(1)} %slice.2283), channel_id=1, source_target_pairs={{0,4},{4,8},{8,12},{12,16},{16,20},{20,24},{24,28},{1,5},{5,9},{9,... | collective-permute-start | bytes 73736 | tf_op jit(solution)/shard_map/ppermute | solution.py:16
  145.7 3.2 collective-permute-start.6
  153.6 11.2 %add_bitcast_fusion.13 = (f32[1,8,8,256]{3,2,1,0:T(8,128)S(1)}, pred[8,8,256]{2,1,0:T(8,128)(4,1)}, pred[8,8,256]{2,1,0:T(8,128)(4,1)}, pred[8,8,256]{2,1,0:T(8,...) fusion(f32[]{:T(128)} %bitcast.23, f32[]{:T(128)} %bitcast.22, ...), kind=kLoop, calls=%fused_computation.359 | loop fusion | flops 1540096 | bytes 786504 | tf_op jit(solution)/shard_map/stack | solution.py:88
  164.8 10.0 %add_bitcast_fusion.23 = f32[1,8,8,256]{3,2,1,0:T(8,128)S(1)} fusion(pred[8,8,256]{2,1,0:T(8,128)(4,1)S(1)} %get-tuple-element.331, pred[8,8,256]{2,1,0:T(8,128)(4,1)S(1)} %get-tuple-element.332, pred[8,8,256]{2,1,0:T(8,128)(4,1)S(1)} %get-tuple-element.333, pred[8,8,256]{2,1,0:T(8,128)(4,1)S(1)} %get-tuple-element.334, ...), kind=kLoop, calls=%fused_computation.369 | loop fusion | flops 507904 | bytes 327744 | tf_op jit(solution)/shard_map/stack | solution.py:88
  174.9 10.1 %add_bitcast_fusion.24 = f32[1,8,8,256]{3,2,1,0:T(8,128)S(1)} fusion(pred[8,8,256]{2,1,0:T(8,128)(4,1)S(1)} %get-tuple-element.331, pred[8,8,256]{2,1,0:T(8,128)(4,1)S(1)} %get-tuple-element.332, pred[8,8,256]{2,1,0:T(8,128)(4,1)S(1)} %get-tuple-element.333, pred[8,8,256]{2,1,0:T(8,128)(4,1)S(1)} %get-tuple-element.334, ...), kind=kLoop, calls=%fused_computation.370 | loop fusion | flops 507904 | bytes 327744 | tf_op jit(solution)/shard_map/stack | solution.py:88
  190.3 2.2 collective-permute-done.9
  192.9 5.5 %collective-permute-start.11 = (f32[3,1,8,256]{3,2,1,0:T(8,128)S(1)}, f32[3,1,8,256]{3,2,1,0:T(8,128)S(1)}, u32[]{:S(2)}, u32[]{:S(2)}) collective-permute-start(f32[3,1,8,256]{3,2,1,0:T(8,128)S(1)} %slice.2324), channel_id=1, source_target_pairs={{0,4},{4,8},{8,12},{12,16},{16,20},{20,24},{24,28},{1,5},{5,9},{9,... | collective-permute-start | bytes 73736 | tf_op jit(solution)/shard_map/ppermute | solution.py:16
  198.5 3.2 collective-permute-start.10
  206.4 10.5 %add_bitcast_fusion.16 = (f32[1,8,8,256]{3,2,1,0:T(8,128)S(1)}, pred[8,8,256]{2,1,0:T(8,128)(4,1)S(1)}, pred[8,8,256]{2,1,0:T(8,128)(4,1)S(1)}, pred[8,8,256]{2,...) fusion(f32[]{:T(128)} %bitcast.23, f32[]{:T(128)} %bitcast.22, ...), kind=kLoop, calls=%fused_computation.362 | loop fusion | flops 1540096 | bytes 786504 | tf_op jit(solution)/shard_map/stack | solution.py:88
  216.9 10.0 %add_bitcast_fusion.20 = f32[1,8,8,256]{3,2,1,0:T(8,128)S(1)} fusion(pred[8,8,256]{2,1,0:T(8,128)(4,1)S(1)} %get-tuple-element.348, pred[8,8,256]{2,1,0:T(8,128)(4,1)S(1)} %get-tuple-element.349, pred[8,8,256]{2,1,0:T(8,128)(4,1)S(1)} %get-tuple-element.350, pred[8,8,256]{2,1,0:T(8,128)(4,1)S(1)} %get-tuple-element.351, ...), kind=kLoop, calls=%fused_computation.366 | loop fusion | flops 507904 | bytes 327744 | tf_op jit(solution)/shard_map/stack | solution.py:88
  226.9 10.1 %add_bitcast_fusion.21 = f32[1,8,8,256]{3,2,1,0:T(8,128)S(1)} fusion(pred[8,8,256]{2,1,0:T(8,128)(4,1)S(1)} %get-tuple-element.348, pred[8,8,256]{2,1,0:T(8,128)(4,1)S(1)} %get-tuple-element.349, pred[8,8,256]{2,1,0:T(8,128)(4,1)S(1)} %get-tuple-element.350, pred[8,8,256]{2,1,0:T(8,128)(4,1)S(1)} %get-tuple-element.351, ...), kind=kLoop, calls=%fused_computation.367 | loop fusion | flops 507904 | bytes 327744 | tf_op jit(solution)/shard_map/stack | solution.py:88
  239.5 2.1 collective-permute-start.13
  244.7 5.7 %collective-permute-start.15 = (f32[3,1,8,256]{3,2,1,0:T(8,128)S(1)}, f32[3,1,8,256]{3,2,1,0:T(8,128)S(1)}, u32[]{:S(2)}, u32[]{:S(2)}) collective-permute-start(f32[3,1,8,256]{3,2,1,0:T(8,128)S(1)} %slice.2365), channel_id=1, source_target_pairs={{0,4},{4,8},{8,12},{12,16},{16,20},{20,24},{24,28},{1,5},{5,9},{9,... | collective-permute-start | bytes 73736 | tf_op jit(solution)/shard_map/ppermute | solution.py:16
  250.5 3.2 collective-permute-start.14
  258.9 10.1 %add_bitcast_fusion.18 = f32[1,8,8,256]{3,2,1,0:T(8,128)S(1)} fusion(pred[8,8,256]{2,1,0:T(8,128)(4,1)S(1)} %copy-done.36, pred[8,8,256]{2,1,0:T(8,128)(4,1)S(1)} %copy-done.35, pred[8,8,256]{2,1,0:T(8,128)(4,1)S(1)} %copy-done.34, pred[8,8,256]{2,1,0:T(8,128)(4,1)S(1)} %copy-done.33, pred[8,8,256]{2,1,0:T(8,128)(4,1)S(1)} %copy-done.32, ...), kind=kLoop, calls=%fused_computation.364 | loop fusion | flops 507904 | bytes 327744 | tf_op jit(solution)/shard_map/stack | solution.py:88
  269.0 10.0 %add_bitcast_fusion.17 = f32[1,8,8,256]{3,2,1,0:T(8,128)S(1)} fusion(pred[8,8,256]{2,1,0:T(8,128)(4,1)S(1)} %copy-done.36, pred[8,8,256]{2,1,0:T(8,128)(4,1)S(1)} %copy-done.35, pred[8,8,256]{2,1,0:T(8,128)(4,1)S(1)} %copy-done.34, pred[8,8,256]{2,1,0:T(8,128)(4,1)S(1)} %copy-done.33, pred[8,8,256]{2,1,0:T(8,128)(4,1)S(1)} %copy-done.32, ...), kind=kLoop, calls=%fused_computation.363 | loop fusion | flops 507904 | bytes 327744 | tf_op jit(solution)/shard_map/stack | solution.py:88
  282.5 2.8 collective-permute-done.17
  285.7 5.7 %collective-permute-start.19 = (f32[3,1,8,256]{3,2,1,0:T(8,128)S(1)}, f32[3,1,8,256]{3,2,1,0:T(8,128)S(1)}, u32[]{:S(2)}, u32[]{:S(2)}) collective-permute-start(f32[3,1,8,256]{3,2,1,0:T(8,128)S(1)} %slice.2406), channel_id=1, source_target_pairs={{0,4},{4,8},{8,12},{12,16},{16,20},{20,24},{24,28},{1,5},{5,9},{9,... | collective-permute-start | bytes 73736 | tf_op jit(solution)/shard_map/ppermute | solution.py:16
  291.5 3.2 collective-permute-start.18
  299.3 10.1 %add_bitcast_fusion.15 = f32[1,8,8,256]{3,2,1,0:T(8,128)S(1)} fusion(pred[8,8,256]{2,1,0:T(8,128)(4,1)S(1)} %get-tuple-element.58, pred[8,8,256]{2,1,0:T(8,128)(4,1)S(1)} %get-tuple-element.57, pred[8,8,256]{2,1,0:T(8,128)(4,1)S(1)} %get-tuple-element.56, pred[8,8,256]{2,1,0:T(8,128)(4,1)S(1)} %get-tuple-element.55, ...), kind=kLoop, calls=%fused_computation.361 | loop fusion | flops 507904 | bytes 327744 | tf_op jit(solution)/shard_map/stack | solution.py:88
  309.5 10.0 %add_bitcast_fusion.14 = f32[1,8,8,256]{3,2,1,0:T(8,128)S(1)} fusion(pred[8,8,256]{2,1,0:T(8,128)(4,1)S(1)} %get-tuple-element.58, pred[8,8,256]{2,1,0:T(8,128)(4,1)S(1)} %get-tuple-element.57, pred[8,8,256]{2,1,0:T(8,128)(4,1)S(1)} %get-tuple-element.56, pred[8,8,256]{2,1,0:T(8,128)(4,1)S(1)} %get-tuple-element.55, ...), kind=kLoop, calls=%fused_computation.360 | loop fusion | flops 507904 | bytes 327744 | tf_op jit(solution)/shard_map/stack | solution.py:88
  322.9 2.8 collective-permute-done.21
  326.1 5.7 %collective-permute-start.23 = (f32[3,1,8,256]{3,2,1,0:T(8,128)S(1)}, f32[3,1,8,256]{3,2,1,0:T(8,128)S(1)}, u32[]{:S(2)}, u32[]{:S(2)}) collective-permute-start(f32[3,1,8,256]{3,2,1,0:T(8,128)S(1)} %slice.2447), channel_id=1, source_target_pairs={{0,4},{4,8},{8,12},{12,16},{16,20},{20,24},{24,28},{1,5},{5,9},{9,... | collective-permute-start | bytes 73736 | tf_op jit(solution)/shard_map/ppermute | solution.py:16
  331.9 3.2 collective-permute-start.22
  340.2 10.1 %add_bitcast_fusion.12 = f32[1,8,8,256]{3,2,1,0:T(8,128)S(1)} fusion(pred[8,8,256]{2,1,0:T(8,128)(4,1)S(1)} %copy-done.52, pred[8,8,256]{2,1,0:T(8,128)(4,1)S(1)} %copy-done.51, pred[8,8,256]{2,1,0:T(8,128)(4,1)S(1)} %copy-done.50, pred[8,8,256]{2,1,0:T(8,128)(4,1)S(1)} %copy-done.49, pred[8,8,256]{2,1,0:T(8,128)(4,1)S(1)} %copy-done.48, ...), kind=kLoop, calls=%fused_computation.358 | loop fusion | flops 507904 | bytes 327744 | tf_op jit(solution)/shard_map/stack | solution.py:88
  350.3 10.0 %add_bitcast_fusion.11 = f32[1,8,8,256]{3,2,1,0:T(8,128)S(1)} fusion(pred[8,8,256]{2,1,0:T(8,128)(4,1)S(1)} %copy-done.52, pred[8,8,256]{2,1,0:T(8,128)(4,1)S(1)} %copy-done.51, pred[8,8,256]{2,1,0:T(8,128)(4,1)S(1)} %copy-done.50, pred[8,8,256]{2,1,0:T(8,128)(4,1)S(1)} %copy-done.49, pred[8,8,256]{2,1,0:T(8,128)(4,1)S(1)} %copy-done.48, ...), kind=kLoop, calls=%fused_computation.357 | loop fusion | flops 507904 | bytes 327744 | tf_op jit(solution)/shard_map/stack | solution.py:88
  363.8 2.8 collective-permute-done.25
  367.0 5.7 %collective-permute-start.27 = (f32[3,1,8,256]{3,2,1,0:T(8,128)S(1)}, f32[3,1,8,256]{3,2,1,0:T(8,128)S(1)}, u32[]{:S(2)}, u32[]{:S(2)}) collective-permute-start(f32[3,1,8,256]{3,2,1,0:T(8,128)S(1)} %slice.2488), channel_id=1, source_target_pairs={{0,4},{4,8},{8,12},{12,16},{16,20},{20,24},{24,28},{1,5},{5,9},{9,... | collective-permute-start | bytes 73736 | tf_op jit(solution)/shard_map/ppermute | solution.py:16
  372.8 3.2 collective-permute-start.26
  380.9 10.1 %add_bitcast_fusion.9 = f32[1,8,8,256]{3,2,1,0:T(8,128)S(1)} fusion(pred[8,8,256]{2,1,0:T(8,128)(4,1)S(1)} %copy-done.20, pred[8,8,256]{2,1,0:T(8,128)(4,1)S(1)} %copy-done.19, pred[8,8,256]{2,1,0:T(8,128)(4,1)S(1)} %copy-done.18, pred[8,8,256]{2,1,0:T(8,128)(4,1)S(1)} %copy-done.17, pred[8,8,256]{2,1,0:T(8,128)(4,1)S(1)} %copy-done.16, ...), kind=kLoop, calls=%fused_computation.355 | loop fusion | flops 507904 | bytes 327744 | tf_op jit(solution)/shard_map/stack | solution.py:88
  391.1 10.0 %add_bitcast_fusion.8 = f32[1,8,8,256]{3,2,1,0:T(8,128)S(1)} fusion(pred[8,8,256]{2,1,0:T(8,128)(4,1)S(1)} %copy-done.20, pred[8,8,256]{2,1,0:T(8,128)(4,1)S(1)} %copy-done.19, pred[8,8,256]{2,1,0:T(8,128)(4,1)S(1)} %copy-done.18, pred[8,8,256]{2,1,0:T(8,128)(4,1)S(1)} %copy-done.17, pred[8,8,256]{2,1,0:T(8,128)(4,1)S(1)} %copy-done.16, ...), kind=kLoop, calls=%fused_computation.354 | loop fusion | flops 507904 | bytes 327744 | tf_op jit(solution)/shard_map/stack | solution.py:88
  404.6 2.8 collective-permute-done.29
  407.7 5.7 %collective-permute-start.31 = (f32[3,1,8,256]{3,2,1,0:T(8,128)S(1)}, f32[3,1,8,256]{3,2,1,0:T(8,128)S(1)}, u32[]{:S(2)}, u32[]{:S(2)}) collective-permute-start(f32[3,1,8,256]{3,2,1,0:T(8,128)S(1)} %slice.2529), channel_id=1, source_target_pairs={{0,4},{4,8},{8,12},{12,16},{16,20},{20,24},{24,28},{1,5},{5,9},{9,... | collective-permute-start | bytes 73736 | tf_op jit(solution)/shard_map/ppermute | solution.py:16
  413.5 3.2 collective-permute-start.30
  (393 shorter events, 77.4 us)
Async XLA Ops:
  0.6 7.9 %copy-start.53 = (s32[16,8,256]{2,1,0:T(8,128)S(1)}, s32[16,8,256]{2,1,0:T(8,128)}, u32[]{:S(2)}) copy-start(s32[16,8,256]{2,1,0:T(8,128)} %param.10) | copy-start | bytes 393220
  39.5 6.7 %copy-start.8 = (s32[32,8,256]{2,1,0:T(8,128)S(1)}, s32[32,8,256]{2,1,0:T(8,128)}, u32[]{:S(2)}) copy-start(s32[32,8,256]{2,1,0:T(8,128)} %param.11) | copy-start | bytes 786436
  39.6 38.0 %collective-permute-start = (f32[9,9,8,256]{3,2,1,0:T(8,128)S(1)}, f32[9,9,8,256]{3,2,1,0:T(8,128)}, u32[]{:S(2)}, u32[]{:S(2)}) collective-permute-start(f32[9,9,8,256]{3,2,1,0:T(8,128)S(1)} %slice.2213), channel_id=1, source_target_pairs={{4,0},{8,4},{12,8},{16,12},{20,16},{24,20},{28,24},{5,1},{9,5},{13... | collective-permute-start | bytes 1990664 | tf_op jit(solution)/shard_map/ppermute | solution.py:16
  79.9 5.3 %collective-permute-start.1 = (f32[3,16,1,256]{3,2,1,0:T(1,128)S(1)}, f32[3,16,1,256]{3,2,1,0:T(1,128)S(1)}, u32[]{:S(2)}, u32[]{:S(2)}) collective-permute-start(f32[3,16,1,256]{3,2,1,0:T(1,128)S(1)} %slice.2225), channel_id=1, source_target_pairs={{1,0},{2,1},{3,2},{5,4},{6,5},{7,6},{9,8},{10,9},{11,10},{13,12},{... | collective-permute-start | bytes 147464 | tf_op jit(solution)/shard_map/ppermute | solution.py:16
  85.6 7.9 %collective-permute-start.3 = (f32[3,1,8,256]{3,2,1,0:T(8,128)S(1)}, f32[3,1,8,256]{3,2,1,0:T(8,128)S(1)}, u32[]{:S(2)}, u32[]{:S(2)}) collective-permute-start(f32[3,1,8,256]{3,2,1,0:T(8,128)S(1)} %slice.2242), channel_id=1, source_target_pairs={{0,4},{4,8},{8,12},{12,16},{16,20},{20,24},{24,28},{1,5},{5,9},{9,... | collective-permute-start | bytes 73736 | tf_op jit(solution)/shard_map/ppermute | solution.py:16
  90.3 4.8 %collective-permute-start.2 = (f32[3,16,1,256]{3,2,1,0:T(1,128)S(1)}, f32[3,16,1,256]{3,2,1,0:T(1,128)S(1)}, u32[]{:S(2)}, u32[]{:S(2)}) collective-permute-start(f32[3,16,1,256]{3,2,1,0:T(1,128)S(1)} %slice.2238), channel_id=1, source_target_pairs={{0,1},{1,2},{2,3},{4,5},{5,6},{6,7},{8,9},{9,10},{10,11},{12,13},{... | collective-permute-start | bytes 147464 | tf_op jit(solution)/shard_map/ppermute | solution.py:16
  95.6 36.5 %copy-start.2 = (f32[9,16,8,256]{3,2,1,0:T(8,128)}, f32[9,16,8,256]{3,2,1,0:T(8,128)S(1)}, u32[]{:S(2)}) copy-start(f32[9,16,8,256]{3,2,1,0:T(8,128)S(1)} %pad_maximum_fusion) | copy-start | bytes 3538948
  95.7 36.5 %collective-permute-start.4 = (f32[9,9,8,256]{3,2,1,0:T(8,128)S(1)}, f32[9,9,8,256]{3,2,1,0:T(8,128)}, u32[]{:S(2)}, u32[]{:S(2)}) collective-permute-start(f32[9,9,8,256]{3,2,1,0:T(8,128)S(1)} %slice.2254), channel_id=1, source_target_pairs={{4,0},{8,4},{12,8},{16,12},{20,16},{24,20},{28,24},{5,1},{9,5},{13... | collective-permute-start | bytes 1990664 | tf_op jit(solution)/shard_map/ppermute | solution.py:16
  134.6 5.4 %collective-permute-start.5 = (f32[3,16,1,256]{3,2,1,0:T(1,128)S(1)}, f32[3,16,1,256]{3,2,1,0:T(1,128)S(1)}, u32[]{:S(2)}, u32[]{:S(2)}) collective-permute-start(f32[3,16,1,256]{3,2,1,0:T(1,128)S(1)} %slice.2266), channel_id=1, source_target_pairs={{1,0},{2,1},{3,2},{5,4},{6,5},{7,6},{9,8},{10,9},{11,10},{13,12},{... | collective-permute-start | bytes 147464 | tf_op jit(solution)/shard_map/ppermute | solution.py:16
  140.4 8.5 %collective-permute-start.7 = (f32[3,1,8,256]{3,2,1,0:T(8,128)S(1)}, f32[3,1,8,256]{3,2,1,0:T(8,128)S(1)}, u32[]{:S(2)}, u32[]{:S(2)}) collective-permute-start(f32[3,1,8,256]{3,2,1,0:T(8,128)S(1)} %slice.2283), channel_id=1, source_target_pairs={{0,4},{4,8},{8,12},{12,16},{16,20},{20,24},{24,28},{1,5},{5,9},{9,... | collective-permute-start | bytes 73736 | tf_op jit(solution)/shard_map/ppermute | solution.py:16
  145.7 4.8 %collective-permute-start.6 = (f32[3,16,1,256]{3,2,1,0:T(1,128)S(1)}, f32[3,16,1,256]{3,2,1,0:T(1,128)S(1)}, u32[]{:S(2)}, u32[]{:S(2)}) collective-permute-start(f32[3,16,1,256]{3,2,1,0:T(1,128)S(1)} %slice.2279), channel_id=1, source_target_pairs={{0,1},{1,2},{2,3},{4,5},{5,6},{6,7},{8,9},{9,10},{10,11},{12,13},{... | collective-permute-start | bytes 147464 | tf_op jit(solution)/shard_map/ppermute | solution.py:16
  150.9 34.1 %copy-start.3 = (f32[9,16,8,256]{3,2,1,0:T(8,128)}, f32[9,16,8,256]{3,2,1,0:T(8,128)S(1)}, u32[]{:S(2)}) copy-start(f32[9,16,8,256]{3,2,1,0:T(8,128)S(1)} %pad_maximum_fusion.1) | copy-start | bytes 3538948
  151.0 34.0 %collective-permute-start.8 = (f32[9,9,8,256]{3,2,1,0:T(8,128)S(1)}, f32[9,9,8,256]{3,2,1,0:T(8,128)}, u32[]{:S(2)}, u32[]{:S(2)}) collective-permute-start(f32[9,9,8,256]{3,2,1,0:T(8,128)S(1)} %slice.2295), channel_id=1, source_target_pairs={{4,0},{8,4},{12,8},{16,12},{20,16},{24,20},{28,24},{5,1},{9,5},{13... | collective-permute-start | bytes 1990664 | tf_op jit(solution)/shard_map/ppermute | solution.py:16
  187.4 5.0 %collective-permute-start.9 = (f32[3,16,1,256]{3,2,1,0:T(1,128)S(1)}, f32[3,16,1,256]{3,2,1,0:T(1,128)S(1)}, u32[]{:S(2)}, u32[]{:S(2)}) collective-permute-start(f32[3,16,1,256]{3,2,1,0:T(1,128)S(1)} %slice.2307), channel_id=1, source_target_pairs={{1,0},{2,1},{3,2},{5,4},{6,5},{7,6},{9,8},{10,9},{11,10},{13,12},{... | collective-permute-start | bytes 147464 | tf_op jit(solution)/shard_map/ppermute | solution.py:16
  192.9 8.8 %collective-permute-start.11 = (f32[3,1,8,256]{3,2,1,0:T(8,128)S(1)}, f32[3,1,8,256]{3,2,1,0:T(8,128)S(1)}, u32[]{:S(2)}, u32[]{:S(2)}) collective-permute-start(f32[3,1,8,256]{3,2,1,0:T(8,128)S(1)} %slice.2324), channel_id=1, source_target_pairs={{0,4},{4,8},{8,12},{12,16},{16,20},{20,24},{24,28},{1,5},{5,9},{9,... | collective-permute-start | bytes 73736 | tf_op jit(solution)/shard_map/ppermute | solution.py:16
  198.5 4.8 %collective-permute-start.10 = (f32[3,16,1,256]{3,2,1,0:T(1,128)S(1)}, f32[3,16,1,256]{3,2,1,0:T(1,128)S(1)}, u32[]{:S(2)}, u32[]{:S(2)}) collective-permute-start(f32[3,16,1,256]{3,2,1,0:T(1,128)S(1)} %slice.2320), channel_id=1, source_target_pairs={{0,1},{1,2},{2,3},{4,5},{5,6},{6,7},{8,9},{9,10},{10,11},{12,13},{... | collective-permute-start | bytes 147464 | tf_op jit(solution)/shard_map/ppermute | solution.py:16
  203.8 33.3 %copy-start.1 = (f32[9,16,8,256]{3,2,1,0:T(8,128)}, f32[9,16,8,256]{3,2,1,0:T(8,128)S(1)}, u32[]{:S(2)}) copy-start(f32[9,16,8,256]{3,2,1,0:T(8,128)S(1)} %pad_maximum_fusion.2) | copy-start | bytes 3538948
  203.8 33.2 %collective-permute-start.12 = (f32[9,9,8,256]{3,2,1,0:T(8,128)S(1)}, f32[9,9,8,256]{3,2,1,0:T(8,128)}, u32[]{:S(2)}, u32[]{:S(2)}) collective-permute-start(f32[9,9,8,256]{3,2,1,0:T(8,128)S(1)} %slice.2336), channel_id=1, source_target_pairs={{4,0},{8,4},{12,8},{16,12},{20,16},{24,20},{28,24},{5,1},{9,5},{13... | collective-permute-start | bytes 1990664 | tf_op jit(solution)/shard_map/ppermute | solution.py:16
  239.5 4.8 %collective-permute-start.13 = (f32[3,16,1,256]{3,2,1,0:T(1,128)S(1)}, f32[3,16,1,256]{3,2,1,0:T(1,128)S(1)}, u32[]{:S(2)}, u32[]{:S(2)}) collective-permute-start(f32[3,16,1,256]{3,2,1,0:T(1,128)S(1)} %slice.2348), channel_id=1, source_target_pairs={{1,0},{2,1},{3,2},{5,4},{6,5},{7,6},{9,8},{10,9},{11,10},{13,12},{... | collective-permute-start | bytes 147464 | tf_op jit(solution)/shard_map/ppermute | solution.py:16
  244.7 9.0 %collective-permute-start.15 = (f32[3,1,8,256]{3,2,1,0:T(8,128)S(1)}, f32[3,1,8,256]{3,2,1,0:T(8,128)S(1)}, u32[]{:S(2)}, u32[]{:S(2)}) collective-permute-start(f32[3,1,8,256]{3,2,1,0:T(8,128)S(1)} %slice.2365), channel_id=1, source_target_pairs={{0,4},{4,8},{8,12},{12,16},{16,20},{20,24},{24,28},{1,5},{5,9},{9,... | collective-permute-start | bytes 73736 | tf_op jit(solution)/shard_map/ppermute | solution.py:16
  250.5 4.8 %collective-permute-start.14 = (f32[3,16,1,256]{3,2,1,0:T(1,128)S(1)}, f32[3,16,1,256]{3,2,1,0:T(1,128)S(1)}, u32[]{:S(2)}, u32[]{:S(2)}) collective-permute-start(f32[3,16,1,256]{3,2,1,0:T(1,128)S(1)} %slice.2361), channel_id=1, source_target_pairs={{0,1},{1,2},{2,3},{4,5},{5,6},{6,7},{8,9},{9,10},{10,11},{12,13},{... | collective-permute-start | bytes 147464 | tf_op jit(solution)/shard_map/ppermute | solution.py:16
  255.8 23.3 %copy-start.5 = (f32[9,16,8,256]{3,2,1,0:T(8,128)}, f32[9,16,8,256]{3,2,1,0:T(8,128)S(1)}, u32[]{:S(2)}) copy-start(f32[9,16,8,256]{3,2,1,0:T(8,128)S(1)} %pad_maximum_fusion.3) | copy-start | bytes 3538948
  255.8 3.0 copy-start.21
  255.8 3.0 copy-start.22
  255.8 3.0 copy-start.23
  255.8 3.0 copy-start.24
  255.8 3.0 copy-start.25
  255.8 3.0 copy-start.26
  256.0 23.1 %collective-permute-start.16 = (f32[9,9,8,256]{3,2,1,0:T(8,128)S(1)}, f32[9,9,8,256]{3,2,1,0:T(8,128)S(1)}, u32[]{:S(2)}, u32[]{:S(2)}) collective-permute-start(f32[9,9,8,256]{3,2,1,0:T(8,128)S(1)} %slice.2377), channel_id=1, source_target_pairs={{4,0},{8,4},{12,8},{16,12},{20,16},{24,20},{28,24},{5,1},{9,5},{13... | collective-permute-start | bytes 1990664 | tf_op jit(solution)/shard_map/ppermute | solution.py:16
  280.4 4.8 %collective-permute-start.17 = (f32[3,16,1,256]{3,2,1,0:T(1,128)S(1)}, f32[3,16,1,256]{3,2,1,0:T(1,128)S(1)}, u32[]{:S(2)}, u32[]{:S(2)}) collective-permute-start(f32[3,16,1,256]{3,2,1,0:T(1,128)S(1)} %slice.2389), channel_id=1, source_target_pairs={{1,0},{2,1},{3,2},{5,4},{6,5},{7,6},{9,8},{10,9},{11,10},{13,12},{... | collective-permute-start | bytes 147464 | tf_op jit(solution)/shard_map/ppermute | solution.py:16
  285.7 9.0 %collective-permute-start.19 = (f32[3,1,8,256]{3,2,1,0:T(8,128)S(1)}, f32[3,1,8,256]{3,2,1,0:T(8,128)S(1)}, u32[]{:S(2)}, u32[]{:S(2)}) collective-permute-start(f32[3,1,8,256]{3,2,1,0:T(8,128)S(1)} %slice.2406), channel_id=1, source_target_pairs={{0,4},{4,8},{8,12},{12,16},{16,20},{20,24},{24,28},{1,5},{5,9},{9,... | collective-permute-start | bytes 73736 | tf_op jit(solution)/shard_map/ppermute | solution.py:16
  291.5 4.8 %collective-permute-start.18 = (f32[3,16,1,256]{3,2,1,0:T(1,128)S(1)}, f32[3,16,1,256]{3,2,1,0:T(1,128)S(1)}, u32[]{:S(2)}, u32[]{:S(2)}) collective-permute-start(f32[3,16,1,256]{3,2,1,0:T(1,128)S(1)} %slice.2402), channel_id=1, source_target_pairs={{0,1},{1,2},{2,3},{4,5},{5,6},{6,7},{8,9},{9,10},{10,11},{12,13},{... | collective-permute-start | bytes 147464 | tf_op jit(solution)/shard_map/ppermute | solution.py:16
  296.7 22.8 %copy-start.6 = (f32[9,16,8,256]{3,2,1,0:T(8,128)}, f32[9,16,8,256]{3,2,1,0:T(8,128)S(1)}, u32[]{:S(2)}) copy-start(f32[9,16,8,256]{3,2,1,0:T(8,128)S(1)} %pad_maximum_fusion.4) | copy-start | bytes 3538948
  296.8 22.7 %collective-permute-start.20 = (f32[9,9,8,256]{3,2,1,0:T(8,128)S(1)}, f32[9,9,8,256]{3,2,1,0:T(8,128)S(1)}, u32[]{:S(2)}, u32[]{:S(2)}) collective-permute-start(f32[9,9,8,256]{3,2,1,0:T(8,128)S(1)} %slice.2418), channel_id=1, source_target_pairs={{4,0},{8,4},{12,8},{16,12},{20,16},{24,20},{28,24},{5,1},{9,5},{13... | collective-permute-start | bytes 1990664 | tf_op jit(solution)/shard_map/ppermute | solution.py:16
  320.9 4.8 %collective-permute-start.21 = (f32[3,16,1,256]{3,2,1,0:T(1,128)S(1)}, f32[3,16,1,256]{3,2,1,0:T(1,128)S(1)}, u32[]{:S(2)}, u32[]{:S(2)}) collective-permute-start(f32[3,16,1,256]{3,2,1,0:T(1,128)S(1)} %slice.2430), channel_id=1, source_target_pairs={{1,0},{2,1},{3,2},{5,4},{6,5},{7,6},{9,8},{10,9},{11,10},{13,12},{... | collective-permute-start | bytes 147464 | tf_op jit(solution)/shard_map/ppermute | solution.py:16
  326.1 9.0 %collective-permute-start.23 = (f32[3,1,8,256]{3,2,1,0:T(8,128)S(1)}, f32[3,1,8,256]{3,2,1,0:T(8,128)S(1)}, u32[]{:S(2)}, u32[]{:S(2)}) collective-permute-start(f32[3,1,8,256]{3,2,1,0:T(8,128)S(1)} %slice.2447), channel_id=1, source_target_pairs={{0,4},{4,8},{8,12},{12,16},{16,20},{20,24},{24,28},{1,5},{5,9},{9,... | collective-permute-start | bytes 73736 | tf_op jit(solution)/shard_map/ppermute | solution.py:16
  331.9 4.8 %collective-permute-start.22 = (f32[3,16,1,256]{3,2,1,0:T(1,128)S(1)}, f32[3,16,1,256]{3,2,1,0:T(1,128)S(1)}, u32[]{:S(2)}, u32[]{:S(2)}) collective-permute-start(f32[3,16,1,256]{3,2,1,0:T(1,128)S(1)} %slice.2443), channel_id=1, source_target_pairs={{0,1},{1,2},{2,3},{4,5},{5,6},{6,7},{8,9},{9,10},{10,11},{12,13},{... | collective-permute-start | bytes 147464 | tf_op jit(solution)/shard_map/ppermute | solution.py:16
  337.1 23.2 %copy-start.7 = (f32[9,16,8,256]{3,2,1,0:T(8,128)}, f32[9,16,8,256]{3,2,1,0:T(8,128)S(1)}, u32[]{:S(2)}) copy-start(f32[9,16,8,256]{3,2,1,0:T(8,128)S(1)} %pad_maximum_fusion.5) | copy-start | bytes 3538948
  337.4 23.0 %collective-permute-start.24 = (f32[9,9,8,256]{3,2,1,0:T(8,128)S(1)}, f32[9,9,8,256]{3,2,1,0:T(8,128)S(1)}, u32[]{:S(2)}, u32[]{:S(2)}) collective-permute-start(f32[9,9,8,256]{3,2,1,0:T(8,128)S(1)} %slice.2459), channel_id=1, source_target_pairs={{4,0},{8,4},{12,8},{16,12},{20,16},{24,20},{28,24},{5,1},{9,5},{13... | collective-permute-start | bytes 1990664 | tf_op jit(solution)/shard_map/ppermute | solution.py:16
  361.8 4.8 %collective-permute-start.25 = (f32[3,16,1,256]{3,2,1,0:T(1,128)S(1)}, f32[3,16,1,256]{3,2,1,0:T(1,128)S(1)}, u32[]{:S(2)}, u32[]{:S(2)}) collective-permute-start(f32[3,16,1,256]{3,2,1,0:T(1,128)S(1)} %slice.2471), channel_id=1, source_target_pairs={{1,0},{2,1},{3,2},{5,4},{6,5},{7,6},{9,8},{10,9},{11,10},{13,12},{... | collective-permute-start | bytes 147464 | tf_op jit(solution)/shard_map/ppermute | solution.py:16
  367.0 9.0 %collective-permute-start.27 = (f32[3,1,8,256]{3,2,1,0:T(8,128)S(1)}, f32[3,1,8,256]{3,2,1,0:T(8,128)S(1)}, u32[]{:S(2)}, u32[]{:S(2)}) collective-permute-start(f32[3,1,8,256]{3,2,1,0:T(8,128)S(1)} %slice.2488), channel_id=1, source_target_pairs={{0,4},{4,8},{8,12},{12,16},{16,20},{20,24},{24,28},{1,5},{5,9},{9,... | collective-permute-start | bytes 73736 | tf_op jit(solution)/shard_map/ppermute | solution.py:16
  372.8 4.8 %collective-permute-start.26 = (f32[3,16,1,256]{3,2,1,0:T(1,128)S(1)}, f32[3,16,1,256]{3,2,1,0:T(1,128)S(1)}, u32[]{:S(2)}, u32[]{:S(2)}) collective-permute-start(f32[3,16,1,256]{3,2,1,0:T(1,128)S(1)} %slice.2484), channel_id=1, source_target_pairs={{0,1},{1,2},{2,3},{4,5},{5,6},{6,7},{8,9},{9,10},{10,11},{12,13},{... | collective-permute-start | bytes 147464 | tf_op jit(solution)/shard_map/ppermute | solution.py:16
  378.0 23.1 %copy-start.4 = (f32[9,16,8,256]{3,2,1,0:T(8,128)}, f32[9,16,8,256]{3,2,1,0:T(8,128)S(1)}, u32[]{:S(2)}) copy-start(f32[9,16,8,256]{3,2,1,0:T(8,128)S(1)} %pad_maximum_fusion.6) | copy-start | bytes 3538948
  378.2 22.9 %collective-permute-start.28 = (f32[9,9,8,256]{3,2,1,0:T(8,128)S(1)}, f32[9,9,8,256]{3,2,1,0:T(8,128)S(1)}, u32[]{:S(2)}, u32[]{:S(2)}) collective-permute-start(f32[9,9,8,256]{3,2,1,0:T(8,128)S(1)} %slice.2500), channel_id=1, source_target_pairs={{4,0},{8,4},{12,8},{16,12},{20,16},{24,20},{28,24},{5,1},{9,5},{13... | collective-permute-start | bytes 1990664 | tf_op jit(solution)/shard_map/ppermute | solution.py:16
  402.5 4.8 %collective-permute-start.29 = (f32[3,16,1,256]{3,2,1,0:T(1,128)S(1)}, f32[3,16,1,256]{3,2,1,0:T(1,128)S(1)}, u32[]{:S(2)}, u32[]{:S(2)}) collective-permute-start(f32[3,16,1,256]{3,2,1,0:T(1,128)S(1)} %slice.2512), channel_id=1, source_target_pairs={{1,0},{2,1},{3,2},{5,4},{6,5},{7,6},{9,8},{10,9},{11,10},{13,12},{... | collective-permute-start | bytes 147464 | tf_op jit(solution)/shard_map/ppermute | solution.py:16
  407.7 10.9 %copy-start = (f32[3,16,8,256]{3,2,1,0:T(8,128)}, f32[3,16,8,256]{3,2,1,0:T(8,128)S(1)}, u32[]{:S(2)}) copy-start(f32[3,16,8,256]{3,2,1,0:T(8,128)S(1)} %slice_subtract_fusion) | copy-start | bytes 1179652
  407.7 9.0 %collective-permute-start.31 = (f32[3,1,8,256]{3,2,1,0:T(8,128)S(1)}, f32[3,1,8,256]{3,2,1,0:T(8,128)S(1)}, u32[]{:S(2)}, u32[]{:S(2)}) collective-permute-start(f32[3,1,8,256]{3,2,1,0:T(8,128)S(1)} %slice.2529), channel_id=1, source_target_pairs={{0,4},{4,8},{8,12},{12,16},{16,20},{20,24},{24,28},{1,5},{5,9},{9,... | collective-permute-start | bytes 73736 | tf_op jit(solution)/shard_map/ppermute | solution.py:16
  413.5 4.8 %collective-permute-start.30 = (f32[3,16,1,256]{3,2,1,0:T(1,128)S(1)}, f32[3,16,1,256]{3,2,1,0:T(1,128)S(1)}, u32[]{:S(2)}, u32[]{:S(2)}) collective-permute-start(f32[3,16,1,256]{3,2,1,0:T(1,128)S(1)} %slice.2525), channel_id=1, source_target_pairs={{0,1},{1,2},{2,3},{4,5},{5,6},{6,7},{8,9},{9,10},{10,11},{12,13},{... | collective-permute-start | bytes 147464 | tf_op jit(solution)/shard_map/ppermute | solution.py:16
  (46 other events, 123.0 us)
where the time goes:
time: 425 us; the launch traced here: 419 us
  other arithmetic  251 us (59%)
  starting transfers between devices  102 us (24%)
  waiting for transfers between devices  32.7 us (8%)
  local copies, waits for them, and re-layouts  20.5 us (5%)
  between operations  13.6 us (3%)
    another operation x20, other arithmetic, lookup(): return jnp.stack(results)  205 us
    ppermute x32, starting transfers between devices, from_behind(): lax.ppermute(value, axis, [(source, source + steps) for source in range(l...  102 us
    ppermute x32, waiting for transfers between devices, from_behind(): lax.ppermute(value, axis, [(source, source + steps) for source in range(l...  32.7 us
    unnamed x2, other arithmetic  20.8 us
    concatenate x8, other arithmetic, body(): stacked = jnp.concatenate([electric, magnetic, coefs], 0)  10.7 us
  transfers between devices with their start and end apart: 32, of which 16 were waited for; matrix products, arithmetic and copies ran while one was open for 50% of the time, Pallas kernels for 0%

commit v1 on v0

v1 whole, which is shorter than its diff:
```python
import functools

import jax
import jax.numpy as jnp
from jax import lax
from jax.experimental import pallas as pl
from jax.experimental.pallas import tpu as pltpu
from jax.sharding import PartitionSpec as P

STEPS = 8
SHIFTS = 4
SHIFT = 8
HALO = STEPS
MAT = 16
LANES = 128


def permute(value, axis, pairs):
    return lax.ppermute(value, axis, pairs)


def neighbour(value, axis, hop):
    count = lax.axis_size(axis)
    pairs = [(s, s + hop) for s in range(count) if 0 <= s + hop < count]
    return permute(value, axis, pairs)


def swap_cores(value):
    return permute(value, "gz", [(s, s ^ 1) for s in range(lax.axis_size("gz"))])


def outer_halo(value):
    count = lax.axis_size("gz")
    pairs = [(s, s - 1) for s in range(1, count, 2)]
    pairs += [(s, s - 3) for s in range(4, count, 2)]
    pairs += [(0, count - 3)]
    return permute(value, "gz", pairs)


def step_kernel(
    planes, rows,
    pos, flags, tables,
    e_dn, e_mid, e_up, h_dn, h_mid, h_up,
    ze_dn, ze_mid, ze_up, zh_dn, zh_mid, zh_up,
    o_dn, o_mid, o_up,
    e_out, h_out,
    E, H, M, A, B, K, sems, out_sems,
):
    gz, gy, last_y = pos[0], pos[1], pos[2]
    top_z = pos[3]
    wide = planes + 2 * HALO
    odd = lax.rem(gz, 2)
    inner_at = pl.multiple_of((1 - odd) * (planes + HALO), HALO)
    outer_at = pl.multiple_of(odd * (planes + HALO), HALO)
    copies = []

    def copy(src, dst):
        one = pltpu.make_async_copy(src, dst, sems.at[len(copies)])
        one.start()
        copies.append(one)

    for b, (e, h, ze, zh, o) in enumerate(
        ((e_dn, h_dn, ze_dn, zh_dn, o_dn), (e_mid, h_mid, ze_mid, zh_mid, o_mid), (e_up, h_up, ze_up, zh_up, o_up))
    ):
        at = pl.ds(b * rows, rows)
        main, inner, outer = pl.ds(HALO, planes), pl.ds(inner_at, HALO), pl.ds(outer_at, HALO)
        copy(h.at[3], M.at[main, at])
        copy(zh.at[3], M.at[inner, at])
        copy(o.at[6], M.at[outer, at])
        copy(e, E.at[:, main, at])
        copy(ze, E.at[:, inner, at])
        copy(o.at[pl.ds(0, 3)], E.at[:, outer, at])
        copy(h.at[pl.ds(0, 3)], H.at[:, main, at])
        copy(zh.at[pl.ds(0, 3)], H.at[:, inner, at])
        copy(o.at[pl.ds(3, 3)], H.at[:, outer, at])
    for one in copies:
        one.wait()

    tile = (8, LANES)
    lane = lax.broadcasted_iota(jnp.int32, tile, 1)
    sub = lax.broadcasted_iota(jnp.int32, tile, 0)
    lane_first, lane_last = lane == 0, lane == LANES - 1
    sub_first, sub_last = sub == 0, sub == 7
    zero = jnp.zeros(tile, jnp.float32)
    tiles = 3
    below = jnp.where(gy == 0, 0.0, 1.0).astype(jnp.float32)
    above = jnp.where(gy == last_y, 0.0, 1.0).astype(jnp.float32)
    halves = (slice(0, LANES), slice(LANES, 2 * LANES))

    def spot(t):
        return slice(8 * t, 8 * t + 8)

    tab = [tables[i] for i in range(3)]

    def prepare(p, carry):
        for t in range(tiles):
            for x in halves:
                ids = M[p, spot(t), x].astype(jnp.int32)
                for out, table in zip((A, B, K), tab):
                    out[p, spot(t), x] = jnp.take_along_axis(table, ids, axis=1)
                for c in range(3):
                    H[c, p, spot(t), x] = 2.0 * H[c, p, spot(t), x]
        return carry

    lax.fori_loop(0, wide, prepare, 0)
    E[:, wide] = jnp.zeros((3, tiles * 8, 2 * LANES), jnp.float32)

    def load(ref, c, p, t):
        return [ref[c, p, spot(t), x] for x in halves]

    def x_next(v):
        r = [pltpu.roll(a, LANES - 1, 1) for a in v]
        return [jnp.where(lane_last, r[1], r[0]), jnp.where(lane_last, zero, r[1])]

    def x_prev(v):
        r = [pltpu.roll(a, 1, 1) for a in v]
        return [jnp.where(lane_first, zero, r[0]), jnp.where(lane_first, r[0], r[1])]

    def y_next(parts):
        r = [[pltpu.roll(a, 7, 0) for a in v] for v in parts]
        result = []
        for t in range(tiles):
            if t == tiles - 1:
                result.append(r[t])
                continue
            far = r[t + 1] if t != 1 else [a * above for a in r[t + 1]]
            result.append([jnp.where(sub_last, a, b) for a, b in zip(far, r[t])])
        return result

    def y_prev(parts):
        r = [[pltpu.roll(a, 1, 0) for a in v] for v in parts]
        result = []
        for t in range(tiles):
            if t == 0:
                result.append(r[t])
                continue
            far = r[t - 1] if t != 1 else [a * below for a in r[t - 1]]
            result.append([jnp.where(sub_first, a, b) for a, b in zip(far, r[t])])
        return result

    def magnetic_plane(p):
        ex, ey, ez = [[load(E, c, p, t) for t in range(tiles)] for c in range(3)]
        ez_y, ex_y = y_next(ez), y_next(ex)
        for t in range(tiles):
            ez_x, ey_x = x_next(ez[t]), x_next(ey[t])
            ey_z, ex_z = load(E, 1, p + 1, t), load(E, 0, p + 1, t)
            hx, hy, hz = [load(H, c, p, t) for c in range(3)]
            for i, x in enumerate(halves):
                H[0, p, spot(t), x] = hx[i] - ((ez_y[t][i] - ez[t][i]) - (ey_z[i] - ey[t][i]))
                H[1, p, spot(t), x] = hy[i] - ((ex_z[i] - ex[t][i]) - (ez_x[i] - ez[t][i]))
                H[2, p, spot(t), x] = hz[i] - ((ey_x[i] - ey[t][i]) - (ex_y[t][i] - ex[t][i]))

    def electric_plane(p):
        hx, hy, hz = [[load(H, c, p, t) for t in range(tiles)] for c in range(3)]
        hz_y, hx_y = y_prev(hz), y_prev(hx)
        for t in range(tiles):
            hz_x, hy_x = x_prev(hz[t]), x_prev(hy[t])
            hy_z, hx_z = load(H, 1, p - 1, t), load(H, 0, p - 1, t)
            ex, ey, ez = [load(E, c, p, t) for c in range(3)]
            for i, x in enumerate(halves):
                cx = (hz[t][i] - hz_y[t][i]) - (hy[t][i] - hy_z[i])
                cy = (hx[t][i] - hx_z[i]) - (hz[t][i] - hz_x[i])
                cz = (hy[t][i] - hy_x[i]) - (hx[t][i] - hx_y[t][i])
                n = K[p, spot(t), x] * (ex[i] * ex[i] + ey[i] * ey[i] + ez[i] * ez[i])
                up = A[p, spot(t), x] + n
                down = B[p, spot(t), x] + n
                guess = pl.reciprocal(down, approx=True)
                r = guess * (2.0 - down * guess)
                E[0, p, spot(t), x] = (up * ex[i] + cx) * r
                E[1, p, spot(t), x] = (up * ey[i] + cy) * r
                E[2, p, spot(t), x] = (up * ez[i] + cz) * r

    def zero_plane(ref, p):
        @pl.when((p >= 0) & (p < wide))
        def _():
            ref[:, p] = jnp.zeros((3, tiles * 8, 2 * LANES), jnp.float32)

    base = planes * gz + SHIFT * SHIFTS - HALO

    def step(s, moved):
        moved = moved + flags[s - 1]

        def magnetic_loop(p, carry):
            magnetic_plane(p)
            return carry

        def electric_loop(p, carry):
            electric_plane(p)
            return carry

        lax.fori_loop(s - 1, wide - s, magnetic_loop, 0)
        zero_plane(H, SHIFT * moved - 1 - base)
        lax.fori_loop(s, wide - s, electric_loop, 0)
        zero_plane(E, top_z + SHIFT * moved - base)
        return moved

    lax.fori_loop(1, STEPS + 1, step, jnp.int32(0))

    def finish(p, carry):
        for c in range(3):
            for x in halves:
                H[c, p, spot(1), x] = 0.5 * H[c, p, spot(1), x]
        return carry

    lax.fori_loop(HALO, HALO + planes, finish, 0)
    outs = [
        pltpu.make_async_copy(ref.at[:, pl.ds(HALO, planes), pl.ds(rows, rows)], out, out_sems.at[i])
        for i, (ref, out) in enumerate(((E, e_out), (H, h_out)))
    ]
    for one in outs:
        one.start()
    for one in outs:
        one.wait()


def run_steps(pos, flags, tables, pieces, planes, rows, width):
    wide = planes + 2 * HALO
    tall = 3 * rows
    smem = pl.BlockSpec(memory_space=pltpu.SMEM)
    field = jax.ShapeDtypeStruct((3, planes, rows, width), jnp.float32)
    vec = [(3, wide + 1, tall, width), (3, wide, tall, width)] + [(wide, tall, width)] * 4
    return pl.pallas_call(
        functools.partial(step_kernel, planes, rows),
        out_shape=(field, field),
        in_specs=[smem, smem, pl.BlockSpec(memory_space=pltpu.VMEM)] + [pl.BlockSpec(memory_space=pl.ANY)] * len(pieces),
        out_specs=(pl.BlockSpec(memory_space=pl.ANY),) * 2,
        scratch_shapes=[pltpu.VMEM(shape, jnp.float32) for shape in vec]
        + [pltpu.SemaphoreType.DMA((27,)), pltpu.SemaphoreType.DMA((2,))],
        compiler_params=pltpu.CompilerParams(vmem_limit_bytes=24 * 2**20),
        name="fdtd_steps",
    )(pos, flags, tables, *pieces)


def body(electric, magnetic, material, incoming, shift_flags, eps_table, sigma_table, kerr_table):
    count_z, count_y = lax.axis_size("gz"), lax.axis_size("gy")
    _, planes, rows, width = electric.shape
    hop = SHIFTS * SHIFT // planes
    assert hop * planes == SHIFTS * SHIFT and hop == 2 and planes == 2 * HALO
    assert rows == HALO and width == 2 * LANES and count_z % 2 == 0 and count_z >= 4
    gz, gy = lax.axis_index("gz"), lax.axis_index("gy")
    odd = gz % 2 == 1

    ids = material.astype(jnp.float32)
    fresh = incoming.astype(jnp.float32)

    moved_e = neighbour(electric, "gz", -hop)
    moved_hm = neighbour(jnp.concatenate([magnetic, ids[None]], 0), "gz", -hop)
    fresh_at = jnp.clip(gz - (count_z - hop), 0, hop - 1) * planes
    fresh_ids = lax.dynamic_slice_in_dim(fresh, fresh_at, planes, 0)
    moved_hm = jnp.concatenate(
        [moved_hm[:3], jnp.where(gz >= count_z - hop, fresh_ids, moved_hm[3])[None]], 0
    )

    def edge(field):
        return jnp.where(odd, field[:, HALO:], jnp.where(gz == 0, 0.0, field[:, :HALO]))

    edge_ids = jnp.where(odd, ids[HALO:], jnp.where(gz == 0, fresh[:HALO], ids[:HALO]))
    outer = jnp.concatenate([edge(electric), edge(magnetic), edge_ids[None]], 0)
    o_up, o_dn = neighbour(outer, "gy", -1), neighbour(outer, "gy", 1)
    o_all = outer_halo(jnp.stack([o_dn, outer, o_up]))

    def inner(field):
        return swap_cores(jnp.where(odd, field[:, :HALO], field[:, HALO:]))

    def around(field):
        up, dn = neighbour(field, "gy", -1), neighbour(field, "gy", 1)
        return [dn, field, up], [inner(dn), inner(field), inner(up)]

    e_main, e_inner = around(moved_e)
    h_main, h_inner = around(moved_hm)

    tables = jnp.stack(
        [4.0 * eps_table - 2.0 * sigma_table, 4.0 * eps_table + 2.0 * sigma_table, 4.0 * kerr_table]
    )
    tables = jnp.broadcast_to(jnp.pad(tables, ((0, 0), (0, LANES - MAT)))[:, None, :], (3, 8, LANES))
    pos = jnp.stack([gz, gy, count_y - 1, count_z * planes]).astype(jnp.int32)
    pieces = e_main + h_main + e_inner + h_inner + [o_all[0], o_all[1], o_all[2]]
    return run_steps(pos, shift_flags, tables, pieces, planes, rows, width)


def solution(mesh):
    field = P(None, "gz", "gy", None)
    return jax.shard_map(
        body,
        mesh=mesh,
        in_specs=(field, field, P("gz", "gy", None), P(None, "gy", None), P(), P(), P(), P()),
        out_specs=(field, field),
        check_vma=False,
    )
```

time: 425 us -> 96.6 us (0.23); the launches traced: 419 us -> 96.2 us
  other arithmetic: 251 us -> 5.29 us
  starting transfers between devices: 102 us -> 30.4 us
  Pallas kernels: 0 us -> 38.8 us
  local copies, waits for them, and re-layouts: 20.5 us -> 0.16 us
  between operations: 13.6 us -> 0.95 us
  waiting for transfers between devices: 32.7 us -> 20.7 us
    another operation x36 -> x5, other arithmetic: 207 us -> 0.94 us  [the longest x2 0.69 us: body(): jnp.stack([4.0 * eps_table - 2.0 * sigma_table, 4.0 * eps_table + 2.0 * s...]
    ppermute x32 -> x15, starting transfers between devices: 102 us -> 30.4 us  [permute(): return lax.ppermute(value, axis, pairs)]
    pallas_call x0 -> x1, Pallas kernels: none -> 38.8 us  [run_steps(): pl.pallas_call(functools.partial(step_kernel, planes, rows), out_shape=(f...]
    unnamed x2 -> x0, other arithmetic: 20.8 us -> none
    slice x131 -> x1, local copies, waits for them, and re-layouts: 17.9 us -> 0.03 us  [body(): moved_hm[:3]]
    ppermute x32 -> x15, waiting for transfers between devices: 32.7 us -> 20.7 us  [permute(): return lax.ppermute(value, axis, pairs)]
    concatenate x8 -> x2, other arithmetic: 10.7 us -> 0.07 us  [the longest x1 0.04 us: body(): moved_hm = neighbour(jnp.concatenate([magnetic, ids[None]], 0), 'gz', -hop)]
    select_n x24 -> x8, other arithmetic: 8.47 us -> 2.34 us  [the longest x2 2.16 us: edge(): jnp.where(odd, field[:, HALO:], jnp.where(gz == 0, 0.0, field[:, :HALO]))]
  transfers between devices with their start and end apart: 32 -> 15, of which waited for: 16 -> 6; matrix products, arithmetic and copies ran while one was open for 50% -> 1% of each run, Pallas kernels for 0% -> 0%
where the time goes in v1:
time: 96.6 us; the launch traced here: 96.2 us
  Pallas kernels  38.8 us (40%)
  starting transfers between devices  30.4 us (31%)
  waiting for transfers between devices  20.7 us (21%)
  other arithmetic  5.29 us (5%)
    pallas_call x1, Pallas kernels, run_steps(): pl.pallas_call(functools.partial(step_kernel, planes, rows), out_shape=(f...  38.8 us
    ppermute x15, starting transfers between devices, permute(): return lax.ppermute(value, axis, pairs)  30.4 us
    ppermute x15, waiting for transfers between devices, permute(): return lax.ppermute(value, axis, pairs)  20.7 us
    select_n x2, other arithmetic, edge(): jnp.where(odd, field[:, HALO:], jnp.where(gz == 0, 0.0, field[:, :HALO]))  2.16 us
  transfers between devices with their start and end apart: 15, of which 6 were waited for; matrix products, arithmetic and copies ran while one was open for 1% of the time, Pallas kernels for 0%

profile of v1, /device:TPU:11, one launch (start us, length us, event | category | flops | bytes accessed | tf_op | source)
XLA Modules:
  0.0 96.2 jit_solution(7357529060736921457)
XLA Ops:
  0.6 0.9 fusion.8
  1.6 1.0 %convert_element_type.9 = f32[32,8,256]{2,1,0:T(8,128)S(1)} convert(s32[32,8,256]{2,1,0:T(8,128)} %param.11) | non-fusion elementwise | flops 65536 | bytes 524288 | tf_op jit(solution)/shard_map/convert_element_type | solution.py:244
  2.5 0.0 copy-start.1
  2.6 1.1 %select_select_fusion = f32[3,8,8,256]{3,2,1,0:T(8,128)S(1)} fusion(f32[3,16,8,256]{3,2,1,0:T(8,128)} %param.9, pred[]{:T(512)S(6)} %eq.11, pred[]{:T(512)S(6)} %eq.10), kind=kLoop, calls=%fused_computation.19 | loop fusion | flops 98304 | bytes 589826 | tf_op jit(solution)/shard_map/jit(_where)/select_n | solution.py:255
  3.7 1.1 %select_select_fusion.1 = f32[3,8,8,256]{3,2,1,0:T(8,128)S(1)} fusion(f32[3,16,8,256]{3,2,1,0:T(8,128)} %param.8, pred[]{:T(512)S(6)} %eq.11, pred[]{:T(512)S(6)} %eq.10), kind=kLoop, calls=%fused_computation.20 | loop fusion | flops 98304 | bytes 589826 | tf_op jit(solution)/shard_map/jit(_where)/select_n | solution.py:255
  4.7 0.0 copy-start.2
  4.8 0.1 fusion.7
  4.9 2.1 %collective-permute-start.13 = (f32[7,8,8,256]{3,2,1,0:T(8,128)S(1)}, f32[7,8,8,256]{3,2,1,0:T(8,128)S(1)}, u32[]{:S(2)}, u32[]{:S(2)}) collective-permute-start(f32[7,8,8,256]{3,2,1,0:T(8,128)S(1)} %get-tuple-element.6), channel_id=1, source_target_pairs={{1,0},{2,1},{3,2},{5,4},{6,5},{7,6},{9,8},{10,9},{11,10},{13,12},{... | collective-permute-start | bytes 1376264 | tf_op jit(solution)/shard_map/ppermute | solution.py:19
  6.9 3.2 %collective-permute-start.12 = (f32[7,8,8,256]{3,2,1,0:T(8,128)S(1)}, f32[7,8,8,256]{3,2,1,0:T(8,128)S(1)}, u32[]{:S(2)}, u32[]{:S(2)}) collective-permute-start(f32[7,8,8,256]{3,2,1,0:T(8,128)S(1)} %get-tuple-element.6), channel_id=1, source_target_pairs={{0,1},{1,2},{2,3},{4,5},{5,6},{6,7},{8,9},{9,10},{10,11},{12,13},{... | collective-permute-start | bytes 1376264 | tf_op jit(solution)/shard_map/ppermute | solution.py:19
  10.1 2.2 %collective-permute-start = (f32[3,16,8,256]{3,2,1,0:T(8,128)}, f32[3,16,8,256]{3,2,1,0:T(8,128)S(1)}, u32[]{:S(2)}, u32[]{:S(2)}) collective-permute-start(f32[3,16,8,256]{3,2,1,0:T(8,128)} %param.8), channel_id=1, source_target_pairs={{8,0},{12,4},{16,8},{20,12},{24,16},{28,20},{9,1},{13,5},{17,9},{2... | collective-permute-start | bytes 1179656 | tf_op jit(solution)/shard_map/ppermute | solution.py:19
  12.3 0.0 copy-done.1
  12.4 1.9 %collective-permute-start.3 = (f32[4,16,8,256]{3,2,1,0:T(8,128)S(1)}, f32[4,16,8,256]{3,2,1,0:T(8,128)S(1)}, u32[]{:S(2)}, u32[]{:S(2)}) collective-permute-start(f32[4,16,8,256]{3,2,1,0:T(8,128)S(1)} %pad_maximum_fusion.2), channel_id=1, source_target_pairs={{8,0},{12,4},{16,8},{20,12},{24,16},{28,20},{9,1},{13,5},{17,9},{2... | collective-permute-start | bytes 1572872 | tf_op jit(solution)/shard_map/ppermute | solution.py:19
  14.3 0.0 copy-done.2
  14.3 0.7 subtract_bitcast_fusion
  15.0 0.1 pad_add_fusion.pos
  15.1 7.4 %collective-permute-done.e_mid = f32[3,16,8,256]{3,2,1,0:T(8,128)S(1)} collective-permute-done((f32[3,16,8,256]{3,2,1,0:T(8,128)}, f32[3,16,8,256]{3,2,1,0:T(8,128)S(1)}, u32[]{:S(2)}, u32[]{:S(2)}) %collective-permute-start) | collective-permute-done | bytes 393248 | tf_op jit(solution)/shard_map/ppermute | solution.py:19
  22.6 4.0 %collective-permute-start.7 = (f32[3,8,8,256]{3,2,1,0:T(8,128)S(1)}, f32[3,8,8,256]{3,2,1,0:T(8,128)S(1)}, u32[]{:S(2)}, u32[]{:S(2)}) collective-permute-start(f32[3,8,8,256]{3,2,1,0:T(8,128)S(1)} %slice_select_fusion.3), channel_id=1, source_target_pairs={{0,4},{4,0},{8,12},{12,8},{16,20},{20,16},{24,28},{28,24},{1,5},{5... | collective-permute-start | bytes 589832 | tf_op jit(solution)/shard_map/ppermute | solution.py:19
  26.5 3.2 %collective-permute-start.1 = (f32[3,16,8,256]{3,2,1,0:T(8,128)S(1)}, f32[3,16,8,256]{3,2,1,0:T(8,128)S(1)}, u32[]{:S(2)}, u32[]{:S(2)}) collective-permute-start(f32[3,16,8,256]{3,2,1,0:T(8,128)S(1)} %collective-permute-done.e_mid), channel_id=1, source_target_pairs={{0,1},{1,2},{2,3},{4,5},{5,6},{6,7},{8,9},{9,10},{10,11},{12,13},{... | collective-permute-start | bytes 1179656 | tf_op jit(solution)/shard_map/ppermute | solution.py:19
  29.8 0.0 collective-permute-done.13
  29.8 2.1 %collective-permute-start.2 = (f32[3,16,8,256]{3,2,1,0:T(8,128)S(1)}, f32[3,16,8,256]{3,2,1,0:T(8,128)S(1)}, u32[]{:S(2)}, u32[]{:S(2)}) collective-permute-start(f32[3,16,8,256]{3,2,1,0:T(8,128)S(1)} %collective-permute-done.e_mid), channel_id=1, source_target_pairs={{1,0},{2,1},{3,2},{5,4},{6,5},{7,6},{9,8},{10,9},{11,10},{13,12},{... | collective-permute-start | bytes 1179656 | tf_op jit(solution)/shard_map/ppermute | solution.py:19
  31.9 0.0 collective-permute-done.12
  31.9 0.1 pad_maximum_fusion
  32.0 2.5 %collective-permute-start.14 = (f32[3,7,8,8,256]{4,3,2,1,0:T(8,128)S(1)}, f32[3,7,8,8,256]{4,3,2,1,0:T(8,128)S(1)}, u32[]{:S(2)}, u32[]{:S(2)}) collective-permute-start(f32[3,7,8,8,256]{4,3,2,1,0:T(8,128)S(1)} %pad_maximum_fusion), channel_id=1, source_target_pairs={{4,0},{12,8},{20,16},{28,24},{16,4},{24,12},{0,20},{5,1},{13,9},{2... | collective-permute-start | bytes 4128776 | tf_op jit(solution)/shard_map/ppermute | solution.py:19
  34.5 0.0 collective-permute-done.3
  34.6 1.9 %collective-permute-start.5 = (f32[4,16,8,256]{3,2,1,0:T(8,128)S(1)}, f32[4,16,8,256]{3,2,1,0:T(8,128)S(1)}, u32[]{:S(2)}, u32[]{:S(2)}) collective-permute-start(f32[4,16,8,256]{3,2,1,0:T(8,128)S(1)} %pad_maximum_fusion.1.h_mid), channel_id=1, source_target_pairs={{1,0},{2,1},{3,2},{5,4},{6,5},{7,6},{9,8},{10,9},{11,10},{13,12},{... | collective-permute-start | bytes 1572872 | tf_op jit(solution)/shard_map/ppermute | solution.py:19
  36.6 2.6 %collective-permute-done.1.e_dn = f32[3,16,8,256]{3,2,1,0:T(8,128)S(1)} collective-permute-done((f32[3,16,8,256]{3,2,1,0:T(8,128)S(1)}, f32[3,16,8,256]{3,2,1,0:T(8,128)S(1)}, u32[]{:S(2)}, u32[]{:S(2)}) %collective-permute-start.1) | collective-permute-done | bytes 393248 | tf_op jit(solution)/shard_map/ppermute | solution.py:19
  39.1 3.2 %collective-permute-start.4 = (f32[4,16,8,256]{3,2,1,0:T(8,128)S(1)}, f32[4,16,8,256]{3,2,1,0:T(8,128)S(1)}, u32[]{:S(2)}, u32[]{:S(2)}) collective-permute-start(f32[4,16,8,256]{3,2,1,0:T(8,128)S(1)} %pad_maximum_fusion.1.h_mid), channel_id=1, source_target_pairs={{0,1},{1,2},{2,3},{4,5},{5,6},{6,7},{8,9},{9,10},{10,11},{12,13},{... | collective-permute-start | bytes 1572872 | tf_op jit(solution)/shard_map/ppermute | solution.py:19
  42.4 0.0 collective-permute-done.2.e_up
  42.4 1.5 %collective-permute-start.10 = (f32[4,8,8,256]{3,2,1,0:T(8,128)S(1)}, f32[4,8,8,256]{3,2,1,0:T(8,128)S(1)}, u32[]{:S(2)}, u32[]{:S(2)}) collective-permute-start(f32[4,8,8,256]{3,2,1,0:T(8,128)S(1)} %fusion.1), channel_id=1, source_target_pairs={{0,4},{4,0},{8,12},{12,8},{16,20},{20,16},{24,28},{28,24},{1,5},{5... | collective-permute-start | bytes 786440 | tf_op jit(solution)/shard_map/ppermute | solution.py:19
  44.0 9.3 %collective-permute-done.5.h_up = f32[4,16,8,256]{3,2,1,0:T(8,128)S(1)} collective-permute-done((f32[4,16,8,256]{3,2,1,0:T(8,128)S(1)}, f32[4,16,8,256]{3,2,1,0:T(8,128)S(1)}, u32[]{:S(2)}, u32[]{:S(2)}) %collective-permute-start.5) | collective-permute-done | bytes 524320 | tf_op jit(solution)/shard_map/ppermute | solution.py:19
  53.3 1.1 %collective-permute-start.6 = (f32[3,8,8,256]{3,2,1,0:T(8,128)S(1)}, f32[3,8,8,256]{3,2,1,0:T(8,128)S(1)}, u32[]{:S(2)}, u32[]{:S(2)}) collective-permute-start(f32[3,8,8,256]{3,2,1,0:T(8,128)S(1)} %slice_select_fusion.4), channel_id=1, source_target_pairs={{0,4},{4,0},{8,12},{12,8},{16,20},{20,16},{24,28},{28,24},{1,5},{5... | collective-permute-start | bytes 589832 | tf_op jit(solution)/shard_map/ppermute | solution.py:19
  54.5 0.0 collective-permute-done.4.h_dn
  54.5 0.9 collective-permute-start.8
  55.4 0.0 copy-start
  55.4 0.0 collective-permute-done.7.ze_mid
  55.4 0.1 collective-permute-start.11
  55.5 0.0 collective-permute-done.14
  55.5 0.5 collective-permute-start.9
  56.0 0.1 slice_bitcast_fusion
  56.1 0.0 collective-permute-done.10.zh_mid
  56.1 0.0 collective-permute-done.6.ze_dn
  56.1 0.3 collective-permute-done.8.ze_up
  56.4 0.6 collective-permute-done.11.zh_up
  57.0 0.4 collective-permute-done.9.zh_dn
  57.4 0.0 copy-done
  57.4 38.8 %fdtd_steps.1 = (f32[3,16,8,256]{3,2,1,0:T(8,128)}, f32[3,16,8,256]{3,2,1,0:T(8,128)}) custom-call(s32[4]{0:T(128)S(1)} %pad_add_fusion.pos, s32[8]{0:T(128)S(1)} %copy-done, f32[3,8,128]{2,1,0:T(8,128)S(1)} %broadcast_in_dim.20.tables, f32[3,16,8,256]{3,2,1,0:T(8,128)S(1)} %collective-permute-done.1.e_dn, f32[3,16,8,256]{3,2,1,0:T(8,128)S(1)} %collective-permute-done.e_mid, ...), custom_call_target="tpu_custom_call" | custom-call | tf_op jit(solution)/shard_map/fdtd_steps/pallas_call | solution.py:222
  (13 shorter events, 0.3 us)
Async XLA Ops:
  2.5 9.8 %copy-start.1 = (f32[3,16,8,256]{3,2,1,0:T(8,128)S(1)}, f32[3,16,8,256]{3,2,1,0:T(8,128)}, u32[]{:S(2)}) copy-start(f32[3,16,8,256]{3,2,1,0:T(8,128)} %param.9) | copy-start | bytes 1179652
  4.7 9.6 %copy-start.2 = (f32[16]{0:T(128)S(1)}, f32[16]{0:T(128)}, u32[]{:S(2)}) copy-start(f32[16]{0:T(128)} %param.14) | copy-start | bytes 196
  4.9 24.9 %collective-permute-start.13 = (f32[7,8,8,256]{3,2,1,0:T(8,128)S(1)}, f32[7,8,8,256]{3,2,1,0:T(8,128)S(1)}, u32[]{:S(2)}, u32[]{:S(2)}) collective-permute-start(f32[7,8,8,256]{3,2,1,0:T(8,128)S(1)} %get-tuple-element.6), channel_id=1, source_target_pairs={{1,0},{2,1},{3,2},{5,4},{6,5},{7,6},{9,8},{10,9},{11,10},{13,12},{... | collective-permute-start | bytes 1376264 | tf_op jit(solution)/shard_map/ppermute | solution.py:19
  6.9 24.9 %collective-permute-start.12 = (f32[7,8,8,256]{3,2,1,0:T(8,128)S(1)}, f32[7,8,8,256]{3,2,1,0:T(8,128)S(1)}, u32[]{:S(2)}, u32[]{:S(2)}) collective-permute-start(f32[7,8,8,256]{3,2,1,0:T(8,128)S(1)} %get-tuple-element.6), channel_id=1, source_target_pairs={{0,1},{1,2},{2,3},{4,5},{5,6},{6,7},{8,9},{9,10},{10,11},{12,13},{... | collective-permute-start | bytes 1376264 | tf_op jit(solution)/shard_map/ppermute | solution.py:19
  10.1 12.4 %collective-permute-start = (f32[3,16,8,256]{3,2,1,0:T(8,128)}, f32[3,16,8,256]{3,2,1,0:T(8,128)S(1)}, u32[]{:S(2)}, u32[]{:S(2)}) collective-permute-start(f32[3,16,8,256]{3,2,1,0:T(8,128)} %param.8), channel_id=1, source_target_pairs={{8,0},{12,4},{16,8},{20,12},{24,16},{28,20},{9,1},{13,5},{17,9},{2... | collective-permute-start | bytes 1179656 | tf_op jit(solution)/shard_map/ppermute | solution.py:19
  12.4 22.1 %collective-permute-start.3 = (f32[4,16,8,256]{3,2,1,0:T(8,128)S(1)}, f32[4,16,8,256]{3,2,1,0:T(8,128)S(1)}, u32[]{:S(2)}, u32[]{:S(2)}) collective-permute-start(f32[4,16,8,256]{3,2,1,0:T(8,128)S(1)} %pad_maximum_fusion.2), channel_id=1, source_target_pairs={{8,0},{12,4},{16,8},{20,12},{24,16},{28,20},{9,1},{13,5},{17,9},{2... | collective-permute-start | bytes 1572872 | tf_op jit(solution)/shard_map/ppermute | solution.py:19
  22.6 32.9 %collective-permute-start.7 = (f32[3,8,8,256]{3,2,1,0:T(8,128)S(1)}, f32[3,8,8,256]{3,2,1,0:T(8,128)S(1)}, u32[]{:S(2)}, u32[]{:S(2)}) collective-permute-start(f32[3,8,8,256]{3,2,1,0:T(8,128)S(1)} %slice_select_fusion.3), channel_id=1, source_target_pairs={{0,4},{4,0},{8,12},{12,8},{16,20},{20,16},{24,28},{28,24},{1,5},{5... | collective-permute-start | bytes 589832 | tf_op jit(solution)/shard_map/ppermute | solution.py:19
  26.5 12.6 %collective-permute-start.1 = (f32[3,16,8,256]{3,2,1,0:T(8,128)S(1)}, f32[3,16,8,256]{3,2,1,0:T(8,128)S(1)}, u32[]{:S(2)}, u32[]{:S(2)}) collective-permute-start(f32[3,16,8,256]{3,2,1,0:T(8,128)S(1)} %collective-permute-done.e_mid), channel_id=1, source_target_pairs={{0,1},{1,2},{2,3},{4,5},{5,6},{6,7},{8,9},{9,10},{10,11},{12,13},{... | collective-permute-start | bytes 1179656 | tf_op jit(solution)/shard_map/ppermute | solution.py:19
  29.8 12.6 %collective-permute-start.2 = (f32[3,16,8,256]{3,2,1,0:T(8,128)S(1)}, f32[3,16,8,256]{3,2,1,0:T(8,128)S(1)}, u32[]{:S(2)}, u32[]{:S(2)}) collective-permute-start(f32[3,16,8,256]{3,2,1,0:T(8,128)S(1)} %collective-permute-done.e_mid), channel_id=1, source_target_pairs={{1,0},{2,1},{3,2},{5,4},{6,5},{7,6},{9,8},{10,9},{11,10},{13,12},{... | collective-permute-start | bytes 1179656 | tf_op jit(solution)/shard_map/ppermute | solution.py:19
  32.0 23.5 %collective-permute-start.14 = (f32[3,7,8,8,256]{4,3,2,1,0:T(8,128)S(1)}, f32[3,7,8,8,256]{4,3,2,1,0:T(8,128)S(1)}, u32[]{:S(2)}, u32[]{:S(2)}) collective-permute-start(f32[3,7,8,8,256]{4,3,2,1,0:T(8,128)S(1)} %pad_maximum_fusion), channel_id=1, source_target_pairs={{4,0},{12,8},{20,16},{28,24},{16,4},{24,12},{0,20},{5,1},{13,9},{2... | collective-permute-start | bytes 4128776 | tf_op jit(solution)/shard_map/ppermute | solution.py:19
  34.6 18.7 %collective-permute-start.5 = (f32[4,16,8,256]{3,2,1,0:T(8,128)S(1)}, f32[4,16,8,256]{3,2,1,0:T(8,128)S(1)}, u32[]{:S(2)}, u32[]{:S(2)}) collective-permute-start(f32[4,16,8,256]{3,2,1,0:T(8,128)S(1)} %pad_maximum_fusion.1.h_mid), channel_id=1, source_target_pairs={{1,0},{2,1},{3,2},{5,4},{6,5},{7,6},{9,8},{10,9},{11,10},{13,12},{... | collective-permute-start | bytes 1572872 | tf_op jit(solution)/shard_map/ppermute | solution.py:19
  39.1 15.3 %collective-permute-start.4 = (f32[4,16,8,256]{3,2,1,0:T(8,128)S(1)}, f32[4,16,8,256]{3,2,1,0:T(8,128)S(1)}, u32[]{:S(2)}, u32[]{:S(2)}) collective-permute-start(f32[4,16,8,256]{3,2,1,0:T(8,128)S(1)} %pad_maximum_fusion.1.h_mid), channel_id=1, source_target_pairs={{0,1},{1,2},{2,3},{4,5},{5,6},{6,7},{8,9},{9,10},{10,11},{12,13},{... | collective-permute-start | bytes 1572872 | tf_op jit(solution)/shard_map/ppermute | solution.py:19
  42.4 13.7 %collective-permute-start.10 = (f32[4,8,8,256]{3,2,1,0:T(8,128)S(1)}, f32[4,8,8,256]{3,2,1,0:T(8,128)S(1)}, u32[]{:S(2)}, u32[]{:S(2)}) collective-permute-start(f32[4,8,8,256]{3,2,1,0:T(8,128)S(1)} %fusion.1), channel_id=1, source_target_pairs={{0,4},{4,0},{8,12},{12,8},{16,20},{20,16},{24,28},{28,24},{1,5},{5... | collective-permute-start | bytes 786440 | tf_op jit(solution)/shard_map/ppermute | solution.py:19
  53.3 2.8 %collective-permute-start.6 = (f32[3,8,8,256]{3,2,1,0:T(8,128)S(1)}, f32[3,8,8,256]{3,2,1,0:T(8,128)S(1)}, u32[]{:S(2)}, u32[]{:S(2)}) collective-permute-start(f32[3,8,8,256]{3,2,1,0:T(8,128)S(1)} %slice_select_fusion.4), channel_id=1, source_target_pairs={{0,4},{4,0},{8,12},{12,8},{16,20},{20,16},{24,28},{28,24},{1,5},{5... | collective-permute-start | bytes 589832 | tf_op jit(solution)/shard_map/ppermute | solution.py:19
  54.5 2.0 %collective-permute-start.8 = (f32[3,8,8,256]{3,2,1,0:T(8,128)S(1)}, f32[3,8,8,256]{3,2,1,0:T(8,128)S(1)}, u32[]{:S(2)}, u32[]{:S(2)}) collective-permute-start(f32[3,8,8,256]{3,2,1,0:T(8,128)S(1)} %slice_select_fusion.2), channel_id=1, source_target_pairs={{0,4},{4,0},{8,12},{12,8},{16,20},{20,16},{24,28},{28,24},{1,5},{5... | collective-permute-start | bytes 589832 | tf_op jit(solution)/shard_map/ppermute | solution.py:19
  55.4 2.0 %copy-start = (s32[8]{0:T(128)S(1)}, s32[8]{0:T(128)}, u32[]{:S(2)}) copy-start(s32[8]{0:T(128)} %flags.1) | copy-start | bytes 100
  55.4 1.6 %collective-permute-start.11 = (f32[4,8,8,256]{3,2,1,0:T(8,128)S(1)}, f32[4,8,8,256]{3,2,1,0:T(8,128)S(1)}, u32[]{:S(2)}, u32[]{:S(2)}) collective-permute-start(f32[4,8,8,256]{3,2,1,0:T(8,128)S(1)} %slice_select_fusion), channel_id=1, source_target_pairs={{0,4},{4,0},{8,12},{12,8},{16,20},{20,16},{24,28},{28,24},{1,5},{5... | collective-permute-start | bytes 786440 | tf_op jit(solution)/shard_map/ppermute | solution.py:19
  55.5 1.9 %collective-permute-start.9 = (f32[4,8,8,256]{3,2,1,0:T(8,128)S(1)}, f32[4,8,8,256]{3,2,1,0:T(8,128)S(1)}, u32[]{:S(2)}, u32[]{:S(2)}) collective-permute-start(f32[4,8,8,256]{3,2,1,0:T(8,128)S(1)} %slice_select_fusion.1), channel_id=1, source_target_pairs={{0,4},{4,0},{8,12},{12,8},{16,20},{20,16},{24,28},{28,24},{1,5},{5... | collective-permute-start | bytes 786440 | tf_op jit(solution)/shard_map/ppermute | solution.py:19

commit v2 on v0

v2 whole, which is shorter than its diff:
```python
import functools

import jax
import jax.numpy as jnp
from jax import lax
from jax.experimental import pallas as pl
from jax.experimental.pallas import tpu as pltpu
from jax.sharding import PartitionSpec as P

STEPS = 8
SHIFTS = 4
SHIFT = 8
HALO = STEPS
MAT = 16
LANES = 128
TILE = 8
TILES = 3
PAD = 8
GROUP = 8
HALVES = (slice(0, LANES), slice(LANES, 2 * LANES))


def e_at(t, off=0):
    return slice(TILE * t + off, TILE * t + off + TILE)


def h_at(t, off=0):
    return slice(TILE * (t + 1) + off, TILE * (t + 1) + off + TILE)


def assemble(planes, odd, first, outer_first, own, other, near, far, outer, store):
    inner_at = (1 - odd) * (planes + HALO)
    outer_at = odd * (planes + HALO)
    near_row = odd * (2 * TILE)
    far_row = (2 - 2 * odd) * TILE

    def run(count, pick, at, row):
        def one(p, carry):
            for c in range(3):
                for i, x in enumerate(HALVES):
                    store(c, at + p, i, row, pick(c, p, x))
            return carry

        lax.fori_loop(0, count, one, 0, unroll=4)

    skip = odd * HALO
    run(planes, lambda c, p, x: own[first + c, p, :, x], HALO, TILE)
    run(HALO, lambda c, p, x: other[first + c, skip + p, :, x], inner_at, TILE)
    run(planes, lambda c, p, x: near[0, first + c, p, :, x], HALO, near_row)
    run(HALO, lambda c, p, x: near[1, first + c, skip + p, :, x], inner_at, near_row)
    run(planes, lambda c, p, x: far[first + c, p, :, x], HALO, far_row)
    run(HALO, lambda c, p, x: far[first + c, planes + p, :, x], inner_at, far_row)
    for t in range(TILES):
        run(HALO, lambda c, p, x: outer[t, outer_first + c, p, :, x], outer_at, TILE * t)


def prepare_kernel(planes, pos, tables, own, other, near, far, outer, E, A, B, K, ids):
    odd = lax.rem(pos[0], 2)

    def store(c, p, i, row, value):
        E[c, p, i, pl.ds(pl.multiple_of(row, TILE), TILE), :] = value

    assemble(planes, odd, 0, 0, own, other, near, far, outer, store)

    def store_id(c, p, i, row, value):
        if c == 0:
            ids[p, i, pl.ds(pl.multiple_of(row, TILE), TILE), :] = value

    assemble(planes, odd, 3, 6, IdsView(own), IdsView(other), IdsView(near), IdsView(far), IdsView(outer), store_id)

    def look_up(p, carry):
        for t in range(TILES):
            for i in range(2):
                index = ids[p, i, e_at(t), :].astype(jnp.int32)
                for k, out in enumerate((A, B, K)):
                    out[p, i, e_at(t), :] = jnp.take_along_axis(tables[k], index, axis=1)
        return carry

    lax.fori_loop(0, planes + 2 * HALO, look_up, 0, unroll=4)


class IdsView:
    def __init__(self, ref):
        self.ref = ref
        self.at = ref.shape[-4] - 1

    def __getitem__(self, key):
        key = list(key)
        key[-4] = self.at
        return self.ref[tuple(key)]


def step_kernel(
    planes, pos, flags, E0, A, B, K, own, other, near, far, outer,
    e_out, h_out, E1, E2, H1, H2, e_stage, h_stage, out_sems,
):
    gz, gy, last_y, top_z = pos[0], pos[1], pos[2], pos[3]
    wide = planes + 2 * HALO
    odd = lax.rem(gz, 2)
    shape = (TILE, LANES)
    lane = lax.broadcasted_iota(jnp.int32, shape, 1)
    sub = lax.broadcasted_iota(jnp.int32, shape, 0)
    lane_first, lane_last = lane == 0, lane == LANES - 1
    below = jnp.where((gy == 0) & (sub == 0), 0.0, 1.0).astype(jnp.float32)
    above = jnp.where((gy == last_y) & (sub == TILE - 1), 0.0, 1.0).astype(jnp.float32)

    def store(c, p, i, row, value):
        H1[c, p, i, pl.ds(pl.multiple_of(row + TILE, TILE), TILE), :] = 2.0 * value

    assemble(planes, odd, 0, 3, own, other, near, far, outer, store)

    def x_next(v):
        r = [pltpu.roll(a, LANES - 1, 1) for a in v]
        return [jnp.where(lane_last, r[1], r[0]), jnp.where(lane_last, 0.0, r[1])]

    def x_prev(v):
        r = [pltpu.roll(a, 1, 1) for a in v]
        return [jnp.where(lane_first, 0.0, r[0]), jnp.where(lane_first, r[0], r[1])]

    def magnetic_plane(E, Hi, Ho, p, last):
        for t in range(TILES - 1 if last else TILES):
            def get(c, dp=0, off=0):
                return [E[c, p + dp, i, e_at(t, off), :] for i in range(2)]

            ex, ey, ez = get(0), get(1), get(2)
            ez_x, ey_x = x_next(ez), x_next(ey)
            ez_y, ex_y = get(2, 0, 1), get(0, 0, 1)
            if t == 1:
                ez_y, ex_y = [a * above for a in ez_y], [a * above for a in ex_y]
            ey_z, ex_z = get(1, 1), get(0, 1)
            for i in range(2):
                old = [Hi[c, p, i, h_at(t), :] for c in range(3)]
                Ho[0, p, i, h_at(t), :] = old[0] - ((ez_y[i] - ez[i]) - (ey_z[i] - ey[i]))
                Ho[1, p, i, h_at(t), :] = old[1] - ((ex_z[i] - ex[i]) - (ez_x[i] - ez[i]))
                Ho[2, p, i, h_at(t), :] = old[2] - ((ey_x[i] - ey[i]) - (ex_y[i] - ex[i]))

    def electric_plane(H, Ei, Eo, p, last):
        for t in [1] if last else range(TILES):
            def get(c, dp=0, off=0):
                return [H[c, p + dp, i, h_at(t, off), :] for i in range(2)]

            hx, hy, hz = get(0), get(1), get(2)
            hz_x, hy_x = x_prev(hz), x_prev(hy)
            hz_y, hx_y = get(2, 0, -1), get(0, 0, -1)
            if t == 1:
                hz_y, hx_y = [a * below for a in hz_y], [a * below for a in hx_y]
            hy_z, hx_z = get(1, -1), get(0, -1)
            for i in range(2):
                ex, ey, ez = [Ei[c, p, i, e_at(t), :] for c in range(3)]
                cx = (hz[i] - hz_y[i]) - (hy[i] - hy_z[i])
                cy = (hx[i] - hx_z[i]) - (hz[i] - hz_x[i])
                cz = (hy[i] - hy_x[i]) - (hx[i] - hx_y[i])
                n = K[p, i, e_at(t), :] * (ex * ex + ey * ey + ez * ez)
                up = A[p, i, e_at(t), :] + n
                r = pltpu.reciprocal(B[p, i, e_at(t), :] + n, approx=True)
                for c, (e, curl) in enumerate(((ex, cx), (ey, cy), (ez, cz))):
                    if last:
                        Eo[c, p - HALO, :, HALVES[i]] = (up * e + curl) * r
                    else:
                        Eo[c, p, i, e_at(t), :] = (up * e + curl) * r

    def zero_plane(ref, p, count):
        @pl.when((p >= 0) & (p < count))
        def _():
            ref[:, p] = jnp.zeros((3,) + ref.shape[2:], jnp.float32)

    base = planes * gz + SHIFT * SHIFTS - HALO

    def grouped(plane, start, count):
        def one(g, carry):
            for j in range(GROUP):
                plane(start + g * GROUP + j)
            return carry

        lax.fori_loop(0, lax.div(count + GROUP - 1, GROUP), one, 0)

    h_copy = pltpu.make_async_copy(h_stage, h_out, out_sems.at[1])
    e_copy = pltpu.make_async_copy(e_stage, e_out, out_sems.at[0])

    def step(s, moved, Ei, Eo, Hi, Ho, last=False):
        moved = moved + flags[s - 1]
        grouped(lambda p: magnetic_plane(Ei, Hi, Ho, p, last), s - 1, wide + 1 - 2 * s)
        zero_plane(Ho, SHIFT * moved - 1 - base, wide)
        if last:
            def finish(p, carry):
                for c in range(3):
                    for i in range(2):
                        h_stage[c, p, :, HALVES[i]] = 0.5 * Ho[c, HALO + p, i, h_at(1), :]
                return carry

            lax.fori_loop(0, planes, finish, 0, unroll=4)
            h_copy.start()
        grouped(lambda p: electric_plane(Ho, Ei, Eo, p, last), s, wide - 2 * s)
        above_window = top_z + SHIFT * moved - base
        if last:
            zero_plane(Eo, above_window - HALO, planes)
        else:
            zero_plane(Eo, above_window, wide)
        return moved

    moved = step(1, jnp.int32(0), E0, E1, H1, H2)

    def pair(k, moved):
        moved = step(2 * k, moved, E1, E2, H2, H1)
        return step(2 * k + 1, moved, E2, E1, H1, H2)

    moved = lax.fori_loop(1, STEPS // 2, pair, moved)
    step(STEPS, moved, E1, e_stage, H2, H1, last=True)
    e_copy.start()
    h_copy.wait()
    e_copy.wait()


SMEM, VMEM, ANY = [pl.BlockSpec(memory_space=m) for m in (pltpu.SMEM, pltpu.VMEM, pl.ANY)]


def prepare(pos, tables, pieces, planes):
    deep = planes + 2 * HALO + PAD
    coef = jax.ShapeDtypeStruct((deep, 2, TILES * TILE, LANES), jnp.float32)
    return pl.pallas_call(
        functools.partial(prepare_kernel, planes),
        out_shape=(jax.ShapeDtypeStruct((3, deep, 2, 4 * TILE, LANES), jnp.float32), coef, coef, coef),
        in_specs=[SMEM] + [VMEM] * (1 + len(pieces)),
        out_specs=(VMEM,) * 4,
        scratch_shapes=[pltpu.VMEM(coef.shape, jnp.float32)],
        compiler_params=pltpu.CompilerParams(vmem_limit_bytes=24 * 2**20),
        name="prepare",
    )(pos, tables, *pieces)


def run_steps(pos, flags, full, pieces, planes, rows, width):
    deep = planes + 2 * HALO + PAD
    field = jax.ShapeDtypeStruct((3, planes, rows, width), jnp.float32)
    work = pltpu.VMEM((3, deep, 2, 4 * TILE, LANES), jnp.float32)
    return pl.pallas_call(
        functools.partial(step_kernel, planes),
        out_shape=(field, field),
        in_specs=[SMEM, SMEM] + [VMEM] * (len(full) + len(pieces)),
        out_specs=(ANY,) * 2,
        scratch_shapes=[work] * 4
        + [pltpu.VMEM(field.shape, jnp.float32)] * 2
        + [pltpu.SemaphoreType.DMA((2,))],
        compiler_params=pltpu.CompilerParams(vmem_limit_bytes=32 * 2**20),
        name="fdtd_steps",
    )(pos, flags, *full, *pieces)


def down(value, hop, wrap=0):
    count = lax.axis_size("gz")
    pairs = [(s, s - hop) for s in range(hop, count)] + [(s, count + s - hop) for s in range(wrap)]
    return lax.ppermute(value, "gz", pairs)


def swap_cores(value):
    return lax.ppermute(value, "gz", [(s, s ^ 1) for s in range(lax.axis_size("gz"))])


def y_halo(value):
    nz, ny = lax.axis_size("gz"), lax.axis_size("gy")
    pairs = []
    for z in range(nz):
        hop = 1 - 2 * (z % 2)
        pairs += [(z * ny + y, z * ny + y + hop) for y in range(ny) if 0 <= y + hop < ny]
    return lax.ppermute(value, ("gz", "gy"), pairs)


def body(electric, magnetic, material, incoming, shift_flags, eps_table, sigma_table, kerr_table):
    count_z, count_y = lax.axis_size("gz"), lax.axis_size("gy")
    _, planes, rows, width = electric.shape
    hop = SHIFTS * SHIFT // planes
    assert hop * planes == SHIFTS * SHIFT and hop == 2 and planes == 2 * HALO
    assert rows == HALO and width == 2 * LANES and count_z % 2 == 0 and count_z >= 4
    gz, gy = lax.axis_index("gz"), lax.axis_index("gy")
    odd = gz % 2 == 1

    moved_e = down(jnp.concatenate([electric, material.astype(jnp.float32)[None]], 0), hop)
    moved_h = down(magnetic, hop)

    def edge(field):
        return jnp.where(odd, field[..., HALO:, :, :], field[..., :HALO, :, :])

    fields = jnp.concatenate([edge(electric), edge(magnetic)], 0)
    fresh = jnp.where(gz == 0, incoming[:HALO], edge(material)).astype(jnp.float32)
    mine = jnp.concatenate([jnp.where(gz == 0, 0.0, fields), fresh[None]], 0)
    theirs = swap_cores(mine)
    mine_y, theirs_y = y_halo(jnp.stack([mine, theirs]))
    part = HALO // 2
    crossed = down(
        jnp.where(
            odd,
            jnp.concatenate([theirs_y, theirs[:, part:]], 1),
            jnp.concatenate([mine_y, mine[:, :part]], 1),
        ),
        2 * hop,
        wrap=2,
    )
    given = swap_cores(jnp.where(odd, jnp.concatenate([mine_y, crossed[:, HALO:]], 1), crossed))
    outer = jnp.stack(
        [
            jnp.where(odd, given[:, :HALO], theirs_y),
            jnp.where(odd, jnp.concatenate([given[:, HALO:], crossed[:, HALO:]], 1), theirs),
            jnp.where(odd, crossed[:, :HALO], given[:, :HALO]),
        ]
    )

    def around(own):
        other = swap_cores(own)
        near = y_halo(jnp.stack([own, other]))
        edge_rows = jnp.where(odd, near[0, :, :HALO], near[0, :, HALO:])
        far = swap_cores(jnp.concatenate([near[1], edge_rows], 1))
        return [own, other, near, far]

    fresh_at = jnp.clip(gz - (count_z - hop), 0, hop - 1) * planes
    entering = lax.dynamic_slice_in_dim(incoming, fresh_at, planes, 0).astype(jnp.float32)
    ids = jnp.where(gz >= count_z - hop, entering, moved_e[3])
    e_pieces = around(jnp.concatenate([moved_e[:3], ids[None]], 0))
    h_pieces = around(moved_h)

    tables = jnp.stack(
        [4.0 * eps_table - 2.0 * sigma_table, 4.0 * eps_table + 2.0 * sigma_table, 4.0 * kerr_table]
    )
    tables = jnp.broadcast_to(jnp.pad(tables, ((0, 0), (0, LANES - MAT)))[:, None, :], (3, TILE, LANES))
    pos = jnp.stack([gz, gy, count_y - 1, count_z * planes]).astype(jnp.int32)
    full = prepare(pos, tables, e_pieces + [outer], planes)
    return run_steps(pos, shift_flags, full, h_pieces + [outer], planes, rows, width)


def solution(mesh):
    field = P(None, "gz", "gy", None)
    return jax.shard_map(
        body,
        mesh=mesh,
        in_specs=(field, field, P("gz", "gy", None), P(None, "gy", None), P(), P(), P(), P()),
        out_specs=(field, field),
        check_vma=False,
    )
```

time: 425 us -> 75.3 us (0.18); the launches traced: 419 us -> 74.7 us
  other arithmetic: 251 us -> 9.53 us
  starting transfers between devices: 102 us -> 21.6 us
  local copies, waits for them, and re-layouts: 20.5 us -> 1.4 us
  Pallas kernels: 0 us -> 15.7 us
  between operations: 13.6 us -> 1 us
  waiting for transfers between devices: 32.7 us -> 25.4 us
    another operation x36 -> x11, other arithmetic: 207 us -> 6.26 us  [the longest x3 2.98 us: around(): near = y_halo(jnp.stack([own, other]))]
    ppermute x32 -> x12, starting transfers between devices: 102 us -> 21.6 us  [the longest x6 9.81 us: swap_cores(): lax.ppermute(value, 'gz', [(s, s ^ 1) for s in range(lax.axis_size('gz'))])]
    unnamed x2 -> x0, other arithmetic: 20.8 us -> none
    slice x131 -> x4, local copies, waits for them, and re-layouts: 17.9 us -> 0.07 us  [the longest x1 0.03 us: body(): e_pieces = around(jnp.concatenate([moved_e[:3], ids[None]], 0))]
    pallas_call x0 -> x2, Pallas kernels: none -> 15.7 us  [the longest x1 13 us: run_steps(): pl.pallas_call(functools.partial(step_kernel, planes), out_shape=(field,...]
    concatenate x8 -> x4, other arithmetic: 10.7 us -> 0.83 us  [the longest x1 0.71 us: body(): mine = jnp.concatenate([jnp.where(gz == 0, 0.0, fields), fresh[None]], 0)]
    ppermute x32 -> x12, waiting for transfers between devices: 32.7 us -> 25.4 us  [the longest x3 20 us: down(): return lax.ppermute(value, 'gz', pairs)]
    select_n x24 -> x7, other arithmetic: 8.47 us -> 2.38 us  [the longest x2 2.11 us: edge(): return jnp.where(odd, field[..., HALO:, :, :], field[..., :HALO, :, :])]
  transfers between devices with their start and end apart: 32 -> 12, of which waited for: 16 -> 5; matrix products, arithmetic and copies ran while one was open for 50% -> 15% of each run, Pallas kernels for 0% -> 4%
where the time goes in v2:
time: 75.3 us; the launch traced here: 74.7 us
  waiting for transfers between devices  25.4 us (34%)
  starting transfers between devices  21.6 us (29%)
  Pallas kernels  15.7 us (21%)
  other arithmetic  9.53 us (13%)
  local copies, waits for them, and re-layouts  1.4 us (2%)
  between operations  1 us (1%)
    ppermute x3, waiting for transfers between devices, down(): return lax.ppermute(value, 'gz', pairs)  20 us
    pallas_call x1, Pallas kernels, run_steps(): pl.pallas_call(functools.partial(step_kernel, planes), out_shape=(field,...  13 us
    ppermute x6, starting transfers between devices, swap_cores(): lax.ppermute(value, 'gz', [(s, s ^ 1) for s in range(lax.axis_size('gz'))])  9.81 us
    ppermute x3, starting transfers between devices, y_halo(): return lax.ppermute(value, ('gz', 'gy'), pairs)  6.32 us
    ppermute x3, starting transfers between devices, down(): return lax.ppermute(value, 'gz', pairs)  5.51 us
    ppermute x3, waiting for transfers between devices, y_halo(): return lax.ppermute(value, ('gz', 'gy'), pairs)  4.47 us
    another operation x3, other arithmetic, around(): near = y_halo(jnp.stack([own, other]))  2.98 us
    pallas_call x1, Pallas kernels, prepare(): pl.pallas_call(functools.partial(prepare_kernel, planes), out_shape=(jax....  2.75 us
  transfers between devices with their start and end apart: 12, of which 5 were waited for; matrix products, arithmetic and copies ran while one was open for 15% of the time, Pallas kernels for 4%

profile of v2, /device:TPU:11, one launch (start us, length us, event | category | flops | bytes accessed | tf_op | source)
XLA Modules:
  0.0 74.7 jit_solution(18183572788291328373)
XLA Ops:
  0.6 0.0 copy-start.3
  0.6 0.0 copy-start.4
  0.7 2.3 %collective-permute-start.8 = (f32[3,16,8,256]{3,2,1,0:T(8,128)}, f32[3,16,8,256]{3,2,1,0:T(8,128)S(1)}, u32[]{:S(2)}, u32[]{:S(2)}) collective-permute-start(f32[3,16,8,256]{3,2,1,0:T(8,128)} %param.9), channel_id=1, source_target_pairs={{8,0},{12,4},{16,8},{20,12},{24,16},{28,20},{9,1},{13,5},{17,9},{2... | collective-permute-start | bytes 1179656 | tf_op jit(solution)/shard_map/ppermute | solution.py:251
  3.0 1.1 %slice_select_fusion.3 = f32[3,8,8,256]{3,2,1,0:T(8,128)S(1)} fusion(f32[3,16,8,256]{3,2,1,0:T(8,128)} %param.9, pred[]{:T(512)S(6)} %eq.9), kind=kLoop, calls=%fused_computation.30 | loop fusion | flops 49152 | bytes 589825 | tf_op jit(solution)/shard_map/jit(_where)/select_n | solution.py:280
  4.0 1.1 %slice_select_fusion.4 = f32[3,8,8,256]{3,2,1,0:T(8,128)S(1)} fusion(f32[3,16,8,256]{3,2,1,0:T(8,128)} %param.8, pred[]{:T(512)S(6)} %eq.9), kind=kLoop, calls=%fused_computation.31 | loop fusion | flops 49152 | bytes 589825 | tf_op jit(solution)/shard_map/jit(_where)/select_n | solution.py:280
  5.1 0.0 copy-start.1
  5.2 0.9 %fusion.9 = (f32[1,7,8,8,256]{4,3,2,1,0:T(8,128)S(1)}, f32[7,8,8,256]{3,2,1,0:T(8,128)}) fusion(f32[1,8,8,256]{3,2,1,0:T(8,128)S(1)} %convert_bitcast_fusion.1, f32[6,8,8,256]{3,2,1,0:T(8,128)S(1)} %maximum_select_fusion.1), kind=kLoop, calls=%fused_computation.44 | loop fusion | flops 114688 | bytes 1376256 | tf_op jit(solution)/shard_map/stack | solution.py:286
  6.0 1.0 %collective-permute-start.4 = (f32[7,8,8,256]{3,2,1,0:T(8,128)}, f32[7,8,8,256]{3,2,1,0:T(8,128)S(1)}, u32[]{:S(2)}, u32[]{:S(2)}) collective-permute-start(f32[7,8,8,256]{3,2,1,0:T(8,128)} %get-tuple-element.17), channel_id=1, source_target_pairs={{0,4},{4,0},{8,12},{12,8},{16,20},{20,16},{24,28},{28,24},{1,5},{5... | collective-permute-start | bytes 1376264 | tf_op jit(solution)/shard_map/ppermute | solution.py:255
  7.1 1.9 %collective-permute-start = (f32[4,16,8,256]{3,2,1,0:T(8,128)S(1)}, f32[4,16,8,256]{3,2,1,0:T(8,128)S(1)}, u32[]{:S(2)}, u32[]{:S(2)}) collective-permute-start(f32[4,16,8,256]{3,2,1,0:T(8,128)S(1)} %pad_maximum_fusion.9), channel_id=1, source_target_pairs={{8,0},{12,4},{16,8},{20,12},{24,16},{28,20},{9,1},{13,5},{17,9},{2... | collective-permute-start | bytes 1572872 | tf_op jit(solution)/shard_map/ppermute | solution.py:251
  9.0 4.8 %collective-permute-done.8.own = f32[3,16,8,256]{3,2,1,0:T(8,128)S(1)} collective-permute-done((f32[3,16,8,256]{3,2,1,0:T(8,128)}, f32[3,16,8,256]{3,2,1,0:T(8,128)S(1)}, u32[]{:S(2)}, u32[]{:S(2)}) %collective-permute-start.8) | collective-permute-done | bytes 393248 | tf_op jit(solution)/shard_map/ppermute | solution.py:251
  13.8 2.7 %collective-permute-start.9 = (f32[3,16,8,256]{3,2,1,0:T(8,128)S(1)}, f32[3,16,8,256]{3,2,1,0:T(8,128)S(1)}, u32[]{:S(2)}, u32[]{:S(2)}) collective-permute-start(f32[3,16,8,256]{3,2,1,0:T(8,128)S(1)} %collective-permute-done.8.own), channel_id=1, source_target_pairs={{0,4},{4,0},{8,12},{12,8},{16,20},{20,16},{24,28},{28,24},{1,5},{5... | collective-permute-start | bytes 1179656 | tf_op jit(solution)/shard_map/ppermute | solution.py:255
  16.5 0.0 collective-permute-done.4
  16.5 1.0 %pad_maximum_fusion.2 = f32[2,7,8,8,256]{4,3,2,1,0:T(8,128)} fusion(f32[1,7,8,8,256]{4,3,2,1,0:T(8,128)S(1)} %bitcast.51, f32[1,7,8,8,256]{4,3,2,1,0:T(8,128)S(1)} %get-tuple-element.16), kind=kLoop, calls=%fused_computation.2 | loop fusion | flops 229376 | bytes 1835008 | tf_op jit(solution)/shard_map/stack | solution.py:286
  17.5 2.2 %collective-permute-start.5 = (f32[2,7,8,8,256]{4,3,2,1,0:T(8,128)}, f32[2,7,8,8,256]{4,3,2,1,0:T(8,128)}, u32[]{:S(2)}, u32[]{:S(2)}) collective-permute-start(f32[2,7,8,8,256]{4,3,2,1,0:T(8,128)} %pad_maximum_fusion.2), channel_id=1, source_target_pairs={{0,1},{1,2},{2,3},{5,4},{6,5},{7,6},{8,9},{9,10},{10,11},{13,12},{... | collective-permute-start | bytes 2752520 | tf_op jit(solution)/shard_map/ppermute | solution.py:264
  19.7 5.3 %collective-permute-done = f32[4,16,8,256]{3,2,1,0:T(8,128)S(1)} collective-permute-done((f32[4,16,8,256]{3,2,1,0:T(8,128)S(1)}, f32[4,16,8,256]{3,2,1,0:T(8,128)S(1)}, u32[]{:S(2)}, u32[]{:S(2)}) %collective-permute-start) | collective-permute-done | bytes 524320 | tf_op jit(solution)/shard_map/ppermute | solution.py:251
  25.1 0.9 %fusion.10 = (f32[1,4,16,8,256]{4,3,2,1,0:T(8,128)}, f32[4,16,8,256]{3,2,1,0:T(8,128)S(1)}) fusion(f32[1,16,8,256]{3,2,1,0:T(8,128)S(1)} %fusion.8, f32[3,16,8,256]{3,2,1,0:T(8,128)S(1)} %slice.86), kind=kLoop, calls=%fused_computation.45 | loop fusion | flops 131072 | bytes 1572864 | tf_op jit(solution)/shard_map/stack | solution.py:308
  26.0 1.5 %collective-permute-start.1 = (f32[4,16,8,256]{3,2,1,0:T(8,128)S(1)}, f32[4,16,8,256]{3,2,1,0:T(8,128)S(1)}, u32[]{:S(2)}, u32[]{:S(2)}) collective-permute-start(f32[4,16,8,256]{3,2,1,0:T(8,128)S(1)} %get-tuple-element.15.own), channel_id=1, source_target_pairs={{0,4},{4,0},{8,12},{12,8},{16,20},{20,16},{24,28},{28,24},{1,5},{5... | collective-permute-start | bytes 1572872 | tf_op jit(solution)/shard_map/ppermute | solution.py:255
  27.5 0.0 copy-done.5
  27.5 0.0 collective-permute-done.9.other
  27.5 1.0 %pad_maximum_fusion.4 = f32[2,3,16,8,256]{4,3,2,1,0:T(8,128)} fusion(f32[1,3,16,8,256]{4,3,2,1,0:T(8,128)S(1)} %bitcast.50, f32[1,3,16,8,256]{4,3,2,1,0:T(8,128)S(1)} %bitcast.49), kind=kLoop, calls=%fused_computation.4 | loop fusion | flops 196608 | bytes 1572864 | tf_op jit(solution)/shard_map/stack | solution.py:308
  28.5 2.1 %collective-permute-start.10 = (f32[2,3,16,8,256]{4,3,2,1,0:T(8,128)}, f32[2,3,16,8,256]{4,3,2,1,0:T(8,128)S(1)}, u32[]{:S(2)}, u32[]{:S(2)}) collective-permute-start(f32[2,3,16,8,256]{4,3,2,1,0:T(8,128)} %pad_maximum_fusion.4), channel_id=1, source_target_pairs={{0,1},{1,2},{2,3},{5,4},{6,5},{7,6},{8,9},{9,10},{10,11},{13,12},{... | collective-permute-start | bytes 2359304 | tf_op jit(solution)/shard_map/ppermute | solution.py:264
  30.6 0.7 fusion.5
  31.3 0.0 collective-permute-done.1.other
  31.3 1.1 %pad_maximum_fusion.1 = f32[2,4,16,8,256]{4,3,2,1,0:T(8,128)S(1)} fusion(f32[1,4,16,8,256]{4,3,2,1,0:T(8,128)S(1)} %bitcast.48, f32[1,4,16,8,256]{4,3,2,1,0:T(8,128)} %get-tuple-element.14), kind=kLoop, calls=%fused_computation.1 | loop fusion | flops 262144 | bytes 2097152 | tf_op jit(solution)/shard_map/stack | solution.py:308
  32.4 0.0 copy-start.2
  32.5 2.1 %collective-permute-start.2 = (f32[2,4,16,8,256]{4,3,2,1,0:T(8,128)S(1)}, f32[2,4,16,8,256]{4,3,2,1,0:T(8,128)S(1)}, u32[]{:S(2)}, u32[]{:S(2)}) collective-permute-start(f32[2,4,16,8,256]{4,3,2,1,0:T(8,128)S(1)} %pad_maximum_fusion.1), channel_id=1, source_target_pairs={{0,1},{1,2},{2,3},{5,4},{6,5},{7,6},{8,9},{9,10},{10,11},{13,12},{... | collective-permute-start | bytes 3145736 | tf_op jit(solution)/shard_map/ppermute | solution.py:264
  34.5 0.0 collective-permute-done.5
  34.5 1.2 %slice_bitcast_fusion.1 = (f32[7,8,8,256]{3,2,1,0:T(8,128)S(1)}, f32[7,8,8,256]{3,2,1,0:T(8,128)S(1)}) fusion(f32[2,7,8,8,256]{4,3,2,1,0:T(8,128)} %collective-permute-done.5), kind=kLoop, calls=%fused_computation.18 | loop fusion | bytes 1835008 | tf_op jit(solution)/shard_map/unstack | solution.py:286
  35.8 0.1 fusion.1
  35.9 1.3 %collective-permute-start.6 = (f32[7,12,8,256]{3,2,1,0:T(8,128)S(1)}, f32[7,12,8,256]{3,2,1,0:T(8,128)S(1)}, u32[]{:S(2)}, u32[]{:S(2)}) collective-permute-start(f32[7,12,8,256]{3,2,1,0:T(8,128)S(1)} %fusion.1), channel_id=1, source_target_pairs={{16,0},{20,4},{24,8},{28,12},{0,16},{4,20},{17,1},{21,5},{25,9},{2... | collective-permute-start | bytes 2064392 | tf_op jit(solution)/shard_map/ppermute | solution.py:251
  37.2 0.1 pad_add_fusion.pos
  37.3 4.5 %collective-permute-done.10.near = f32[2,3,16,8,256]{4,3,2,1,0:T(8,128)S(1)} collective-permute-done((f32[2,3,16,8,256]{4,3,2,1,0:T(8,128)}, f32[2,3,16,8,256]{4,3,2,1,0:T(8,128)S(1)}, u32[]{:S(2)}, u32[]{:S(2)}) %collective-permute-start.10) | collective-permute-done | bytes 786464 | tf_op jit(solution)/shard_map/ppermute | solution.py:264
  41.8 9.9 %collective-permute-done.6 = f32[7,12,8,256]{3,2,1,0:T(8,128)S(1)} collective-permute-done((f32[7,12,8,256]{3,2,1,0:T(8,128)S(1)}, f32[7,12,8,256]{3,2,1,0:T(8,128)S(1)}, u32[]{:S(2)}, u32[]{:S(2)}) %collective-permute-start.6) | collective-permute-done | bytes 688160 | tf_op jit(solution)/shard_map/ppermute | solution.py:251
  51.7 0.1 fusion
  51.8 4.0 %collective-permute-start.7 = (f32[7,12,8,256]{3,2,1,0:T(8,128)S(1)}, f32[7,12,8,256]{3,2,1,0:T(8,128)S(1)}, u32[]{:S(2)}, u32[]{:S(2)}) collective-permute-start(f32[7,12,8,256]{3,2,1,0:T(8,128)S(1)} %fusion), channel_id=1, source_target_pairs={{0,4},{4,0},{8,12},{12,8},{16,20},{20,16},{24,28},{28,24},{1,5},{5... | collective-permute-start | bytes 2064392 | tf_op jit(solution)/shard_map/ppermute | solution.py:255
  55.8 0.0 collective-permute-done.2.near
  55.9 0.1 pad_maximum_fusion.3
  55.9 0.1 collective-permute-start.3
  56.1 0.6 collective-permute-start.11
  56.6 0.9 %collective-permute-done.7 = f32[7,12,8,256]{3,2,1,0:T(8,128)S(1)} collective-permute-done((f32[7,12,8,256]{3,2,1,0:T(8,128)S(1)}, f32[7,12,8,256]{3,2,1,0:T(8,128)S(1)}, u32[]{:S(2)}, u32[]{:S(2)}) %collective-permute-start.7) | collective-permute-done | bytes 688160 | tf_op jit(solution)/shard_map/ppermute | solution.py:255
  57.6 0.1 fusion.3
  57.7 1.1 %select_bitcast_fusion = (f32[1,7,8,8,256]{4,3,2,1,0:T(8,128)S(1)}, f32[1,7,8,8,256]{4,3,2,1,0:T(8,128)S(1)}) fusion(f32[7,12,8,256]{3,2,1,0:T(8,128)S(1)} %collective-permute-done.7, pred[]{:T(512)S(6)} %eq.9, f32[2,7,8,8,256]{4,3,2,1,0:T(8,128)} %collective-permute-done.5, f32[7,12,8,256]{3,2,1,0:T(8,128)S(1)} %collective-permute-done.6), kind=kLoop, calls=%fused_computation.22 | loop fusion | flops 229376 | bytes 2293761 | tf_op jit(solution)/shard_map/stack | solution.py:298
  58.8 0.1 pad_maximum_fusion.outer
  58.9 0.0 collective-permute-done.3.far
  58.9 0.0 copy-start
  58.9 2.8 %prepare.1 = (f32[3,40,2,32,128]{4,3,2,1,0:T(8,128)S(1)}, f32[40,2,24,128]{3,2,1,0:T(8,128)S(1)}, f32[40,2,24,128]{3,2,1,0:T(8,128)S(1)}, f32[40,2,24,128]{3,2,1,0:T(8,128)S(1)}) custom-call(s32[4]{0:T(128)S(1)} %pad_add_fusion.pos, f32[3,8,128]{2,1,0:T(8,128)S(1)} %broadcast_in_dim.19.tables, f32[4,16,8,256]{3,2,1,0:T(8,128)S(1)} %get-tuple-element.15.own, ...), custom_call_target="tpu_custom_call" | custom-call | tf_op jit(solution)/shard_map/prepare/pallas_call | solution.py:220
  61.7 0.0 collective-permute-done.11.far
  61.7 13.0 %fdtd_steps.1 = (f32[3,16,8,256]{3,2,1,0:T(8,128)}, f32[3,16,8,256]{3,2,1,0:T(8,128)}) custom-call(s32[4]{0:T(128)S(1)} %pad_add_fusion.pos, s32[8]{0:T(128)S(1)} %copy-done, f32[3,40,2,32,128]{4,3,2,1,0:T(8,128)S(1)} %get-tuple-element.6.E0, f32[40,2,24,128]{3,2,1,0:T(8,128)S(1)} %get-tuple-element.7.A, f32[40,2,24,128]{3,2,1,0:T(8,128)S(1)} %get-tuple-element.8.B, ...), custom_call_target="tpu_custom_call" | custom-call | tf_op jit(solution)/shard_map/fdtd_steps/pallas_call | solution.py:235
  (27 shorter events, 0.4 us)
Async XLA Ops:
  0.6 4.5 %copy-start.3 = (s32[16,8,256]{2,1,0:T(8,128)S(1)}, s32[16,8,256]{2,1,0:T(8,128)}, u32[]{:S(2)}) copy-start(s32[16,8,256]{2,1,0:T(8,128)} %param.10) | copy-start | bytes 393220
  0.6 4.5 %copy-start.4 = (s32[32,8,256]{2,1,0:T(8,128)S(1)}, s32[32,8,256]{2,1,0:T(8,128)}, u32[]{:S(2)}) copy-start(s32[32,8,256]{2,1,0:T(8,128)} %param.11) | copy-start | bytes 786436
  0.7 13.1 %collective-permute-start.8 = (f32[3,16,8,256]{3,2,1,0:T(8,128)}, f32[3,16,8,256]{3,2,1,0:T(8,128)S(1)}, u32[]{:S(2)}, u32[]{:S(2)}) collective-permute-start(f32[3,16,8,256]{3,2,1,0:T(8,128)} %param.9), channel_id=1, source_target_pairs={{8,0},{12,4},{16,8},{20,12},{24,16},{28,20},{9,1},{13,5},{17,9},{2... | collective-permute-start | bytes 1179656 | tf_op jit(solution)/shard_map/ppermute | solution.py:251
  5.1 1.9 %copy-start.1 = (f32[3,16,8,256]{3,2,1,0:T(8,128)S(1)}, f32[3,16,8,256]{3,2,1,0:T(8,128)}, u32[]{:S(2)}) copy-start(f32[3,16,8,256]{3,2,1,0:T(8,128)} %param.8) | copy-start | bytes 1179652
  6.0 10.4 %collective-permute-start.4 = (f32[7,8,8,256]{3,2,1,0:T(8,128)}, f32[7,8,8,256]{3,2,1,0:T(8,128)S(1)}, u32[]{:S(2)}, u32[]{:S(2)}) collective-permute-start(f32[7,8,8,256]{3,2,1,0:T(8,128)} %get-tuple-element.17), channel_id=1, source_target_pairs={{0,4},{4,0},{8,12},{12,8},{16,20},{20,16},{24,28},{28,24},{1,5},{5... | collective-permute-start | bytes 1376264 | tf_op jit(solution)/shard_map/ppermute | solution.py:255
  7.1 17.9 %collective-permute-start = (f32[4,16,8,256]{3,2,1,0:T(8,128)S(1)}, f32[4,16,8,256]{3,2,1,0:T(8,128)S(1)}, u32[]{:S(2)}, u32[]{:S(2)}) collective-permute-start(f32[4,16,8,256]{3,2,1,0:T(8,128)S(1)} %pad_maximum_fusion.9), channel_id=1, source_target_pairs={{8,0},{12,4},{16,8},{20,12},{24,16},{28,20},{9,1},{13,5},{17,9},{2... | collective-permute-start | bytes 1572872 | tf_op jit(solution)/shard_map/ppermute | solution.py:251
  13.8 13.8 %collective-permute-start.9 = (f32[3,16,8,256]{3,2,1,0:T(8,128)S(1)}, f32[3,16,8,256]{3,2,1,0:T(8,128)S(1)}, u32[]{:S(2)}, u32[]{:S(2)}) collective-permute-start(f32[3,16,8,256]{3,2,1,0:T(8,128)S(1)} %collective-permute-done.8.own), channel_id=1, source_target_pairs={{0,4},{4,0},{8,12},{12,8},{16,20},{20,16},{24,28},{28,24},{1,5},{5... | collective-permute-start | bytes 1179656 | tf_op jit(solution)/shard_map/ppermute | solution.py:255
  17.5 10.0 %copy-start.5 = (f32[16]{0:T(128)S(1)}, f32[16]{0:T(128)}, u32[]{:S(2)}) copy-start(f32[16]{0:T(128)} %param.14) | copy-start | bytes 196
  17.5 10.0 %copy-start.6 = (f32[16]{0:T(128)S(1)}, f32[16]{0:T(128)}, u32[]{:S(2)}) copy-start(f32[16]{0:T(128)} %param.13) | copy-start | bytes 196
  17.5 10.0 %copy-start.7 = (f32[16]{0:T(128)S(1)}, f32[16]{0:T(128)}, u32[]{:S(2)}) copy-start(f32[16]{0:T(128)} %param.15) | copy-start | bytes 196
  17.5 17.0 %collective-permute-start.5 = (f32[2,7,8,8,256]{4,3,2,1,0:T(8,128)}, f32[2,7,8,8,256]{4,3,2,1,0:T(8,128)}, u32[]{:S(2)}, u32[]{:S(2)}) collective-permute-start(f32[2,7,8,8,256]{4,3,2,1,0:T(8,128)} %pad_maximum_fusion.2), channel_id=1, source_target_pairs={{0,1},{1,2},{2,3},{5,4},{6,5},{7,6},{8,9},{9,10},{10,11},{13,12},{... | collective-permute-start | bytes 2752520 | tf_op jit(solution)/shard_map/ppermute | solution.py:264
  26.0 5.3 %collective-permute-start.1 = (f32[4,16,8,256]{3,2,1,0:T(8,128)S(1)}, f32[4,16,8,256]{3,2,1,0:T(8,128)S(1)}, u32[]{:S(2)}, u32[]{:S(2)}) collective-permute-start(f32[4,16,8,256]{3,2,1,0:T(8,128)S(1)} %get-tuple-element.15.own), channel_id=1, source_target_pairs={{0,4},{4,0},{8,12},{12,8},{16,20},{20,16},{24,28},{28,24},{1,5},{5... | collective-permute-start | bytes 1572872 | tf_op jit(solution)/shard_map/ppermute | solution.py:255
  28.5 13.2 %collective-permute-start.10 = (f32[2,3,16,8,256]{4,3,2,1,0:T(8,128)}, f32[2,3,16,8,256]{4,3,2,1,0:T(8,128)S(1)}, u32[]{:S(2)}, u32[]{:S(2)}) collective-permute-start(f32[2,3,16,8,256]{4,3,2,1,0:T(8,128)} %pad_maximum_fusion.4), channel_id=1, source_target_pairs={{0,1},{1,2},{2,3},{5,4},{6,5},{7,6},{8,9},{9,10},{10,11},{13,12},{... | collective-permute-start | bytes 2359304 | tf_op jit(solution)/shard_map/ppermute | solution.py:264
  32.4 3.3 %copy-start.2 = (f32[7,4,8,256]{3,2,1,0:T(8,128)S(1)}, f32[7,4,8,256]{3,2,1,0:T(8,128)}, u32[]{:S(2)}) copy-start(f32[7,4,8,256]{3,2,1,0:T(8,128)} %fusion.5) | copy-start | bytes 688132
  32.5 23.3 %collective-permute-start.2 = (f32[2,4,16,8,256]{4,3,2,1,0:T(8,128)S(1)}, f32[2,4,16,8,256]{4,3,2,1,0:T(8,128)S(1)}, u32[]{:S(2)}, u32[]{:S(2)}) collective-permute-start(f32[2,4,16,8,256]{4,3,2,1,0:T(8,128)S(1)} %pad_maximum_fusion.1), channel_id=1, source_target_pairs={{0,1},{1,2},{2,3},{5,4},{6,5},{7,6},{8,9},{9,10},{10,11},{13,12},{... | collective-permute-start | bytes 3145736 | tf_op jit(solution)/shard_map/ppermute | solution.py:264
  35.9 15.8 %collective-permute-start.6 = (f32[7,12,8,256]{3,2,1,0:T(8,128)S(1)}, f32[7,12,8,256]{3,2,1,0:T(8,128)S(1)}, u32[]{:S(2)}, u32[]{:S(2)}) collective-permute-start(f32[7,12,8,256]{3,2,1,0:T(8,128)S(1)} %fusion.1), channel_id=1, source_target_pairs={{16,0},{20,4},{24,8},{28,12},{0,16},{4,20},{17,1},{21,5},{25,9},{2... | collective-permute-start | bytes 2064392 | tf_op jit(solution)/shard_map/ppermute | solution.py:251
  51.8 5.7 %collective-permute-start.7 = (f32[7,12,8,256]{3,2,1,0:T(8,128)S(1)}, f32[7,12,8,256]{3,2,1,0:T(8,128)S(1)}, u32[]{:S(2)}, u32[]{:S(2)}) collective-permute-start(f32[7,12,8,256]{3,2,1,0:T(8,128)S(1)} %fusion), channel_id=1, source_target_pairs={{0,4},{4,0},{8,12},{12,8},{16,20},{20,16},{24,28},{28,24},{1,5},{5... | collective-permute-start | bytes 2064392 | tf_op jit(solution)/shard_map/ppermute | solution.py:255
  55.9 2.9 %collective-permute-start.3 = (f32[4,24,8,256]{3,2,1,0:T(8,128)S(1)}, f32[4,24,8,256]{3,2,1,0:T(8,128)S(1)}, u32[]{:S(2)}, u32[]{:S(2)}) collective-permute-start(f32[4,24,8,256]{3,2,1,0:T(8,128)S(1)} %pad_maximum_fusion.3), channel_id=1, source_target_pairs={{0,4},{4,0},{8,12},{12,8},{16,20},{20,16},{24,28},{28,24},{1,5},{5... | collective-permute-start | bytes 2359304 | tf_op jit(solution)/shard_map/ppermute | solution.py:255
  56.1 5.6 %collective-permute-start.11 = (f32[3,24,8,256]{3,2,1,0:T(8,128)S(1)}, f32[3,24,8,256]{3,2,1,0:T(8,128)S(1)}, u32[]{:S(2)}, u32[]{:S(2)}) collective-permute-start(f32[3,24,8,256]{3,2,1,0:T(8,128)S(1)} %pad_maximum_fusion.8), channel_id=1, source_target_pairs={{0,4},{4,0},{8,12},{12,8},{16,20},{20,16},{24,28},{28,24},{1,5},{5... | collective-permute-start | bytes 1769480 | tf_op jit(solution)/shard_map/ppermute | solution.py:255
  58.9 2.8 %copy-start = (s32[8]{0:T(128)S(1)}, s32[8]{0:T(128)}, u32[]{:S(2)}) copy-start(s32[8]{0:T(128)} %flags.1) | copy-start | bytes 100

commit v3 on v2

--- a/solution.py
+++ b/solution.py
@@ -28,45 +28,61 @@
     return slice(TILE * (t + 1) + off, TILE * (t + 1) + off + TILE)
 
 
-def assemble(planes, odd, first, outer_first, own, other, near, far, outer, store):
+def assemble(planes, odd, first, outer_first, pieces, store):
+    pieces = [*pieces[:3], *[pieces[3].at[t] for t in range(TILES)], *[pieces[4].at[t] for t in range(TILES)]]
     inner_at = (1 - odd) * (planes + HALO)
     outer_at = odd * (planes + HALO)
-    near_row = odd * (2 * TILE)
-    far_row = (2 - 2 * odd) * TILE
-
-    def run(count, pick, at, row):
-        def one(p, carry):
+    places = [(at, t * TILE) for at in (HALO, inner_at, outer_at) for t in range(TILES)]
+
+    for k, (ref, (at, row)) in enumerate(zip(pieces, places)):
+        start = outer_first if k >= 6 else first
+
+        def one(p, carry, ref=ref, start=start, at=at, row=row):
             for c in range(3):
                 for i, x in enumerate(HALVES):
-                    store(c, at + p, i, row, pick(c, p, x))
+                    store(c, at + p, i, row, ref, start, p, x)
             return carry
 
-        lax.fori_loop(0, count, one, 0, unroll=4)
-
-    skip = odd * HALO
-    run(planes, lambda c, p, x: own[first + c, p, :, x], HALO, TILE)
-    run(HALO, lambda c, p, x: other[first + c, skip + p, :, x], inner_at, TILE)
-    run(planes, lambda c, p, x: near[0, first + c, p, :, x], HALO, near_row)
-    run(HALO, lambda c, p, x: near[1, first + c, skip + p, :, x], inner_at, near_row)
-    run(planes, lambda c, p, x: far[first + c, p, :, x], HALO, far_row)
-    run(HALO, lambda c, p, x: far[first + c, planes + p, :, x], inner_at, far_row)
-    for t in range(TILES):
-        run(HALO, lambda c, p, x: outer[t, outer_first + c, p, :, x], outer_at, TILE * t)
-
-
-def prepare_kernel(planes, pos, tables, own, other, near, far, outer, E, A, B, K, ids):
+        lax.fori_loop(0, ref.shape[1], one, 0, unroll=4)
+
+
+def start_kernel(planes, pos, electric, magnetic, material, incoming, edge, block, entering, ids, late, fresh, sems):
+    gz, count_z = pos[0], pos[4]
+    edge_at = lax.rem(gz, 2) * HALO
+    late_at = jnp.clip(gz - count_z + 2, 0, 1) * planes
+    near = pl.ds(edge_at, HALO)
+    pairs = [(material, ids), (incoming.at[pl.ds(0, HALO)], fresh)]
+    pairs += [(electric.at[c], block.at[c]) for c in range(3)]
+    pairs += [(magnetic.at[c, near], edge.at[3 + c]) for c in range(3)]
+    pairs += [(incoming.at[pl.ds(late_at, planes)], late)]
+    copies = [pltpu.make_async_copy(src, dst, sems.at[i]) for i, (src, dst) in enumerate(pairs)]
+    for one in copies:
+        one.start()
+    for one in copies:
+        one.wait()
+    block[3] = ids[...].astype(jnp.float32)
+    entering[...] = late[...].astype(jnp.float32)
+    for p in range(HALO):
+        for c in range(3):
+            edge[c, p] = block[c, edge_at + p]
+        edge[6, p] = jnp.where(gz == 0, fresh[p], ids[edge_at + p]).astype(jnp.float32)
+
+    @pl.when(gz == 0)
+    def _():
+        edge[0:6] = jnp.zeros((6,) + edge.shape[1:], jnp.float32)
+
+
+def prepare_kernel(planes, pos, tables, *refs):
+    pieces, (E, A, B, K, ids) = refs[:5], refs[5:]
     odd = lax.rem(pos[0], 2)
 
-    def store(c, p, i, row, value):
-        E[c, p, i, pl.ds(pl.multiple_of(row, TILE), TILE), :] = value
-
-    assemble(planes, odd, 0, 0, own, other, near, far, outer, store)
-
-    def store_id(c, p, i, row, value):
+    def store(c, p, i, row, ref, start, q, x):
+        at = pl.ds(row, TILE)
+        E[c, p, i, at, :] = ref[start + c, q, :, x]
         if c == 0:
-            ids[p, i, pl.ds(pl.multiple_of(row, TILE), TILE), :] = value
-
-    assemble(planes, odd, 3, 6, IdsView(own), IdsView(other), IdsView(near), IdsView(far), IdsView(outer), store_id)
+            ids[p, i, at, :] = ref[ref.shape[0] - 1, q, :, x]
+
+    assemble(planes, odd, 0, 0, pieces, store)
 
     def look_up(p, carry):
         for t in range(TILES):
@@ -79,21 +95,10 @@
     lax.fori_loop(0, planes + 2 * HALO, look_up, 0, unroll=4)
 
 
-class IdsView:
-    def __init__(self, ref):
-        self.ref = ref
-        self.at = ref.shape[-4] - 1
-
-    def __getitem__(self, key):
-        key = list(key)
-        key[-4] = self.at
-        return self.ref[tuple(key)]
-
-
 def step_kernel(
-    planes, pos, flags, E0, A, B, K, own, other, near, far, outer,
-    e_out, h_out, E1, E2, H1, H2, e_stage, h_stage, out_sems,
+    planes, pos, flags, E0, A, B, K, *refs
 ):
+    pieces, (e_out, h_out, E1, E2, H1, H2, e_stage, h_stage, out_sems) = refs[:5], refs[5:]
     gz, gy, last_y, top_z = pos[0], pos[1], pos[2], pos[3]
     wide = planes + 2 * HALO
     odd = lax.rem(gz, 2)
@@ -104,10 +109,10 @@
     below = jnp.where((gy == 0) & (sub == 0), 0.0, 1.0).astype(jnp.float32)
     above = jnp.where((gy == last_y) & (sub == TILE - 1), 0.0, 1.0).astype(jnp.float32)
 
-    def store(c, p, i, row, value):
-        H1[c, p, i, pl.ds(pl.multiple_of(row + TILE, TILE), TILE), :] = 2.0 * value
-
-    assemble(planes, odd, 0, 3, own, other, near, far, outer, store)
+    def store(c, p, i, row, ref, start, q, x):
+        H1[c, p, i, pl.ds(row + TILE, TILE), :] = 2.0 * ref[start + c, q, :, x]
+
+    assemble(planes, odd, 0, 3, pieces, store)
 
     def x_next(v):
         r = [pltpu.roll(a, LANES - 1, 1) for a in v]
@@ -214,6 +219,24 @@
 SMEM, VMEM, ANY = [pl.BlockSpec(memory_space=m) for m in (pltpu.SMEM, pltpu.VMEM, pl.ANY)]
 
 
+def start(pos, electric, magnetic, material, incoming, planes, rows, width):
+    def shape(*lead):
+        return jax.ShapeDtypeStruct(lead + (rows, width), jnp.float32)
+
+    def whole(count):
+        return pltpu.VMEM((count, rows, width), jnp.int32)
+
+    return pl.pallas_call(
+        functools.partial(start_kernel, planes),
+        out_shape=(shape(7, HALO), shape(4, planes), shape(planes)),
+        in_specs=[SMEM] + [ANY] * 4,
+        out_specs=(VMEM,) * 3,
+        scratch_shapes=[whole(planes), whole(planes), whole(HALO), pltpu.SemaphoreType.DMA((9,))],
+        compiler_params=pltpu.CompilerParams(vmem_limit_bytes=60 * 2**20),
+        name="start",
+    )(pos, electric, magnetic, material, incoming)
+
+
 def prepare(pos, tables, pieces, planes):
     deep = planes + 2 * HALO + PAD
     coef = jax.ShapeDtypeStruct((deep, 2, TILES * TILE, LANES), jnp.float32)
@@ -223,7 +246,8 @@
         in_specs=[SMEM] + [VMEM] * (1 + len(pieces)),
         out_specs=(VMEM,) * 4,
         scratch_shapes=[pltpu.VMEM(coef.shape, jnp.float32)],
-        compiler_params=pltpu.CompilerParams(vmem_limit_bytes=24 * 2**20),
+        compiler_params=pltpu.CompilerParams(vmem_limit_bytes=4 * 2**20),
+        cost_estimate=pl.CostEstimate(flops=0, bytes_accessed=32 * 2**20, transcendentals=0),
         name="prepare",
     )(pos, tables, *pieces)
 
@@ -240,28 +264,24 @@
         scratch_shapes=[work] * 4
         + [pltpu.VMEM(field.shape, jnp.float32)] * 2
         + [pltpu.SemaphoreType.DMA((2,))],
-        compiler_params=pltpu.CompilerParams(vmem_limit_bytes=32 * 2**20),
+        compiler_params=pltpu.CompilerParams(vmem_limit_bytes=20 * 2**20),
         name="fdtd_steps",
     )(pos, flags, *full, *pieces)
 
 
-def down(value, hop, wrap=0):
+def shift(value, axis, hop):
+    count = lax.axis_size(axis)
+    return lax.ppermute(value, axis, [(s, s + hop) for s in range(count) if 0 <= s + hop < count])
+
+
+def outer_planes(value):
     count = lax.axis_size("gz")
-    pairs = [(s, s - hop) for s in range(hop, count)] + [(s, count + s - hop) for s in range(wrap)]
-    return lax.ppermute(value, "gz", pairs)
+    pairs = [(s, s - 1) for s in range(1, count, 2)] + [(s, s - 3) for s in range(4, count, 2)]
+    return lax.ppermute(value, "gz", pairs + [(0, count - 3)])
 
 
 def swap_cores(value):
     return lax.ppermute(value, "gz", [(s, s ^ 1) for s in range(lax.axis_size("gz"))])
-
-
-def y_halo(value):
-    nz, ny = lax.axis_size("gz"), lax.axis_size("gy")
-    pairs = []
-    for z in range(nz):
-        hop = 1 - 2 * (z % 2)
-        pairs += [(z * ny + y, z * ny + y + hop) for y in range(ny) if 0 <= y + hop < ny]
-    return lax.ppermute(value, ("gz", "gy"), pairs)
 
 
 def body(electric, magnetic, material, incoming, shift_flags, eps_table, sigma_table, kerr_table):
@@ -272,57 +292,36 @@
     assert rows == HALO and width == 2 * LANES and count_z % 2 == 0 and count_z >= 4
     gz, gy = lax.axis_index("gz"), lax.axis_index("gy")
     odd = gz % 2 == 1
-
-    moved_e = down(jnp.concatenate([electric, material.astype(jnp.float32)[None]], 0), hop)
-    moved_h = down(magnetic, hop)
-
-    def edge(field):
-        return jnp.where(odd, field[..., HALO:, :, :], field[..., :HALO, :, :])
-
-    fields = jnp.concatenate([edge(electric), edge(magnetic)], 0)
-    fresh = jnp.where(gz == 0, incoming[:HALO], edge(material)).astype(jnp.float32)
-    mine = jnp.concatenate([jnp.where(gz == 0, 0.0, fields), fresh[None]], 0)
-    theirs = swap_cores(mine)
-    mine_y, theirs_y = y_halo(jnp.stack([mine, theirs]))
-    part = HALO // 2
-    crossed = down(
-        jnp.where(
-            odd,
-            jnp.concatenate([theirs_y, theirs[:, part:]], 1),
-            jnp.concatenate([mine_y, mine[:, :part]], 1),
-        ),
-        2 * hop,
-        wrap=2,
-    )
-    given = swap_cores(jnp.where(odd, jnp.concatenate([mine_y, crossed[:, HALO:]], 1), crossed))
-    outer = jnp.stack(
-        [
-            jnp.where(odd, given[:, :HALO], theirs_y),
-            jnp.where(odd, jnp.concatenate([given[:, HALO:], crossed[:, HALO:]], 1), theirs),
-            jnp.where(odd, crossed[:, :HALO], given[:, :HALO]),
-        ]
-    )
+    pos = jnp.stack([gz, gy, count_y - 1, count_z * planes, count_z]).astype(jnp.int32)
+
+    edge, block, entering = start(pos, electric, magnetic, material, incoming, planes, rows, width)
+
+    def spread(own):
+        dn, up = shift(own, "gy", 1), shift(own, "gy", -1)
+        return dn, up
+
+    moved_e = shift(block, "gz", -hop)
+    moved_h = shift(lax.optimization_barrier((magnetic, edge))[0], "gz", -hop)
+    edge_dn, edge_up = spread(edge)
+    outer = outer_planes(jnp.stack([edge_dn, edge, edge_up]))
+    outer_pieces = [outer]
 
     def around(own):
-        other = swap_cores(own)
-        near = y_halo(jnp.stack([own, other]))
-        edge_rows = jnp.where(odd, near[0, :, :HALO], near[0, :, HALO:])
-        far = swap_cores(jnp.concatenate([near[1], edge_rows], 1))
-        return [own, other, near, far]
-
-    fresh_at = jnp.clip(gz - (count_z - hop), 0, hop - 1) * planes
-    entering = lax.dynamic_slice_in_dim(incoming, fresh_at, planes, 0).astype(jnp.float32)
+        dn, up = spread(own)
+        return [dn, own, up], jnp.stack([jnp.where(odd, field[:, :HALO], field[:, HALO:]) for field in (dn, own, up)])
+
     ids = jnp.where(gz >= count_z - hop, entering, moved_e[3])
-    e_pieces = around(jnp.concatenate([moved_e[:3], ids[None]], 0))
-    h_pieces = around(moved_h)
+    block = jnp.concatenate([moved_e[:3], ids[None]], 0)
+    e_pieces, e_near = around(block)
+    h_pieces, h_near = around(lax.optimization_barrier((moved_h, block, edge_dn, edge_up))[0])
 
     tables = jnp.stack(
         [4.0 * eps_table - 2.0 * sigma_table, 4.0 * eps_table + 2.0 * sigma_table, 4.0 * kerr_table]
     )
     tables = jnp.broadcast_to(jnp.pad(tables, ((0, 0), (0, LANES - MAT)))[:, None, :], (3, TILE, LANES))
-    pos = jnp.stack([gz, gy, count_y - 1, count_z * planes]).astype(jnp.int32)
-    full = prepare(pos, tables, e_pieces + [outer], planes)
-    return run_steps(pos, shift_flags, full, h_pieces + [outer], planes, rows, width)
+    full = prepare(pos, tables, e_pieces + [swap_cores(e_near)] + outer_pieces, planes)
+    h_near, *full = lax.optimization_barrier((h_near, *full))
+    return run_steps(pos, shift_flags, full, h_pieces + [swap_cores(h_near)] + outer_pieces, planes, rows, width)
 
 
 def solution(mesh):

time: 75.3 us -> 67.3 us (0.89)
  waiting for transfers between devices: 25.4 us -> 15.7 us
  other arithmetic: 9.53 us -> 1.5 us
  starting transfers between devices: 21.6 us -> 28.7 us
  Pallas kernels: 15.7 us -> 18.6 us
    ppermute x6 -> x9, starting transfers between devices: 11.8 us -> 25.3 us  [the longest x8 20.1 us: shift(): lax.ppermute(value, axis, [(s, s + hop) for s in range(count) if 0 <= s +...]
    ppermute x6 -> x9, waiting for transfers between devices: 24.4 us -> 14.1 us  [the longest x8 14.1 us: shift(): lax.ppermute(value, axis, [(s, s + hop) for s in range(count) if 0 <= s +...]
    ppermute x6 -> x2, starting transfers between devices: 9.81 us -> 3.43 us  [swap_cores(): lax.ppermute(value, 'gz', [(s, s ^ 1) for s in range(lax.axis_size('gz'))])]
    another operation x9, other arithmetic: 6.25 us -> 1.42 us  [the longest x1 1.13 us: body(): outer = outer_planes(jnp.stack([edge_dn, edge, edge_up]))]
    pallas_call x0 -> x1, Pallas kernels: none -> 3.01 us  [start(): pl.pallas_call(functools.partial(start_kernel, planes), out_shape=(shape(...]
    select_n x7 -> x0, other arithmetic: 2.38 us -> none  [the longest x2 2.11 us: edge(): return jnp.where(odd, field[..., HALO:, :, :], field[..., :HALO, :, :])]
    concatenate x4 -> x1, other arithmetic: 0.83 us -> 0.04 us  [body(): block = jnp.concatenate([moved_e[:3], ids[None]], 0)]
    ppermute x6 -> x2, waiting for transfers between devices: 0.95 us -> 1.63 us  [swap_cores(): lax.ppermute(value, 'gz', [(s, s ^ 1) for s in range(lax.axis_size('gz'))])]
  transfers between devices with their start and end apart: 12 -> 11, of which waited for: 5 -> 4; matrix products, arithmetic and copies ran while one was open for 15% -> 2% of each run, Pallas kernels for 4% -> 0%
where the time goes in v3:
time: 67.3 us; the launch traced here: 66.2 us
  starting transfers between devices  28.7 us (43%)
  Pallas kernels  18.6 us (28%)
  waiting for transfers between devices  15.7 us (23%)
  other arithmetic  1.5 us (2%)
  between operations  0.98 us (1%)
  local copies, waits for them, and re-layouts  0.69 us (1%)
    ppermute x8, starting transfers between devices, shift(): lax.ppermute(value, axis, [(s, s + hop) for s in range(count) if 0 <= s +...  20.1 us
    ppermute x8, waiting for transfers between devices, shift(): lax.ppermute(value, axis, [(s, s + hop) for s in range(count) if 0 <= s +...  14.1 us
    pallas_call x1, Pallas kernels, run_steps(): pl.pallas_call(functools.partial(step_kernel, planes), out_shape=(field,...  13 us
    ppermute x1, starting transfers between devices, outer_planes(): return lax.ppermute(value, 'gz', pairs + [(0, count - 3)])  5.16 us
    ppermute x2, starting transfers between devices, swap_cores(): lax.ppermute(value, 'gz', [(s, s ^ 1) for s in range(lax.axis_size('gz'))])  3.43 us
    pallas_call x1, Pallas kernels, start(): pl.pallas_call(functools.partial(start_kernel, planes), out_shape=(shape(...  3.01 us
    pallas_call x1, Pallas kernels, prepare(): pl.pallas_call(functools.partial(prepare_kernel, planes), out_shape=(jax....  2.67 us
    ppermute x2, waiting for transfers between devices, swap_cores(): lax.ppermute(value, 'gz', [(s, s ^ 1) for s in range(lax.axis_size('gz'))])  1.63 us
  transfers between devices with their start and end apart: 11, of which 4 were waited for; matrix products, arithmetic and copies ran while one was open for 2% of the time, Pallas kernels for 0%

profile of v3, /device:TPU:11, one launch (start us, length us, event | category | flops | bytes accessed | tf_op | source)
XLA Modules:
  0.0 66.2 jit_solution(9780919921049490596)
XLA Ops:
  0.6 0.6 stack.59.pos
  1.3 3.0 %start.1 = (f32[7,8,8,256]{3,2,1,0:T(8,128)}, f32[4,16,8,256]{3,2,1,0:T(8,128)}, f32[16,8,256]{2,1,0:T(8,128)}) custom-call(s32[5]{0:T(128)} %stack.59.pos, f32[3,16,8,256]{3,2,1,0:T(8,128)} %electric.1, f32[3,16,8,256]{3,2,1,0:T(8,128)} %magnetic.1, s32[16,8,256]{2,1,0:T(8,128)} %material.1, s32[32,8,256]{2,1,0:T(8,128)} %incoming.1), custom_call_target="tpu_custom_call" | custom-call | tf_op jit(solution)/shard_map/start/pallas_call | solution.py:229
  4.3 0.0 copy-start.3
  4.3 0.0 copy-start.4
  4.3 0.0 copy-start.5
  4.3 0.0 copy-start.2
  4.3 2.3 %collective-permute-start.1 = (f32[4,16,8,256]{3,2,1,0:T(8,128)}, f32[4,16,8,256]{3,2,1,0:T(8,128)S(1)}, u32[]{:S(2)}, u32[]{:S(2)}) collective-permute-start(f32[4,16,8,256]{3,2,1,0:T(8,128)} %get-tuple-element.18), channel_id=1, source_target_pairs={{8,0},{12,4},{16,8},{20,12},{24,16},{28,20},{9,1},{13,5},{17,9},{2... | collective-permute-start | bytes 1572872 | tf_op jit(solution)/shard_map/ppermute | solution.py:274
  6.6 3.2 %collective-permute-start.2 = (f32[7,8,8,256]{3,2,1,0:T(8,128)}, f32[7,8,8,256]{3,2,1,0:T(8,128)S(1)}, u32[]{:S(2)}, u32[]{:S(2)}) collective-permute-start(f32[7,8,8,256]{3,2,1,0:T(8,128)} %get-tuple-element.16), channel_id=1, source_target_pairs={{0,1},{1,2},{2,3},{4,5},{5,6},{6,7},{8,9},{9,10},{10,11},{12,13},{... | collective-permute-start | bytes 1376264 | tf_op jit(solution)/shard_map/ppermute | solution.py:274
  9.8 2.1 %collective-permute-start.3 = (f32[7,8,8,256]{3,2,1,0:T(8,128)}, f32[7,8,8,256]{3,2,1,0:T(8,128)}, u32[]{:S(2)}, u32[]{:S(2)}) collective-permute-start(f32[7,8,8,256]{3,2,1,0:T(8,128)} %get-tuple-element.16), channel_id=1, source_target_pairs={{1,0},{2,1},{3,2},{5,4},{6,5},{7,6},{9,8},{10,9},{11,10},{13,12},{... | collective-permute-start | bytes 1376264 | tf_op jit(solution)/shard_map/ppermute | solution.py:274
  12.0 1.9 %collective-permute-start = (f32[3,16,8,256]{3,2,1,0:T(8,128)}, f32[3,16,8,256]{3,2,1,0:T(8,128)S(1)}, u32[]{:S(2)}, u32[]{:S(2)}) collective-permute-start(f32[3,16,8,256]{3,2,1,0:T(8,128)} %magnetic.1), channel_id=1, source_target_pairs={{8,0},{12,4},{16,8},{20,12},{24,16},{28,20},{9,1},{13,5},{17,9},{2... | collective-permute-start | bytes 1179656 | tf_op jit(solution)/shard_map/ppermute | solution.py:274
  13.9 6.4 %collective-permute-done.1 = f32[4,16,8,256]{3,2,1,0:T(8,128)S(1)} collective-permute-done((f32[4,16,8,256]{3,2,1,0:T(8,128)}, f32[4,16,8,256]{3,2,1,0:T(8,128)S(1)}, u32[]{:S(2)}, u32[]{:S(2)}) %collective-permute-start.1) | collective-permute-done | bytes 524320 | tf_op jit(solution)/shard_map/ppermute | solution.py:274
  20.4 2.1 %collective-permute-start.7 = (f32[4,16,8,256]{3,2,1,0:T(8,128)S(1)}, f32[4,16,8,256]{3,2,1,0:T(8,128)S(1)}, u32[]{:S(2)}, u32[]{:S(2)}) collective-permute-start(f32[4,16,8,256]{3,2,1,0:T(8,128)S(1)} %pad_maximum_fusion.1.refs_1_), channel_id=1, source_target_pairs={{1,0},{2,1},{3,2},{5,4},{6,5},{7,6},{9,8},{10,9},{11,10},{13,12},{... | collective-permute-start | bytes 1572872 | tf_op jit(solution)/shard_map/ppermute | solution.py:274
  22.5 0.0 copy-done.3
  22.5 0.0 copy-done.4
  22.5 0.0 copy-done.5
  22.5 3.2 %collective-permute-start.6 = (f32[4,16,8,256]{3,2,1,0:T(8,128)S(1)}, f32[4,16,8,256]{3,2,1,0:T(8,128)S(1)}, u32[]{:S(2)}, u32[]{:S(2)}) collective-permute-start(f32[4,16,8,256]{3,2,1,0:T(8,128)S(1)} %pad_maximum_fusion.1.refs_1_), channel_id=1, source_target_pairs={{0,1},{1,2},{2,3},{4,5},{5,6},{6,7},{8,9},{9,10},{10,11},{12,13},{... | collective-permute-start | bytes 1572872 | tf_op jit(solution)/shard_map/ppermute | solution.py:274
  25.7 0.0 collective-permute-done.2
  25.7 0.0 collective-permute-done.3
  25.8 0.0 copy-done.2
  25.8 1.1 %pad_maximum_fusion = f32[3,7,8,8,256]{4,3,2,1,0:T(8,128)S(1)} fusion(f32[1,7,8,8,256]{4,3,2,1,0:T(8,128)} %bitcast.15, f32[1,7,8,8,256]{4,3,2,1,0:T(8,128)S(1)} %bitcast.31, f32[1,7,8,8,256]{4,3,2,1,0:T(8,128)S(1)} %bitcast.32), kind=kLoop, calls=%fused_computation | loop fusion | flops 688128 | bytes 2752512 | tf_op jit(solution)/shard_map/stack | solution.py:306
  26.9 5.2 %collective-permute-start.9 = (f32[3,7,8,8,256]{4,3,2,1,0:T(8,128)S(1)}, f32[3,7,8,8,256]{4,3,2,1,0:T(8,128)S(1)}, u32[]{:S(2)}, u32[]{:S(2)}) collective-permute-start(f32[3,7,8,8,256]{4,3,2,1,0:T(8,128)S(1)} %pad_maximum_fusion), channel_id=1, source_target_pairs={{4,0},{12,8},{20,16},{28,24},{16,4},{24,12},{0,20},{5,1},{13,9},{2... | collective-permute-start | bytes 4128776 | tf_op jit(solution)/shard_map/ppermute | solution.py:280
  32.1 0.0 collective-permute-done.refs_1_
  32.1 3.2 %collective-permute-start.4 = (f32[3,16,8,256]{3,2,1,0:T(8,128)S(1)}, f32[3,16,8,256]{3,2,1,0:T(8,128)S(1)}, u32[]{:S(2)}, u32[]{:S(2)}) collective-permute-start(f32[3,16,8,256]{3,2,1,0:T(8,128)S(1)} %collective-permute-done.refs_1_), channel_id=1, source_target_pairs={{0,1},{1,2},{2,3},{4,5},{5,6},{6,7},{8,9},{9,10},{10,11},{12,13},{... | collective-permute-start | bytes 1179656 | tf_op jit(solution)/shard_map/ppermute | solution.py:274
  35.3 2.1 %collective-permute-start.5 = (f32[3,16,8,256]{3,2,1,0:T(8,128)S(1)}, f32[3,16,8,256]{3,2,1,0:T(8,128)S(1)}, u32[]{:S(2)}, u32[]{:S(2)}) collective-permute-start(f32[3,16,8,256]{3,2,1,0:T(8,128)S(1)} %collective-permute-done.refs_1_), channel_id=1, source_target_pairs={{1,0},{2,1},{3,2},{5,4},{6,5},{7,6},{9,8},{10,9},{11,10},{13,12},{... | collective-permute-start | bytes 1179656 | tf_op jit(solution)/shard_map/ppermute | solution.py:274
  37.5 0.0 collective-permute-done.7.refs_2_
  37.5 0.0 collective-permute-done.6.refs_0_
  37.6 0.1 pad_maximum_fusion.2
  37.6 0.0 copy-start
  37.6 2.8 %collective-permute-start.8 = (f32[3,4,8,8,256]{4,3,2,1,0:T(8,128)S(1)}, f32[3,4,8,8,256]{4,3,2,1,0:T(8,128)S(1)}, u32[]{:S(2)}, u32[]{:S(2)}) collective-permute-start(f32[3,4,8,8,256]{4,3,2,1,0:T(8,128)S(1)} %pad_maximum_fusion.2), channel_id=1, source_target_pairs={{0,4},{4,0},{8,12},{12,8},{16,20},{20,16},{24,28},{28,24},{1,5},{5... | collective-permute-start | bytes 2359304 | tf_op jit(solution)/shard_map/ppermute | solution.py:284
  40.5 4.7 %collective-permute-done.4.refs_0_ = f32[3,16,8,256]{3,2,1,0:T(8,128)S(1)} collective-permute-done((f32[3,16,8,256]{3,2,1,0:T(8,128)S(1)}, f32[3,16,8,256]{3,2,1,0:T(8,128)S(1)}, u32[]{:S(2)}, u32[]{:S(2)}) %collective-permute-start.4) | collective-permute-done | bytes 393248 | tf_op jit(solution)/shard_map/ppermute | solution.py:274
  45.2 3.0 %collective-permute-done.5.refs_2_ = f32[3,16,8,256]{3,2,1,0:T(8,128)S(1)} collective-permute-done((f32[3,16,8,256]{3,2,1,0:T(8,128)S(1)}, f32[3,16,8,256]{3,2,1,0:T(8,128)S(1)}, u32[]{:S(2)}, u32[]{:S(2)}) %collective-permute-start.5) | collective-permute-done | bytes 393248 | tf_op jit(solution)/shard_map/ppermute | solution.py:274
  48.3 0.0 collective-permute-done.8.refs_3_
  48.3 0.0 collective-permute-done.9.refs_4_
  48.4 0.0 copy-done
  48.4 0.0 copy-start.1
  48.4 2.7 %prepare.1 = (f32[3,40,2,32,128]{4,3,2,1,0:T(8,128)S(1)}, f32[40,2,24,128]{3,2,1,0:T(8,128)S(1)}, f32[40,2,24,128]{3,2,1,0:T(8,128)S(1)}, f32[40,2,24,128]{3,2,1,0:T(8,128)S(1)}) custom-call(s32[5]{0:T(128)S(1)} %copy-done, f32[3,8,128]{2,1,0:T(8,128)S(1)} %broadcast_in_dim.10.tables, f32[4,16,8,256]{3,2,1,0:T(8,128)S(1)} %collective-permute-done.6.refs_0_, ...), custom_call_target="tpu_custom_call" | custom-call | bytes 33554432 | tf_op jit(solution)/shard_map/prepare/pallas_call | solution.py:243
  51.0 0.6 collective-permute-start.10
  51.6 1.6 %collective-permute-done.10.refs_3_ = f32[3,3,8,8,256]{4,3,2,1,0:T(8,128)S(1)} collective-permute-done((f32[3,3,8,8,256]{4,3,2,1,0:T(8,128)S(1)}, f32[3,3,8,8,256]{4,3,2,1,0:T(8,128)S(1)}, u32[]{:S(2)}, u32[]{:S(2)}) %collective-permute-start.10) | collective-permute-done | bytes 589856 | tf_op jit(solution)/shard_map/ppermute | solution.py:284
  53.3 0.0 copy-done.1
  53.3 13.0 %fdtd_steps.1 = (f32[3,16,8,256]{3,2,1,0:T(8,128)}, f32[3,16,8,256]{3,2,1,0:T(8,128)}) custom-call(s32[5]{0:T(128)S(1)} %copy-done, s32[8]{0:T(128)S(1)} %copy-done.1, f32[3,40,2,32,128]{4,3,2,1,0:T(8,128)S(1)} %get-tuple-element.25.E0, f32[40,2,24,128]{3,2,1,0:T(8,128)S(1)} %get-tuple-element.26.A, f32[40,2,24,128]{3,2,1,0:T(8,128)S(1)} %get-tuple-element.27.B, ...), custom_call_target="tpu_custom_call" | custom-call | tf_op jit(solution)/shard_map/fdtd_steps/pallas_call | solution.py:259
  (13 shorter events, 0.3 us)
Async XLA Ops:
  4.3 18.2 %copy-start.3 = (f32[16]{0:T(128)S(1)}, f32[16]{0:T(128)}, u32[]{:S(2)}) copy-start(f32[16]{0:T(128)} %param.14) | copy-start | bytes 196
  4.3 18.2 %copy-start.4 = (f32[16]{0:T(128)S(1)}, f32[16]{0:T(128)}, u32[]{:S(2)}) copy-start(f32[16]{0:T(128)} %param.13) | copy-start | bytes 196
  4.3 18.2 %copy-start.5 = (f32[16]{0:T(128)S(1)}, f32[16]{0:T(128)}, u32[]{:S(2)}) copy-start(f32[16]{0:T(128)} %param.15) | copy-start | bytes 196
  4.3 21.4 %copy-start.2 = (f32[7,8,8,256]{3,2,1,0:T(8,128)S(1)}, f32[7,8,8,256]{3,2,1,0:T(8,128)}, u32[]{:S(2)}) copy-start(f32[7,8,8,256]{3,2,1,0:T(8,128)} %get-tuple-element.16) | copy-start | bytes 1376260
  4.3 15.9 %collective-permute-start.1 = (f32[4,16,8,256]{3,2,1,0:T(8,128)}, f32[4,16,8,256]{3,2,1,0:T(8,128)S(1)}, u32[]{:S(2)}, u32[]{:S(2)}) collective-permute-start(f32[4,16,8,256]{3,2,1,0:T(8,128)} %get-tuple-element.18), channel_id=1, source_target_pairs={{8,0},{12,4},{16,8},{20,12},{24,16},{28,20},{9,1},{13,5},{17,9},{2... | collective-permute-start | bytes 1572872 | tf_op jit(solution)/shard_map/ppermute | solution.py:274
  6.6 19.1 %collective-permute-start.2 = (f32[7,8,8,256]{3,2,1,0:T(8,128)}, f32[7,8,8,256]{3,2,1,0:T(8,128)S(1)}, u32[]{:S(2)}, u32[]{:S(2)}) collective-permute-start(f32[7,8,8,256]{3,2,1,0:T(8,128)} %get-tuple-element.16), channel_id=1, source_target_pairs={{0,1},{1,2},{2,3},{4,5},{5,6},{6,7},{8,9},{9,10},{10,11},{12,13},{... | collective-permute-start | bytes 1376264 | tf_op jit(solution)/shard_map/ppermute | solution.py:274
  9.8 15.9 %collective-permute-start.3 = (f32[7,8,8,256]{3,2,1,0:T(8,128)}, f32[7,8,8,256]{3,2,1,0:T(8,128)}, u32[]{:S(2)}, u32[]{:S(2)}) collective-permute-start(f32[7,8,8,256]{3,2,1,0:T(8,128)} %get-tuple-element.16), channel_id=1, source_target_pairs={{1,0},{2,1},{3,2},{5,4},{6,5},{7,6},{9,8},{10,9},{11,10},{13,12},{... | collective-permute-start | bytes 1376264 | tf_op jit(solution)/shard_map/ppermute | solution.py:274
  12.0 20.1 %collective-permute-start = (f32[3,16,8,256]{3,2,1,0:T(8,128)}, f32[3,16,8,256]{3,2,1,0:T(8,128)S(1)}, u32[]{:S(2)}, u32[]{:S(2)}) collective-permute-start(f32[3,16,8,256]{3,2,1,0:T(8,128)} %magnetic.1), channel_id=1, source_target_pairs={{8,0},{12,4},{16,8},{20,12},{24,16},{28,20},{9,1},{13,5},{17,9},{2... | collective-permute-start | bytes 1179656 | tf_op jit(solution)/shard_map/ppermute | solution.py:274
  20.4 17.1 %collective-permute-start.7 = (f32[4,16,8,256]{3,2,1,0:T(8,128)S(1)}, f32[4,16,8,256]{3,2,1,0:T(8,128)S(1)}, u32[]{:S(2)}, u32[]{:S(2)}) collective-permute-start(f32[4,16,8,256]{3,2,1,0:T(8,128)S(1)} %pad_maximum_fusion.1.refs_1_), channel_id=1, source_target_pairs={{1,0},{2,1},{3,2},{5,4},{6,5},{7,6},{9,8},{10,9},{11,10},{13,12},{... | collective-permute-start | bytes 1572872 | tf_op jit(solution)/shard_map/ppermute | solution.py:274
  22.5 15.0 %collective-permute-start.6 = (f32[4,16,8,256]{3,2,1,0:T(8,128)S(1)}, f32[4,16,8,256]{3,2,1,0:T(8,128)S(1)}, u32[]{:S(2)}, u32[]{:S(2)}) collective-permute-start(f32[4,16,8,256]{3,2,1,0:T(8,128)S(1)} %pad_maximum_fusion.1.refs_1_), channel_id=1, source_target_pairs={{0,1},{1,2},{2,3},{4,5},{5,6},{6,7},{8,9},{9,10},{10,11},{12,13},{... | collective-permute-start | bytes 1572872 | tf_op jit(solution)/shard_map/ppermute | solution.py:274
  26.9 21.4 %collective-permute-start.9 = (f32[3,7,8,8,256]{4,3,2,1,0:T(8,128)S(1)}, f32[3,7,8,8,256]{4,3,2,1,0:T(8,128)S(1)}, u32[]{:S(2)}, u32[]{:S(2)}) collective-permute-start(f32[3,7,8,8,256]{4,3,2,1,0:T(8,128)S(1)} %pad_maximum_fusion), channel_id=1, source_target_pairs={{4,0},{12,8},{20,16},{28,24},{16,4},{24,12},{0,20},{5,1},{13,9},{2... | collective-permute-start | bytes 4128776 | tf_op jit(solution)/shard_map/ppermute | solution.py:280
  32.1 13.1 %collective-permute-start.4 = (f32[3,16,8,256]{3,2,1,0:T(8,128)S(1)}, f32[3,16,8,256]{3,2,1,0:T(8,128)S(1)}, u32[]{:S(2)}, u32[]{:S(2)}) collective-permute-start(f32[3,16,8,256]{3,2,1,0:T(8,128)S(1)} %collective-permute-done.refs_1_), channel_id=1, source_target_pairs={{0,1},{1,2},{2,3},{4,5},{5,6},{6,7},{8,9},{9,10},{10,11},{12,13},{... | collective-permute-start | bytes 1179656 | tf_op jit(solution)/shard_map/ppermute | solution.py:274
  35.3 12.9 %collective-permute-start.5 = (f32[3,16,8,256]{3,2,1,0:T(8,128)S(1)}, f32[3,16,8,256]{3,2,1,0:T(8,128)S(1)}, u32[]{:S(2)}, u32[]{:S(2)}) collective-permute-start(f32[3,16,8,256]{3,2,1,0:T(8,128)S(1)} %collective-permute-done.refs_1_), channel_id=1, source_target_pairs={{1,0},{2,1},{3,2},{5,4},{6,5},{7,6},{9,8},{10,9},{11,10},{13,12},{... | collective-permute-start | bytes 1179656 | tf_op jit(solution)/shard_map/ppermute | solution.py:274
  37.6 10.7 %copy-start = (s32[5]{0:T(128)S(1)}, s32[5]{0:T(128)}, u32[]{:S(2)}) copy-start(s32[5]{0:T(128)} %stack.59.pos) | copy-start | bytes 64
  37.6 10.7 %collective-permute-start.8 = (f32[3,4,8,8,256]{4,3,2,1,0:T(8,128)S(1)}, f32[3,4,8,8,256]{4,3,2,1,0:T(8,128)S(1)}, u32[]{:S(2)}, u32[]{:S(2)}) collective-permute-start(f32[3,4,8,8,256]{4,3,2,1,0:T(8,128)S(1)} %pad_maximum_fusion.2), channel_id=1, source_target_pairs={{0,4},{4,0},{8,12},{12,8},{16,20},{20,16},{24,28},{28,24},{1,5},{5... | collective-permute-start | bytes 2359304 | tf_op jit(solution)/shard_map/ppermute | solution.py:284
  48.4 4.9 %copy-start.1 = (s32[8]{0:T(128)S(1)}, s32[8]{0:T(128)}, u32[]{:S(2)}) copy-start(s32[8]{0:T(128)} %flags.1) | copy-start | bytes 100
  51.0 2.2 %collective-permute-start.10 = (f32[3,3,8,8,256]{4,3,2,1,0:T(8,128)S(1)}, f32[3,3,8,8,256]{4,3,2,1,0:T(8,128)S(1)}, u32[]{:S(2)}, u32[]{:S(2)}) collective-permute-start(f32[3,3,8,8,256]{4,3,2,1,0:T(8,128)S(1)} %pad_maximum_fusion.3), channel_id=1, source_target_pairs={{0,4},{4,0},{8,12},{12,8},{16,20},{20,16},{24,28},{28,24},{1,5},{5... | collective-permute-start | bytes 1769480 | tf_op jit(solution)/shard_map/ppermute | solution.py:284

commit v4 on v3

--- a/solution.py
+++ b/solution.py
@@ -16,7 +16,7 @@
 TILE = 8
 TILES = 3
 PAD = 8
-GROUP = 8
+GROUP = 6
 HALVES = (slice(0, LANES), slice(LANES, 2 * LANES))
 
 
@@ -52,8 +52,8 @@
     late_at = jnp.clip(gz - count_z + 2, 0, 1) * planes
     near = pl.ds(edge_at, HALO)
     pairs = [(material, ids), (incoming.at[pl.ds(0, HALO)], fresh)]
-    pairs += [(electric.at[c], block.at[c]) for c in range(3)]
-    pairs += [(magnetic.at[c, near], edge.at[3 + c]) for c in range(3)]
+    pairs += [(magnetic.at[c], block.at[c]) for c in range(3)]
+    pairs += [(electric.at[c, near], edge.at[c]) for c in range(3)]
     pairs += [(incoming.at[pl.ds(late_at, planes)], late)]
     copies = [pltpu.make_async_copy(src, dst, sems.at[i]) for i, (src, dst) in enumerate(pairs)]
     for one in copies:
@@ -64,7 +64,7 @@
     entering[...] = late[...].astype(jnp.float32)
     for p in range(HALO):
         for c in range(3):
-            edge[c, p] = block[c, edge_at + p]
+            edge[3 + c, p] = block[c, edge_at + p]
         edge[6, p] = jnp.where(gz == 0, fresh[p], ids[edge_at + p]).astype(jnp.float32)
 
     @pl.when(gz == 0)
@@ -72,33 +72,11 @@
         edge[0:6] = jnp.zeros((6,) + edge.shape[1:], jnp.float32)
 
 
-def prepare_kernel(planes, pos, tables, *refs):
-    pieces, (E, A, B, K, ids) = refs[:5], refs[5:]
-    odd = lax.rem(pos[0], 2)
-
-    def store(c, p, i, row, ref, start, q, x):
-        at = pl.ds(row, TILE)
-        E[c, p, i, at, :] = ref[start + c, q, :, x]
-        if c == 0:
-            ids[p, i, at, :] = ref[ref.shape[0] - 1, q, :, x]
-
-    assemble(planes, odd, 0, 0, pieces, store)
-
-    def look_up(p, carry):
-        for t in range(TILES):
-            for i in range(2):
-                index = ids[p, i, e_at(t), :].astype(jnp.int32)
-                for k, out in enumerate((A, B, K)):
-                    out[p, i, e_at(t), :] = jnp.take_along_axis(tables[k], index, axis=1)
-        return carry
-
-    lax.fori_loop(0, planes + 2 * HALO, look_up, 0, unroll=4)
-
-
 def step_kernel(
-    planes, pos, flags, E0, A, B, K, *refs
+    planes, pos, flags, tables, *refs
 ):
-    pieces, (e_out, h_out, E1, E2, H1, H2, e_stage, h_stage, out_sems) = refs[:5], refs[5:]
+    e_pieces, h_pieces, outer, refs = refs[:4], refs[4:8], refs[8:9], refs[9:]
+    e_out, h_out, E1, E2, H1, H2, A, B, K, ids, e_stage, h_stage, out_sems = refs
     gz, gy, last_y, top_z = pos[0], pos[1], pos[2], pos[3]
     wide = planes + 2 * HALO
     odd = lax.rem(gz, 2)
@@ -109,10 +87,26 @@
     below = jnp.where((gy == 0) & (sub == 0), 0.0, 1.0).astype(jnp.float32)
     above = jnp.where((gy == last_y) & (sub == TILE - 1), 0.0, 1.0).astype(jnp.float32)
 
-    def store(c, p, i, row, ref, start, q, x):
+    def store_e(c, p, i, row, ref, start, q, x):
+        at = pl.ds(row, TILE)
+        E2[c, p, i, at, :] = ref[start + c, q, :, x]
+
+    def store_h(c, p, i, row, ref, start, q, x):
         H1[c, p, i, pl.ds(row + TILE, TILE), :] = 2.0 * ref[start + c, q, :, x]
-
-    assemble(planes, odd, 0, 3, pieces, store)
+        if c == 0:
+            ids[p, i, pl.ds(row, TILE), :] = ref[ref.shape[0] - 1, q, :, x]
+
+    def look_up(p, carry):
+        for t in range(TILES):
+            for i in range(2):
+                index = ids[p, i, e_at(t), :].astype(jnp.int32)
+                for k, out in enumerate((A, B, K)):
+                    out[p, i, e_at(t), :] = jnp.take_along_axis(tables[k], index, axis=1)
+        return carry
+
+    assemble(planes, odd, 0, 0, e_pieces + outer, store_e)
+    assemble(planes, odd, 0, 3, h_pieces + outer, store_h)
+    lax.fori_loop(0, wide, look_up, 0, unroll=8)
 
     def x_next(v):
         r = [pltpu.roll(a, LANES - 1, 1) for a in v]
@@ -171,21 +165,32 @@
 
     base = planes * gz + SHIFT * SHIFTS - HALO
 
-    def grouped(plane, start, count):
-        def one(g, carry):
-            for j in range(GROUP):
-                plane(start + g * GROUP + j)
-            return carry
-
-        lax.fori_loop(0, lax.div(count + GROUP - 1, GROUP), one, 0)
-
     h_copy = pltpu.make_async_copy(h_stage, h_out, out_sems.at[1])
-    e_copy = pltpu.make_async_copy(e_stage, e_out, out_sems.at[0])
+    e_copy = pltpu.make_async_copy(e_stage.at[:, pl.ds(0, planes)], e_out, out_sems.at[0])
 
     def step(s, moved, Ei, Eo, Hi, Ho, last=False):
         moved = moved + flags[s - 1]
-        grouped(lambda p: magnetic_plane(Ei, Hi, Ho, p, last), s - 1, wide + 1 - 2 * s)
-        zero_plane(Ho, SHIFT * moved - 1 - base, wide)
+        below_window = SHIFT * moved - 1 - base
+        above_window = top_z + SHIFT * moved - base
+        groups = lax.div(wide - 2 * s + GROUP - 1, GROUP)
+
+        def close(start, count):
+            @pl.when((below_window >= start) & (below_window < start + count))
+            def _():
+                Ho[:, below_window] = jnp.zeros((3,) + Ho.shape[2:], jnp.float32)
+
+        def one(g, carry):
+            start = s + g * GROUP
+            for j in range(GROUP):
+                electric_plane(Ho, Ei, Eo, start + j, last)
+                magnetic_plane(Ei, Hi, Ho, start + GROUP + j, last)
+            close(start + GROUP, GROUP)
+            return carry
+
+        for j in range(GROUP + 1):
+            magnetic_plane(Ei, Hi, Ho, s - 1 + j, last)
+        close(s - 1, GROUP + 1)
+        lax.fori_loop(0, groups - 1, one, 0)
         if last:
             def finish(p, carry):
                 for c in range(3):
@@ -195,15 +200,15 @@
 
             lax.fori_loop(0, planes, finish, 0, unroll=4)
             h_copy.start()
-        grouped(lambda p: electric_plane(Ho, Ei, Eo, p, last), s, wide - 2 * s)
-        above_window = top_z + SHIFT * moved - base
+        for j in range(GROUP):
+            electric_plane(Ho, Ei, Eo, s + (groups - 1) * GROUP + j, last)
         if last:
             zero_plane(Eo, above_window - HALO, planes)
         else:
             zero_plane(Eo, above_window, wide)
         return moved
 
-    moved = step(1, jnp.int32(0), E0, E1, H1, H2)
+    moved = step(1, jnp.int32(0), E2, E1, H1, H2)
 
     def pair(k, moved):
         moved = step(2 * k, moved, E1, E2, H2, H1)
@@ -237,36 +242,25 @@
     )(pos, electric, magnetic, material, incoming)
 
 
-def prepare(pos, tables, pieces, planes):
-    deep = planes + 2 * HALO + PAD
-    coef = jax.ShapeDtypeStruct((deep, 2, TILES * TILE, LANES), jnp.float32)
-    return pl.pallas_call(
-        functools.partial(prepare_kernel, planes),
-        out_shape=(jax.ShapeDtypeStruct((3, deep, 2, 4 * TILE, LANES), jnp.float32), coef, coef, coef),
-        in_specs=[SMEM] + [VMEM] * (1 + len(pieces)),
-        out_specs=(VMEM,) * 4,
-        scratch_shapes=[pltpu.VMEM(coef.shape, jnp.float32)],
-        compiler_params=pltpu.CompilerParams(vmem_limit_bytes=4 * 2**20),
-        cost_estimate=pl.CostEstimate(flops=0, bytes_accessed=32 * 2**20, transcendentals=0),
-        name="prepare",
-    )(pos, tables, *pieces)
-
-
-def run_steps(pos, flags, full, pieces, planes, rows, width):
+def run_steps(pos, flags, tables, pieces, planes, rows, width):
     deep = planes + 2 * HALO + PAD
     field = jax.ShapeDtypeStruct((3, planes, rows, width), jnp.float32)
-    work = pltpu.VMEM((3, deep, 2, 4 * TILE, LANES), jnp.float32)
+
+    def vmem(*shape):
+        return pltpu.VMEM(shape, jnp.float32)
+
     return pl.pallas_call(
         functools.partial(step_kernel, planes),
         out_shape=(field, field),
-        in_specs=[SMEM, SMEM] + [VMEM] * (len(full) + len(pieces)),
+        in_specs=[SMEM, SMEM] + [VMEM] * (1 + len(pieces)),
         out_specs=(ANY,) * 2,
-        scratch_shapes=[work] * 4
-        + [pltpu.VMEM(field.shape, jnp.float32)] * 2
+        scratch_shapes=[vmem(3, deep, 2, 4 * TILE, LANES)] * 4
+        + [vmem(deep, 2, TILES * TILE, LANES)] * 4
+        + [vmem(3, planes + GROUP, rows, width), vmem(*field.shape)]
         + [pltpu.SemaphoreType.DMA((2,))],
-        compiler_params=pltpu.CompilerParams(vmem_limit_bytes=20 * 2**20),
+        compiler_params=pltpu.CompilerParams(vmem_limit_bytes=28 * 2**20),
         name="fdtd_steps",
-    )(pos, flags, *full, *pieces)
+    )(pos, flags, tables, *pieces)
 
 
 def shift(value, axis, hop):
@@ -300,8 +294,7 @@
         dn, up = shift(own, "gy", 1), shift(own, "gy", -1)
         return dn, up
 
-    moved_e = shift(block, "gz", -hop)
-    moved_h = shift(lax.optimization_barrier((magnetic, edge))[0], "gz", -hop)
+    moved_e, moved_h = shift(electric, "gz", -hop), shift(block, "gz", -hop)
     edge_dn, edge_up = spread(edge)
     outer = outer_planes(jnp.stack([edge_dn, edge, edge_up]))
     outer_pieces = [outer]
@@ -310,18 +303,19 @@
         dn, up = spread(own)
         return [dn, own, up], jnp.stack([jnp.where(odd, field[:, :HALO], field[:, HALO:]) for field in (dn, own, up)])
 
-    ids = jnp.where(gz >= count_z - hop, entering, moved_e[3])
-    block = jnp.concatenate([moved_e[:3], ids[None]], 0)
-    e_pieces, e_near = around(block)
-    h_pieces, h_near = around(lax.optimization_barrier((moved_h, block, edge_dn, edge_up))[0])
+    ids = jnp.where(gz >= count_z - hop, entering, moved_h[3])
+    moved_h = jnp.concatenate([moved_h[:3], ids[None]], 0)
+    e_pieces, e_near = around(moved_e)
+    h_pieces, h_near = around(lax.optimization_barrier((moved_h, moved_e, edge_dn, edge_up))[0])
 
     tables = jnp.stack(
         [4.0 * eps_table - 2.0 * sigma_table, 4.0 * eps_table + 2.0 * sigma_table, 4.0 * kerr_table]
     )
     tables = jnp.broadcast_to(jnp.pad(tables, ((0, 0), (0, LANES - MAT)))[:, None, :], (3, TILE, LANES))
-    full = prepare(pos, tables, e_pieces + [swap_cores(e_near)] + outer_pieces, planes)
-    h_near, *full = lax.optimization_barrier((h_near, *full))
-    return run_steps(pos, shift_flags, full, h_pieces + [swap_cores(h_near)] + outer_pieces, planes, rows, width)
+    e_near = swap_cores(e_near)
+    h_near, e_near = lax.optimization_barrier((h_near, e_near))
+    pieces = e_pieces + [e_near] + h_pieces + [swap_cores(h_near)] + outer_pieces
+    return run_steps(pos, shift_flags, tables, pieces, planes, rows, width)
 
 
 def solution(mesh):

time: 67.3 us -> 65.2 us (0.969)
  Pallas kernels: 18.6 us -> 15.7 us
  waiting for transfers between devices: 15.7 us -> 18.4 us
  starting transfers between devices: 28.7 us -> 26.7 us
    pallas_call x1 -> x0, Pallas kernels: 2.67 us -> none  [prepare(): pl.pallas_call(functools.partial(prepare_kernel, planes), out_shape=(jax....]
    ppermute x2, starting transfers between devices: 3.43 us -> 0.87 us  [swap_cores(): lax.ppermute(value, 'gz', [(s, s ^ 1) for s in range(lax.axis_size('gz'))])]
    ppermute x8, waiting for transfers between devices: 14.1 us -> 16.5 us  [shift(): lax.ppermute(value, axis, [(s, s + hop) for s in range(count) if 0 <= s +...]
  transfers between devices with their start and end apart: 11 -> 11, of which waited for: 4 -> 5; matrix products, arithmetic and copies ran while one was open for 2% -> 3% of each run, Pallas kernels for 0% -> 5%
where the time goes in v4:
time: 65.2 us; the launch traced here: 63.9 us
  starting transfers between devices  26.7 us (41%)
  waiting for transfers between devices  18.4 us (28%)
  Pallas kernels  15.7 us (24%)
  other arithmetic  1.52 us (2%)
  between operations  0.93 us (1%)
  local copies, waits for them, and re-layouts  0.75 us (1%)
    ppermute x8, starting transfers between devices, shift(): lax.ppermute(value, axis, [(s, s + hop) for s in range(count) if 0 <= s +...  20 us
    ppermute x8, waiting for transfers between devices, shift(): lax.ppermute(value, axis, [(s, s + hop) for s in range(count) if 0 <= s +...  16.5 us
    pallas_call x1, Pallas kernels, run_steps(): pl.pallas_call(functools.partial(step_kernel, planes), out_shape=(field,...  12.6 us
    ppermute x1, starting transfers between devices, outer_planes(): return lax.ppermute(value, 'gz', pairs + [(0, count - 3)])  5.83 us
    pallas_call x1, Pallas kernels, start(): pl.pallas_call(functools.partial(start_kernel, planes), out_shape=(shape(...  3.01 us
    ppermute x2, waiting for transfers between devices, swap_cores(): lax.ppermute(value, 'gz', [(s, s ^ 1) for s in range(lax.axis_size('gz'))])  1.87 us
  transfers between devices with their start and end apart: 11, of which 5 were waited for; matrix products, arithmetic and copies ran while one was open for 3% of the time, Pallas kernels for 5%

profile of v4, /device:TPU:11, one launch (start us, length us, event | category | flops | bytes accessed | tf_op | source)
XLA Modules:
  0.0 63.9 jit_solution(5237839744725872772)
XLA Ops:
  0.6 2.2 %collective-permute-start = (f32[3,16,8,256]{3,2,1,0:T(8,128)}, f32[3,16,8,256]{3,2,1,0:T(8,128)S(1)}, u32[]{:S(2)}, u32[]{:S(2)}) collective-permute-start(f32[3,16,8,256]{3,2,1,0:T(8,128)} %electric.1), channel_id=1, source_target_pairs={{8,0},{12,4},{16,8},{20,12},{24,16},{28,20},{9,1},{13,5},{17,9},{2... | collective-permute-start | bytes 1179656 | tf_op jit(solution)/shard_map/ppermute | solution.py:268
  2.8 0.7 %stack.59.pos = s32[5]{0:T(128)} concatenate(s32[1]{0:T(128)} %bitcast, s32[1]{0:T(128)} %bitcast.1, s32[1]{0:T(128)} %constant.28.clone.1, s32[1]{0:T(128)} %constant.29.clone.1, s32[1]{0:T(128)} %constant.30.clone.1), dimensions={0} | concatenate | bytes 40 | tf_op jit(solution)/shard_map/stack | solution.py:289
  3.5 3.0 %start.1 = (f32[7,8,8,256]{3,2,1,0:T(8,128)}, f32[4,16,8,256]{3,2,1,0:T(8,128)}, f32[16,8,256]{2,1,0:T(8,128)}) custom-call(s32[5]{0:T(128)} %stack.59.pos, f32[3,16,8,256]{3,2,1,0:T(8,128)} %electric.1, f32[3,16,8,256]{3,2,1,0:T(8,128)} %magnetic.1, s32[16,8,256]{2,1,0:T(8,128)} %material.1, s32[32,8,256]{2,1,0:T(8,128)} %incoming.1), custom_call_target="tpu_custom_call" | custom-call | tf_op jit(solution)/shard_map/start/pallas_call | solution.py:234
  6.5 3.2 %collective-permute-start.4 = (f32[7,8,8,256]{3,2,1,0:T(8,128)}, f32[7,8,8,256]{3,2,1,0:T(8,128)S(1)}, u32[]{:S(2)}, u32[]{:S(2)}) collective-permute-start(f32[7,8,8,256]{3,2,1,0:T(8,128)} %get-tuple-element.10), channel_id=1, source_target_pairs={{0,1},{1,2},{2,3},{4,5},{5,6},{6,7},{8,9},{9,10},{10,11},{12,13},{... | collective-permute-start | bytes 1376264 | tf_op jit(solution)/shard_map/ppermute | solution.py:268
  9.7 2.1 %collective-permute-start.5 = (f32[7,8,8,256]{3,2,1,0:T(8,128)}, f32[7,8,8,256]{3,2,1,0:T(8,128)S(1)}, u32[]{:S(2)}, u32[]{:S(2)}) collective-permute-start(f32[7,8,8,256]{3,2,1,0:T(8,128)} %get-tuple-element.10), channel_id=1, source_target_pairs={{1,0},{2,1},{3,2},{5,4},{6,5},{7,6},{9,8},{10,9},{11,10},{13,12},{... | collective-permute-start | bytes 1376264 | tf_op jit(solution)/shard_map/ppermute | solution.py:268
  11.8 1.9 %collective-permute-start.3 = (f32[4,16,8,256]{3,2,1,0:T(8,128)}, f32[4,16,8,256]{3,2,1,0:T(8,128)S(1)}, u32[]{:S(2)}, u32[]{:S(2)}) collective-permute-start(f32[4,16,8,256]{3,2,1,0:T(8,128)} %get-tuple-element.8), channel_id=1, source_target_pairs={{8,0},{12,4},{16,8},{20,12},{24,16},{28,20},{9,1},{13,5},{17,9},{2... | collective-permute-start | bytes 1572872 | tf_op jit(solution)/shard_map/ppermute | solution.py:268
  13.8 0.0 collective-permute-done.refs_1_
  13.8 1.9 %collective-permute-start.2 = (f32[3,16,8,256]{3,2,1,0:T(8,128)S(1)}, f32[3,16,8,256]{3,2,1,0:T(8,128)S(1)}, u32[]{:S(2)}, u32[]{:S(2)}) collective-permute-start(f32[3,16,8,256]{3,2,1,0:T(8,128)S(1)} %collective-permute-done.refs_1_), channel_id=1, source_target_pairs={{1,0},{2,1},{3,2},{5,4},{6,5},{7,6},{9,8},{10,9},{11,10},{13,12},{... | collective-permute-start | bytes 1179656 | tf_op jit(solution)/shard_map/ppermute | solution.py:268
  15.7 3.4 %collective-permute-start.1 = (f32[3,16,8,256]{3,2,1,0:T(8,128)S(1)}, f32[3,16,8,256]{3,2,1,0:T(8,128)S(1)}, u32[]{:S(2)}, u32[]{:S(2)}) collective-permute-start(f32[3,16,8,256]{3,2,1,0:T(8,128)S(1)} %collective-permute-done.refs_1_), channel_id=1, source_target_pairs={{0,1},{1,2},{2,3},{4,5},{5,6},{6,7},{8,9},{9,10},{10,11},{12,13},{... | collective-permute-start | bytes 1179656 | tf_op jit(solution)/shard_map/ppermute | solution.py:268
  19.1 0.6 collective-permute-done.4
  19.7 2.9 %collective-permute-done.5 = f32[7,8,8,256]{3,2,1,0:T(8,128)S(1)} collective-permute-done((f32[7,8,8,256]{3,2,1,0:T(8,128)}, f32[7,8,8,256]{3,2,1,0:T(8,128)S(1)}, u32[]{:S(2)}, u32[]{:S(2)}) %collective-permute-start.5) | collective-permute-done | bytes 458784 | tf_op jit(solution)/shard_map/ppermute | solution.py:268
  22.6 0.0 copy-start.2
  22.6 1.2 %pad_maximum_fusion = f32[3,7,8,8,256]{4,3,2,1,0:T(8,128)S(1)} fusion(f32[1,7,8,8,256]{4,3,2,1,0:T(8,128)S(1)} %bitcast.33, f32[1,7,8,8,256]{4,3,2,1,0:T(8,128)} %bitcast.31, f32[1,7,8,8,256]{4,3,2,1,0:T(8,128)S(1)} %bitcast.32), kind=kLoop, calls=%fused_computation | loop fusion | flops 688128 | bytes 2752512 | tf_op jit(solution)/shard_map/stack | solution.py:299
  23.8 5.8 %collective-permute-start.10 = (f32[3,7,8,8,256]{4,3,2,1,0:T(8,128)S(1)}, f32[3,7,8,8,256]{4,3,2,1,0:T(8,128)S(1)}, u32[]{:S(2)}, u32[]{:S(2)}) collective-permute-start(f32[3,7,8,8,256]{4,3,2,1,0:T(8,128)S(1)} %pad_maximum_fusion), channel_id=1, source_target_pairs={{4,0},{12,8},{20,16},{28,24},{16,4},{24,12},{0,20},{5,1},{13,9},{2... | collective-permute-start | bytes 4128776 | tf_op jit(solution)/shard_map/ppermute | solution.py:274
  29.6 0.0 collective-permute-done.3
  29.6 0.0 copy-done.2
  29.7 3.2 %collective-permute-start.6 = (f32[4,16,8,256]{3,2,1,0:T(8,128)S(1)}, f32[4,16,8,256]{3,2,1,0:T(8,128)S(1)}, u32[]{:S(2)}, u32[]{:S(2)}) collective-permute-start(f32[4,16,8,256]{3,2,1,0:T(8,128)S(1)} %pad_maximum_fusion.3.refs_5_), channel_id=1, source_target_pairs={{0,1},{1,2},{2,3},{4,5},{5,6},{6,7},{8,9},{9,10},{10,11},{12,13},{... | collective-permute-start | bytes 1572872 | tf_op jit(solution)/shard_map/ppermute | solution.py:268
  33.0 2.1 %collective-permute-start.7 = (f32[4,16,8,256]{3,2,1,0:T(8,128)S(1)}, f32[4,16,8,256]{3,2,1,0:T(8,128)S(1)}, u32[]{:S(2)}, u32[]{:S(2)}) collective-permute-start(f32[4,16,8,256]{3,2,1,0:T(8,128)S(1)} %pad_maximum_fusion.3.refs_5_), channel_id=1, source_target_pairs={{1,0},{2,1},{3,2},{5,4},{6,5},{7,6},{9,8},{10,9},{11,10},{13,12},{... | collective-permute-start | bytes 1572872 | tf_op jit(solution)/shard_map/ppermute | solution.py:268
  35.1 0.0 collective-permute-done.2.refs_2_
  35.2 0.0 collective-permute-done.1.refs_0_
  35.3 0.2 collective-permute-start.8
  35.4 10.2 %collective-permute-done.6.refs_4_ = f32[4,16,8,256]{3,2,1,0:T(8,128)S(1)} collective-permute-done((f32[4,16,8,256]{3,2,1,0:T(8,128)S(1)}, f32[4,16,8,256]{3,2,1,0:T(8,128)S(1)}, u32[]{:S(2)}, u32[]{:S(2)}) %collective-permute-start.6) | collective-permute-done | bytes 524320 | tf_op jit(solution)/shard_map/ppermute | solution.py:268
  45.6 0.0 copy-start.3
  45.6 0.0 copy-start.4
  45.6 0.0 copy-start.5
  45.7 0.0 copy-start
  45.7 0.0 copy-start.1
  45.7 2.9 %collective-permute-done.7.refs_6_ = f32[4,16,8,256]{3,2,1,0:T(8,128)S(1)} collective-permute-done((f32[4,16,8,256]{3,2,1,0:T(8,128)S(1)}, f32[4,16,8,256]{3,2,1,0:T(8,128)S(1)}, u32[]{:S(2)}, u32[]{:S(2)}) %collective-permute-start.7) | collective-permute-done | bytes 524320 | tf_op jit(solution)/shard_map/ppermute | solution.py:268
  48.6 0.1 pad_maximum_fusion.1
  48.6 0.0 collective-permute-done.8.refs_3_
  48.7 0.7 %collective-permute-start.9 = (f32[3,4,8,8,256]{4,3,2,1,0:T(8,128)S(1)}, f32[3,4,8,8,256]{4,3,2,1,0:T(8,128)S(1)}, u32[]{:S(2)}, u32[]{:S(2)}) collective-permute-start(f32[3,4,8,8,256]{4,3,2,1,0:T(8,128)S(1)} %pad_maximum_fusion.1), channel_id=1, source_target_pairs={{0,4},{4,0},{8,12},{12,8},{16,20},{20,16},{24,28},{28,24},{1,5},{5... | collective-permute-start | bytes 2359304 | tf_op jit(solution)/shard_map/ppermute | solution.py:278
  49.4 0.0 copy-done.3
  49.4 0.0 copy-done.4
  49.4 0.0 copy-done.5
  49.4 0.0 collective-permute-done.10.refs_8_
  49.4 1.9 %collective-permute-done.9.refs_7_ = f32[3,4,8,8,256]{4,3,2,1,0:T(8,128)S(1)} collective-permute-done((f32[3,4,8,8,256]{4,3,2,1,0:T(8,128)S(1)}, f32[3,4,8,8,256]{4,3,2,1,0:T(8,128)S(1)}, u32[]{:S(2)}, u32[]{:S(2)}) %collective-permute-start.9) | collective-permute-done | bytes 786464 | tf_op jit(solution)/shard_map/ppermute | solution.py:278
  51.3 0.0 copy-done
  51.3 0.0 copy-done.1
  51.3 12.6 %fdtd_steps.1 = (f32[3,16,8,256]{3,2,1,0:T(8,128)}, f32[3,16,8,256]{3,2,1,0:T(8,128)}) custom-call(s32[5]{0:T(128)S(1)} %copy-done, s32[8]{0:T(128)S(1)} %copy-done.1, f32[3,8,128]{2,1,0:T(8,128)S(1)} %broadcast_in_dim.4.tables, f32[3,16,8,256]{3,2,1,0:T(8,128)S(1)} %collective-permute-done.1.refs_0_, f32[3,16,8,256]{3,2,1,0:T(8,128)S(1)} %collective-permute-done.refs_1_, ...), custom_call_target="tpu_custom_call" | custom-call | tf_op jit(solution)/shard_map/fdtd_steps/pallas_call | solution.py:252
  (13 shorter events, 0.3 us)
Async XLA Ops:
  0.6 13.1 %collective-permute-start = (f32[3,16,8,256]{3,2,1,0:T(8,128)}, f32[3,16,8,256]{3,2,1,0:T(8,128)S(1)}, u32[]{:S(2)}, u32[]{:S(2)}) collective-permute-start(f32[3,16,8,256]{3,2,1,0:T(8,128)} %electric.1), channel_id=1, source_target_pairs={{8,0},{12,4},{16,8},{20,12},{24,16},{28,20},{9,1},{13,5},{17,9},{2... | collective-permute-start | bytes 1179656 | tf_op jit(solution)/shard_map/ppermute | solution.py:268
  6.5 13.2 %collective-permute-start.4 = (f32[7,8,8,256]{3,2,1,0:T(8,128)}, f32[7,8,8,256]{3,2,1,0:T(8,128)S(1)}, u32[]{:S(2)}, u32[]{:S(2)}) collective-permute-start(f32[7,8,8,256]{3,2,1,0:T(8,128)} %get-tuple-element.10), channel_id=1, source_target_pairs={{0,1},{1,2},{2,3},{4,5},{5,6},{6,7},{8,9},{9,10},{10,11},{12,13},{... | collective-permute-start | bytes 1376264 | tf_op jit(solution)/shard_map/ppermute | solution.py:268
  9.7 12.9 %collective-permute-start.5 = (f32[7,8,8,256]{3,2,1,0:T(8,128)}, f32[7,8,8,256]{3,2,1,0:T(8,128)S(1)}, u32[]{:S(2)}, u32[]{:S(2)}) collective-permute-start(f32[7,8,8,256]{3,2,1,0:T(8,128)} %get-tuple-element.10), channel_id=1, source_target_pairs={{1,0},{2,1},{3,2},{5,4},{6,5},{7,6},{9,8},{10,9},{11,10},{13,12},{... | collective-permute-start | bytes 1376264 | tf_op jit(solution)/shard_map/ppermute | solution.py:268
  11.8 17.8 %collective-permute-start.3 = (f32[4,16,8,256]{3,2,1,0:T(8,128)}, f32[4,16,8,256]{3,2,1,0:T(8,128)S(1)}, u32[]{:S(2)}, u32[]{:S(2)}) collective-permute-start(f32[4,16,8,256]{3,2,1,0:T(8,128)} %get-tuple-element.8), channel_id=1, source_target_pairs={{8,0},{12,4},{16,8},{20,12},{24,16},{28,20},{9,1},{13,5},{17,9},{2... | collective-permute-start | bytes 1572872 | tf_op jit(solution)/shard_map/ppermute | solution.py:268
  13.8 21.3 %collective-permute-start.2 = (f32[3,16,8,256]{3,2,1,0:T(8,128)S(1)}, f32[3,16,8,256]{3,2,1,0:T(8,128)S(1)}, u32[]{:S(2)}, u32[]{:S(2)}) collective-permute-start(f32[3,16,8,256]{3,2,1,0:T(8,128)S(1)} %collective-permute-done.refs_1_), channel_id=1, source_target_pairs={{1,0},{2,1},{3,2},{5,4},{6,5},{7,6},{9,8},{10,9},{11,10},{13,12},{... | collective-permute-start | bytes 1179656 | tf_op jit(solution)/shard_map/ppermute | solution.py:268
  15.7 19.5 %collective-permute-start.1 = (f32[3,16,8,256]{3,2,1,0:T(8,128)S(1)}, f32[3,16,8,256]{3,2,1,0:T(8,128)S(1)}, u32[]{:S(2)}, u32[]{:S(2)}) collective-permute-start(f32[3,16,8,256]{3,2,1,0:T(8,128)S(1)} %collective-permute-done.refs_1_), channel_id=1, source_target_pairs={{0,1},{1,2},{2,3},{4,5},{5,6},{6,7},{8,9},{9,10},{10,11},{12,13},{... | collective-permute-start | bytes 1179656 | tf_op jit(solution)/shard_map/ppermute | solution.py:268
  22.6 7.0 %copy-start.2 = (f32[16,8,256]{2,1,0:T(8,128)S(1)}, f32[16,8,256]{2,1,0:T(8,128)}, u32[]{:S(2)}) copy-start(f32[16,8,256]{2,1,0:T(8,128)} %get-tuple-element.9) | copy-start | bytes 393220
  23.8 25.6 %collective-permute-start.10 = (f32[3,7,8,8,256]{4,3,2,1,0:T(8,128)S(1)}, f32[3,7,8,8,256]{4,3,2,1,0:T(8,128)S(1)}, u32[]{:S(2)}, u32[]{:S(2)}) collective-permute-start(f32[3,7,8,8,256]{4,3,2,1,0:T(8,128)S(1)} %pad_maximum_fusion), channel_id=1, source_target_pairs={{4,0},{12,8},{20,16},{28,24},{16,4},{24,12},{0,20},{5,1},{13,9},{2... | collective-permute-start | bytes 4128776 | tf_op jit(solution)/shard_map/ppermute | solution.py:274
  29.7 15.8 %collective-permute-start.6 = (f32[4,16,8,256]{3,2,1,0:T(8,128)S(1)}, f32[4,16,8,256]{3,2,1,0:T(8,128)S(1)}, u32[]{:S(2)}, u32[]{:S(2)}) collective-permute-start(f32[4,16,8,256]{3,2,1,0:T(8,128)S(1)} %pad_maximum_fusion.3.refs_5_), channel_id=1, source_target_pairs={{0,1},{1,2},{2,3},{4,5},{5,6},{6,7},{8,9},{9,10},{10,11},{12,13},{... | collective-permute-start | bytes 1572872 | tf_op jit(solution)/shard_map/ppermute | solution.py:268
  33.0 15.6 %collective-permute-start.7 = (f32[4,16,8,256]{3,2,1,0:T(8,128)S(1)}, f32[4,16,8,256]{3,2,1,0:T(8,128)S(1)}, u32[]{:S(2)}, u32[]{:S(2)}) collective-permute-start(f32[4,16,8,256]{3,2,1,0:T(8,128)S(1)} %pad_maximum_fusion.3.refs_5_), channel_id=1, source_target_pairs={{1,0},{2,1},{3,2},{5,4},{6,5},{7,6},{9,8},{10,9},{11,10},{13,12},{... | collective-permute-start | bytes 1572872 | tf_op jit(solution)/shard_map/ppermute | solution.py:268
  35.3 13.4 %collective-permute-start.8 = (f32[3,3,8,8,256]{4,3,2,1,0:T(8,128)S(1)}, f32[3,3,8,8,256]{4,3,2,1,0:T(8,128)S(1)}, u32[]{:S(2)}, u32[]{:S(2)}) collective-permute-start(f32[3,3,8,8,256]{4,3,2,1,0:T(8,128)S(1)} %pad_maximum_fusion.2), channel_id=1, source_target_pairs={{0,4},{4,0},{8,12},{12,8},{16,20},{20,16},{24,28},{28,24},{1,5},{5... | collective-permute-start | bytes 1769480 | tf_op jit(solution)/shard_map/ppermute | solution.py:278
  45.6 3.8 %copy-start.3 = (f32[16]{0:T(128)S(1)}, f32[16]{0:T(128)}, u32[]{:S(2)}) copy-start(f32[16]{0:T(128)} %param.14) | copy-start | bytes 196
  45.6 3.7 %copy-start.4 = (f32[16]{0:T(128)S(1)}, f32[16]{0:T(128)}, u32[]{:S(2)}) copy-start(f32[16]{0:T(128)} %param.13) | copy-start | bytes 196
  45.6 3.7 %copy-start.5 = (f32[16]{0:T(128)S(1)}, f32[16]{0:T(128)}, u32[]{:S(2)}) copy-start(f32[16]{0:T(128)} %param.15) | copy-start | bytes 196
  45.7 5.6 %copy-start = (s32[5]{0:T(128)S(1)}, s32[5]{0:T(128)}, u32[]{:S(2)}) copy-start(s32[5]{0:T(128)} %stack.59.pos) | copy-start | bytes 64
  45.7 5.6 %copy-start.1 = (s32[8]{0:T(128)S(1)}, s32[8]{0:T(128)}, u32[]{:S(2)}) copy-start(s32[8]{0:T(128)} %flags.1) | copy-start | bytes 100
  48.7 2.6 %collective-permute-start.9 = (f32[3,4,8,8,256]{4,3,2,1,0:T(8,128)S(1)}, f32[3,4,8,8,256]{4,3,2,1,0:T(8,128)S(1)}, u32[]{:S(2)}, u32[]{:S(2)}) collective-permute-start(f32[3,4,8,8,256]{4,3,2,1,0:T(8,128)S(1)} %pad_maximum_fusion.1), channel_id=1, source_target_pairs={{0,4},{4,0},{8,12},{12,8},{16,20},{20,16},{24,28},{28,24},{1,5},{5... | collective-permute-start | bytes 2359304 | tf_op jit(solution)/shard_map/ppermute | solution.py:278

commit v5 on v4

--- a/solution.py
+++ b/solution.py
@@ -29,7 +29,12 @@
 
 
 def assemble(planes, odd, first, outer_first, pieces, store):
-    pieces = [*pieces[:3], *[pieces[3].at[t] for t in range(TILES)], *[pieces[4].at[t] for t in range(TILES)]]
+    *pieces, outer = pieces
+    if len(pieces) == 5:
+        beside = [pieces[3].at[0], pieces[3].at[1], pieces[4].at[0]]
+    else:
+        beside = [pieces[3].at[t] for t in range(TILES)]
+    pieces = [*pieces[:3], *beside, *[outer.at[t] for t in range(TILES)]]
     inner_at = (1 - odd) * (planes + HALO)
     outer_at = odd * (planes + HALO)
     places = [(at, t * TILE) for at in (HALO, inner_at, outer_at) for t in range(TILES)]
@@ -75,7 +80,7 @@
 def step_kernel(
     planes, pos, flags, tables, *refs
 ):
-    e_pieces, h_pieces, outer, refs = refs[:4], refs[4:8], refs[8:9], refs[9:]
+    e_pieces, h_pieces, outer, refs = refs[:4], refs[4:9], refs[9:10], refs[10:]
     e_out, h_out, E1, E2, H1, H2, A, B, K, ids, e_stage, h_stage, out_sems = refs
     gz, gy, last_y, top_z = pos[0], pos[1], pos[2], pos[3]
     wide = planes + 2 * HALO
@@ -301,7 +306,8 @@
 
     def around(own):
         dn, up = spread(own)
-        return [dn, own, up], jnp.stack([jnp.where(odd, field[:, :HALO], field[:, HALO:]) for field in (dn, own, up)])
+        near = [jnp.where(odd, field[:, :HALO], field[:, HALO:]) for field in (dn, own, up)]
+        return [dn, own, up], near
 
     ids = jnp.where(gz >= count_z - hop, entering, moved_h[3])
     moved_h = jnp.concatenate([moved_h[:3], ids[None]], 0)
@@ -312,9 +318,10 @@
         [4.0 * eps_table - 2.0 * sigma_table, 4.0 * eps_table + 2.0 * sigma_table, 4.0 * kerr_table]
     )
     tables = jnp.broadcast_to(jnp.pad(tables, ((0, 0), (0, LANES - MAT)))[:, None, :], (3, TILE, LANES))
-    e_near = swap_cores(e_near)
-    h_near, e_near = lax.optimization_barrier((h_near, e_near))
-    pieces = e_pieces + [e_near] + h_pieces + [swap_cores(h_near)] + outer_pieces
+    e_near = swap_cores(jnp.stack(e_near))
+    up, e_near = lax.optimization_barrier((h_near[2], e_near))
+    h_near = [swap_cores(jnp.stack(h_near[:2])), swap_cores(up[None])]
+    pieces = e_pieces + [e_near] + h_pieces + h_near + outer_pieces
     return run_steps(pos, shift_flags, tables, pieces, planes, rows, width)
 
 

time: 65.2 us -> 64.4 us (0.988)
  the two profiles are of different devices: /device:TPU:11 before, /device:TPU:5 now
where the time goes in v5:
time: 64.4 us; the launch traced here: 64 us
  starting transfers between devices  28.4 us (44%)
  waiting for transfers between devices  16.8 us (26%)
  Pallas kernels  15.7 us (24%)
  other arithmetic  1.5 us (2%)
  between operations  0.94 us (1%)
  local copies, waits for them, and re-layouts  0.7 us (1%)
    ppermute x8, starting transfers between devices, shift(): lax.ppermute(value, axis, [(s, s + hop) for s in range(count) if 0 <= s +...  20.2 us
    ppermute x8, waiting for transfers between devices, shift(): lax.ppermute(value, axis, [(s, s + hop) for s in range(count) if 0 <= s +...  15.7 us
    pallas_call x1, Pallas kernels, run_steps(): pl.pallas_call(functools.partial(step_kernel, planes), out_shape=(field,...  12.7 us
    ppermute x1, starting transfers between devices, outer_planes(): return lax.ppermute(value, 'gz', pairs + [(0, count - 3)])  5.83 us
    pallas_call x1, Pallas kernels, start(): pl.pallas_call(functools.partial(start_kernel, planes), out_shape=(shape(...  3.01 us
    ppermute x3, starting transfers between devices, swap_cores(): lax.ppermute(value, 'gz', [(s, s ^ 1) for s in range(lax.axis_size('gz'))])  2.4 us
  transfers between devices with their start and end apart: 12, of which 4 were waited for; matrix products, arithmetic and copies ran while one was open for 3% of the time, Pallas kernels for 5%

profile of v5, /device:TPU:5, one launch (start us, length us, event | category | flops | bytes accessed | tf_op | source)
XLA Modules:
  0.0 64.0 jit_solution(5633160623775593913)
XLA Ops:
  0.6 3.1 %collective-permute-start = (f32[3,16,8,256]{3,2,1,0:T(8,128)}, f32[3,16,8,256]{3,2,1,0:T(8,128)S(1)}, u32[]{:S(2)}, u32[]{:S(2)}) collective-permute-start(f32[3,16,8,256]{3,2,1,0:T(8,128)} %electric.1), channel_id=1, source_target_pairs={{8,0},{12,4},{16,8},{20,12},{24,16},{28,20},{9,1},{13,5},{17,9},{2... | collective-permute-start | bytes 1179656 | tf_op jit(solution)/shard_map/ppermute | solution.py:273
  3.7 0.6 stack.56.pos
  4.3 3.0 %start.1 = (f32[7,8,8,256]{3,2,1,0:T(8,128)}, f32[4,16,8,256]{3,2,1,0:T(8,128)}, f32[16,8,256]{2,1,0:T(8,128)}) custom-call(s32[5]{0:T(128)} %stack.56.pos, f32[3,16,8,256]{3,2,1,0:T(8,128)} %electric.1, f32[3,16,8,256]{3,2,1,0:T(8,128)} %magnetic.1, s32[16,8,256]{2,1,0:T(8,128)} %material.1, s32[32,8,256]{2,1,0:T(8,128)} %incoming.1), custom_call_target="tpu_custom_call" | custom-call | tf_op jit(solution)/shard_map/start/pallas_call | solution.py:239
  7.4 3.2 %collective-permute-start.4 = (f32[7,8,8,256]{3,2,1,0:T(8,128)}, f32[7,8,8,256]{3,2,1,0:T(8,128)S(1)}, u32[]{:S(2)}, u32[]{:S(2)}) collective-permute-start(f32[7,8,8,256]{3,2,1,0:T(8,128)} %get-tuple-element.10), channel_id=1, source_target_pairs={{0,1},{1,2},{2,3},{4,5},{5,6},{6,7},{8,9},{9,10},{10,11},{12,13},{... | collective-permute-start | bytes 1376264 | tf_op jit(solution)/shard_map/ppermute | solution.py:273
  10.6 1.3 %collective-permute-start.5 = (f32[7,8,8,256]{3,2,1,0:T(8,128)}, f32[7,8,8,256]{3,2,1,0:T(8,128)S(1)}, u32[]{:S(2)}, u32[]{:S(2)}) collective-permute-start(f32[7,8,8,256]{3,2,1,0:T(8,128)} %get-tuple-element.10), channel_id=1, source_target_pairs={{1,0},{2,1},{3,2},{5,4},{6,5},{7,6},{9,8},{10,9},{11,10},{13,12},{... | collective-permute-start | bytes 1376264 | tf_op jit(solution)/shard_map/ppermute | solution.py:273
  11.9 2.2 %collective-permute-start.3 = (f32[4,16,8,256]{3,2,1,0:T(8,128)}, f32[4,16,8,256]{3,2,1,0:T(8,128)S(1)}, u32[]{:S(2)}, u32[]{:S(2)}) collective-permute-start(f32[4,16,8,256]{3,2,1,0:T(8,128)} %get-tuple-element.8), channel_id=1, source_target_pairs={{8,0},{12,4},{16,8},{20,12},{24,16},{28,20},{9,1},{13,5},{17,9},{2... | collective-permute-start | bytes 1572872 | tf_op jit(solution)/shard_map/ppermute | solution.py:273
  14.1 0.0 collective-permute-done.refs_1_
  14.1 1.3 %collective-permute-start.2 = (f32[3,16,8,256]{3,2,1,0:T(8,128)S(1)}, f32[3,16,8,256]{3,2,1,0:T(8,128)S(1)}, u32[]{:S(2)}, u32[]{:S(2)}) collective-permute-start(f32[3,16,8,256]{3,2,1,0:T(8,128)S(1)} %collective-permute-done.refs_1_), channel_id=1, source_target_pairs={{1,0},{2,1},{3,2},{5,4},{6,5},{7,6},{9,8},{10,9},{11,10},{13,12},{... | collective-permute-start | bytes 1179656 | tf_op jit(solution)/shard_map/ppermute | solution.py:273
  15.4 4.6 %collective-permute-start.1 = (f32[3,16,8,256]{3,2,1,0:T(8,128)S(1)}, f32[3,16,8,256]{3,2,1,0:T(8,128)S(1)}, u32[]{:S(2)}, u32[]{:S(2)}) collective-permute-start(f32[3,16,8,256]{3,2,1,0:T(8,128)S(1)} %collective-permute-done.refs_1_), channel_id=1, source_target_pairs={{0,1},{1,2},{2,3},{4,5},{5,6},{6,7},{8,9},{9,10},{10,11},{12,13},{... | collective-permute-start | bytes 1179656 | tf_op jit(solution)/shard_map/ppermute | solution.py:273
  20.1 0.0 collective-permute-done.4
  20.1 3.4 %collective-permute-done.5 = f32[7,8,8,256]{3,2,1,0:T(8,128)S(1)} collective-permute-done((f32[7,8,8,256]{3,2,1,0:T(8,128)}, f32[7,8,8,256]{3,2,1,0:T(8,128)S(1)}, u32[]{:S(2)}, u32[]{:S(2)}) %collective-permute-start.5) | collective-permute-done | bytes 458784 | tf_op jit(solution)/shard_map/ppermute | solution.py:273
  23.5 0.0 copy-start.2
  23.5 1.2 %pad_maximum_fusion = f32[3,7,8,8,256]{4,3,2,1,0:T(8,128)S(1)} fusion(f32[1,7,8,8,256]{4,3,2,1,0:T(8,128)S(1)} %bitcast.32, f32[1,7,8,8,256]{4,3,2,1,0:T(8,128)} %bitcast.30, f32[1,7,8,8,256]{4,3,2,1,0:T(8,128)S(1)} %bitcast.31), kind=kLoop, calls=%fused_computation | loop fusion | flops 688128 | bytes 2752512 | tf_op jit(solution)/shard_map/stack | solution.py:304
  24.7 5.8 %collective-permute-start.11 = (f32[3,7,8,8,256]{4,3,2,1,0:T(8,128)S(1)}, f32[3,7,8,8,256]{4,3,2,1,0:T(8,128)S(1)}, u32[]{:S(2)}, u32[]{:S(2)}) collective-permute-start(f32[3,7,8,8,256]{4,3,2,1,0:T(8,128)S(1)} %pad_maximum_fusion), channel_id=1, source_target_pairs={{4,0},{12,8},{20,16},{28,24},{16,4},{24,12},{0,20},{5,1},{13,9},{2... | collective-permute-start | bytes 4128776 | tf_op jit(solution)/shard_map/ppermute | solution.py:279
  30.5 0.0 collective-permute-done.3
  30.5 0.0 copy-done.2
  30.6 3.2 %collective-permute-start.8 = (f32[4,16,8,256]{3,2,1,0:T(8,128)S(1)}, f32[4,16,8,256]{3,2,1,0:T(8,128)S(1)}, u32[]{:S(2)}, u32[]{:S(2)}) collective-permute-start(f32[4,16,8,256]{3,2,1,0:T(8,128)S(1)} %pad_maximum_fusion.2.refs_5_), channel_id=1, source_target_pairs={{0,1},{1,2},{2,3},{4,5},{5,6},{6,7},{8,9},{9,10},{10,11},{12,13},{... | collective-permute-start | bytes 1572872 | tf_op jit(solution)/shard_map/ppermute | solution.py:273
  33.8 1.3 %collective-permute-start.6 = (f32[4,16,8,256]{3,2,1,0:T(8,128)S(1)}, f32[4,16,8,256]{3,2,1,0:T(8,128)S(1)}, u32[]{:S(2)}, u32[]{:S(2)}) collective-permute-start(f32[4,16,8,256]{3,2,1,0:T(8,128)S(1)} %pad_maximum_fusion.2.refs_5_), channel_id=1, source_target_pairs={{1,0},{2,1},{3,2},{5,4},{6,5},{7,6},{9,8},{10,9},{11,10},{13,12},{... | collective-permute-start | bytes 1572872 | tf_op jit(solution)/shard_map/ppermute | solution.py:273
  35.2 0.0 collective-permute-done.2.refs_2_
  35.2 0.0 collective-permute-done.1.refs_0_
  35.3 0.0 copy-start.3
  35.3 0.0 copy-start.4
  35.3 0.0 copy-start.5
  35.4 0.0 copy-start
  35.4 0.0 copy-start.1
  35.4 0.4 collective-permute-start.7
  35.7 9.4 %collective-permute-done.8.refs_4_ = f32[4,16,8,256]{3,2,1,0:T(8,128)S(1)} collective-permute-done((f32[4,16,8,256]{3,2,1,0:T(8,128)S(1)}, f32[4,16,8,256]{3,2,1,0:T(8,128)S(1)}, u32[]{:S(2)}, u32[]{:S(2)}) %collective-permute-start.8) | collective-permute-done | bytes 524320 | tf_op jit(solution)/shard_map/ppermute | solution.py:273
  45.2 0.9 %collective-permute-start.9 = (f32[2,4,8,8,256]{4,3,2,1,0:T(8,128)S(1)}, f32[2,4,8,8,256]{4,3,2,1,0:T(8,128)S(1)}, u32[]{:S(2)}, u32[]{:S(2)}) collective-permute-start(f32[2,4,8,8,256]{4,3,2,1,0:T(8,128)S(1)} %pad_maximum_fusion.3), channel_id=1, source_target_pairs={{0,4},{4,0},{8,12},{12,8},{16,20},{20,16},{24,28},{28,24},{1,5},{5... | collective-permute-start | bytes 1572872 | tf_op jit(solution)/shard_map/ppermute | solution.py:283
  46.1 2.9 %collective-permute-done.6.refs_6_ = f32[4,16,8,256]{3,2,1,0:T(8,128)S(1)} collective-permute-done((f32[4,16,8,256]{3,2,1,0:T(8,128)S(1)}, f32[4,16,8,256]{3,2,1,0:T(8,128)S(1)}, u32[]{:S(2)}, u32[]{:S(2)}) %collective-permute-start.6) | collective-permute-done | bytes 524320 | tf_op jit(solution)/shard_map/ppermute | solution.py:273
  49.0 0.0 collective-permute-done.7.refs_3_
  49.0 1.2 %collective-permute-start.10 = (f32[1,4,8,8,256]{4,3,2,1,0:T(8,128)S(1)}, f32[1,4,8,8,256]{4,3,2,1,0:T(8,128)S(1)}, u32[]{:S(2)}, u32[]{:S(2)}) collective-permute-start(f32[1,4,8,8,256]{4,3,2,1,0:T(8,128)S(1)} %bitcast.33), channel_id=1, source_target_pairs={{0,4},{4,0},{8,12},{12,8},{16,20},{20,16},{24,28},{28,24},{1,5},{5... | collective-permute-start | bytes 786440 | tf_op jit(solution)/shard_map/ppermute | solution.py:283
  50.2 0.0 copy-done.3
  50.2 0.0 copy-done.4
  50.2 0.0 copy-done.5
  50.2 0.0 collective-permute-done.9.refs_7_
  50.2 1.1 %collective-permute-done.10.refs_8_ = f32[1,4,8,8,256]{4,3,2,1,0:T(8,128)S(1)} collective-permute-done((f32[1,4,8,8,256]{4,3,2,1,0:T(8,128)S(1)}, f32[1,4,8,8,256]{4,3,2,1,0:T(8,128)S(1)}, u32[]{:S(2)}, u32[]{:S(2)}) %collective-permute-start.10) | collective-permute-done | bytes 262176 | tf_op jit(solution)/shard_map/ppermute | solution.py:283
  51.3 0.0 collective-permute-done.11.refs_9_
  51.4 0.0 copy-done
  51.4 0.0 copy-done.1
  51.4 12.7 %fdtd_steps.1 = (f32[3,16,8,256]{3,2,1,0:T(8,128)}, f32[3,16,8,256]{3,2,1,0:T(8,128)}) custom-call(s32[5]{0:T(128)S(1)} %copy-done, s32[8]{0:T(128)S(1)} %copy-done.1, f32[3,8,128]{2,1,0:T(8,128)S(1)} %broadcast_in_dim.12.tables, f32[3,16,8,256]{3,2,1,0:T(8,128)S(1)} %collective-permute-done.1.refs_0_, f32[3,16,8,256]{3,2,1,0:T(8,128)S(1)} %collective-permute-done.refs_1_, ...), custom_call_target="tpu_custom_call" | custom-call | tf_op jit(solution)/shard_map/fdtd_steps/pallas_call | solution.py:257
  (14 shorter events, 0.4 us)
Async XLA Ops:
  0.6 13.5 %collective-permute-start = (f32[3,16,8,256]{3,2,1,0:T(8,128)}, f32[3,16,8,256]{3,2,1,0:T(8,128)S(1)}, u32[]{:S(2)}, u32[]{:S(2)}) collective-permute-start(f32[3,16,8,256]{3,2,1,0:T(8,128)} %electric.1), channel_id=1, source_target_pairs={{8,0},{12,4},{16,8},{20,12},{24,16},{28,20},{9,1},{13,5},{17,9},{2... | collective-permute-start | bytes 1179656 | tf_op jit(solution)/shard_map/ppermute | solution.py:273
  7.4 12.7 %collective-permute-start.4 = (f32[7,8,8,256]{3,2,1,0:T(8,128)}, f32[7,8,8,256]{3,2,1,0:T(8,128)S(1)}, u32[]{:S(2)}, u32[]{:S(2)}) collective-permute-start(f32[7,8,8,256]{3,2,1,0:T(8,128)} %get-tuple-element.10), channel_id=1, source_target_pairs={{0,1},{1,2},{2,3},{4,5},{5,6},{6,7},{8,9},{9,10},{10,11},{12,13},{... | collective-permute-start | bytes 1376264 | tf_op jit(solution)/shard_map/ppermute | solution.py:273
  10.6 12.9 %collective-permute-start.5 = (f32[7,8,8,256]{3,2,1,0:T(8,128)}, f32[7,8,8,256]{3,2,1,0:T(8,128)S(1)}, u32[]{:S(2)}, u32[]{:S(2)}) collective-permute-start(f32[7,8,8,256]{3,2,1,0:T(8,128)} %get-tuple-element.10), channel_id=1, source_target_pairs={{1,0},{2,1},{3,2},{5,4},{6,5},{7,6},{9,8},{10,9},{11,10},{13,12},{... | collective-permute-start | bytes 1376264 | tf_op jit(solution)/shard_map/ppermute | solution.py:273
  11.9 18.6 %collective-permute-start.3 = (f32[4,16,8,256]{3,2,1,0:T(8,128)}, f32[4,16,8,256]{3,2,1,0:T(8,128)S(1)}, u32[]{:S(2)}, u32[]{:S(2)}) collective-permute-start(f32[4,16,8,256]{3,2,1,0:T(8,128)} %get-tuple-element.8), channel_id=1, source_target_pairs={{8,0},{12,4},{16,8},{20,12},{24,16},{28,20},{9,1},{13,5},{17,9},{2... | collective-permute-start | bytes 1572872 | tf_op jit(solution)/shard_map/ppermute | solution.py:273
  14.1 21.1 %collective-permute-start.2 = (f32[3,16,8,256]{3,2,1,0:T(8,128)S(1)}, f32[3,16,8,256]{3,2,1,0:T(8,128)S(1)}, u32[]{:S(2)}, u32[]{:S(2)}) collective-permute-start(f32[3,16,8,256]{3,2,1,0:T(8,128)S(1)} %collective-permute-done.refs_1_), channel_id=1, source_target_pairs={{1,0},{2,1},{3,2},{5,4},{6,5},{7,6},{9,8},{10,9},{11,10},{13,12},{... | collective-permute-start | bytes 1179656 | tf_op jit(solution)/shard_map/ppermute | solution.py:273
  15.4 19.8 %collective-permute-start.1 = (f32[3,16,8,256]{3,2,1,0:T(8,128)S(1)}, f32[3,16,8,256]{3,2,1,0:T(8,128)S(1)}, u32[]{:S(2)}, u32[]{:S(2)}) collective-permute-start(f32[3,16,8,256]{3,2,1,0:T(8,128)S(1)} %collective-permute-done.refs_1_), channel_id=1, source_target_pairs={{0,1},{1,2},{2,3},{4,5},{5,6},{6,7},{8,9},{9,10},{10,11},{12,13},{... | collective-permute-start | bytes 1179656 | tf_op jit(solution)/shard_map/ppermute | solution.py:273
  23.5 7.0 %copy-start.2 = (f32[16,8,256]{2,1,0:T(8,128)S(1)}, f32[16,8,256]{2,1,0:T(8,128)}, u32[]{:S(2)}) copy-start(f32[16,8,256]{2,1,0:T(8,128)} %get-tuple-element.9) | copy-start | bytes 393220
  24.7 26.7 %collective-permute-start.11 = (f32[3,7,8,8,256]{4,3,2,1,0:T(8,128)S(1)}, f32[3,7,8,8,256]{4,3,2,1,0:T(8,128)S(1)}, u32[]{:S(2)}, u32[]{:S(2)}) collective-permute-start(f32[3,7,8,8,256]{4,3,2,1,0:T(8,128)S(1)} %pad_maximum_fusion), channel_id=1, source_target_pairs={{4,0},{12,8},{20,16},{28,24},{16,4},{24,12},{0,20},{5,1},{13,9},{2... | collective-permute-start | bytes 4128776 | tf_op jit(solution)/shard_map/ppermute | solution.py:279
  30.6 14.5 %collective-permute-start.8 = (f32[4,16,8,256]{3,2,1,0:T(8,128)S(1)}, f32[4,16,8,256]{3,2,1,0:T(8,128)S(1)}, u32[]{:S(2)}, u32[]{:S(2)}) collective-permute-start(f32[4,16,8,256]{3,2,1,0:T(8,128)S(1)} %pad_maximum_fusion.2.refs_5_), channel_id=1, source_target_pairs={{0,1},{1,2},{2,3},{4,5},{5,6},{6,7},{8,9},{9,10},{10,11},{12,13},{... | collective-permute-start | bytes 1572872 | tf_op jit(solution)/shard_map/ppermute | solution.py:273
  33.8 15.1 %collective-permute-start.6 = (f32[4,16,8,256]{3,2,1,0:T(8,128)S(1)}, f32[4,16,8,256]{3,2,1,0:T(8,128)S(1)}, u32[]{:S(2)}, u32[]{:S(2)}) collective-permute-start(f32[4,16,8,256]{3,2,1,0:T(8,128)S(1)} %pad_maximum_fusion.2.refs_5_), channel_id=1, source_target_pairs={{1,0},{2,1},{3,2},{5,4},{6,5},{7,6},{9,8},{10,9},{11,10},{13,12},{... | collective-permute-start | bytes 1572872 | tf_op jit(solution)/shard_map/ppermute | solution.py:273
  35.3 14.9 %copy-start.3 = (f32[16]{0:T(128)S(1)}, f32[16]{0:T(128)}, u32[]{:S(2)}) copy-start(f32[16]{0:T(128)} %param.14) | copy-start | bytes 196
  35.3 14.9 %copy-start.4 = (f32[16]{0:T(128)S(1)}, f32[16]{0:T(128)}, u32[]{:S(2)}) copy-start(f32[16]{0:T(128)} %param.13) | copy-start | bytes 196
  35.3 14.8 %copy-start.5 = (f32[16]{0:T(128)S(1)}, f32[16]{0:T(128)}, u32[]{:S(2)}) copy-start(f32[16]{0:T(128)} %param.15) | copy-start | bytes 196
  35.4 16.0 %copy-start = (s32[5]{0:T(128)S(1)}, s32[5]{0:T(128)}, u32[]{:S(2)}) copy-start(s32[5]{0:T(128)} %stack.56.pos) | copy-start | bytes 64
  35.4 16.0 %copy-start.1 = (s32[8]{0:T(128)S(1)}, s32[8]{0:T(128)}, u32[]{:S(2)}) copy-start(s32[8]{0:T(128)} %flags.1) | copy-start | bytes 100
  35.4 13.6 %collective-permute-start.7 = (f32[3,3,8,8,256]{4,3,2,1,0:T(8,128)S(1)}, f32[3,3,8,8,256]{4,3,2,1,0:T(8,128)S(1)}, u32[]{:S(2)}, u32[]{:S(2)}) collective-permute-start(f32[3,3,8,8,256]{4,3,2,1,0:T(8,128)S(1)} %pad_maximum_fusion.1), channel_id=1, source_target_pairs={{0,4},{4,0},{8,12},{12,8},{16,20},{20,16},{24,28},{28,24},{1,5},{5... | collective-permute-start | bytes 1769480 | tf_op jit(solution)/shard_map/ppermute | solution.py:283
  45.2 5.0 %collective-permute-start.9 = (f32[2,4,8,8,256]{4,3,2,1,0:T(8,128)S(1)}, f32[2,4,8,8,256]{4,3,2,1,0:T(8,128)S(1)}, u32[]{:S(2)}, u32[]{:S(2)}) collective-permute-start(f32[2,4,8,8,256]{4,3,2,1,0:T(8,128)S(1)} %pad_maximum_fusion.3), channel_id=1, source_target_pairs={{0,4},{4,0},{8,12},{12,8},{16,20},{20,16},{24,28},{28,24},{1,5},{5... | collective-permute-start | bytes 1572872 | tf_op jit(solution)/shard_map/ppermute | solution.py:283
  49.0 2.3 %collective-permute-start.10 = (f32[1,4,8,8,256]{4,3,2,1,0:T(8,128)S(1)}, f32[1,4,8,8,256]{4,3,2,1,0:T(8,128)S(1)}, u32[]{:S(2)}, u32[]{:S(2)}) collective-permute-start(f32[1,4,8,8,256]{4,3,2,1,0:T(8,128)S(1)} %bitcast.33), channel_id=1, source_target_pairs={{0,4},{4,0},{8,12},{12,8},{16,20},{20,16},{24,28},{28,24},{1,5},{5... | collective-permute-start | bytes 786440 | tf_op jit(solution)/shard_map/ppermute | solution.py:283
